TPU v7x, 32 devices: a whole 2x2x4 slice. The times are simulated.
32 devices in a mesh: parts: 2 (over y), section: 4 (over x, core), tensor: 4 (over z).
Axes of the slice: x: 2, y: 2, z: 4, core: 2. Of those that a mesh axis runs over, the one named last changes fastest.
Arguments:
- prompt: bfloat16 [8, 256, 5120], P(('parts', 'section'), None, 'tensor'), parts along dimension 0, may hold values from -6 to 6
- key_value_weight: bfloat16 [5120, 2048], P('tensor'), may hold values from -0.078125 to 0.078125
- key_gain: float32 [128], replicated, may hold values from 0.1 to 1.9
- prompt_blocks: int32 [12], P('parts'), parts along dimension 0, may hold values from 1 to 8, 16 in all
- block_owner: int32 [32], P('parts'), parts along dimension 0, may hold values from 0 to 3, as said below
- block_slot: int32 [32], P('parts'), parts along dimension 0, may hold values from 0 to 3
- queries: bfloat16 [32, 8192], P(('parts', 'section')), parts along dimension 0, may hold values from -15 to 15
- cache_keys: bfloat16 [32, 512, 1024], P(('parts', 'section'), 'tensor'), parts along dimension 0, may hold values from -6 to 6
- cache_values: bfloat16 [32, 512, 1024], P(('parts', 'section'), 'tensor'), parts along dimension 0, may hold values from -6 to 6
- new_keys: bfloat16 [32, 1024], P(('parts', 'section')), parts along dimension 0, may hold values from -12 to 12
- new_values: bfloat16 [32, 1024], P(('parts', 'section')), parts along dimension 0, may hold values from -6 to 6
- decode_lengths: int32 [32], P(('parts', 'section')), parts along dimension 0, may hold values from 64 to 512, as said below
Outputs:
- attended: bfloat16 [32, 8192], P(('parts', 'section'), 'tensor'), parts along dimension 0
- block_pool: bfloat16 [8, 4, 16, 2048], P(('parts', 'section')), parts along dimension 0
There are 2 independent parts, one for each index of `parts`. A program takes and returns all parts, laid end to end along the dimension named above; an argument that names none is the same for every part. Nothing has to cross between parts.
Inputs may be any that keep to these rules, and one draw needn't show every extreme that they name: Prompt j takes prompt_blocks[j] whole blocks of 16 tokens; together they fill all 16 blocks; the longest takes exactly 8. `block_owner`: no two blocks share an owner and a slot; in every draw some group receives exactly 4 blocks. `decode_lengths`: in every group some row has all 512 positions live.
All inputs are finite; a program needn't handle non-finite values.
Results may differ from a plain program's by a relative error of at most 0.0015.
Values may be sent and summed in bfloat16 or wider, within the bound.
No kernel may reach another device: no remote copies, remote signals or barrier semaphores. Data moves between devices by JAX's collectives and lax.ppermute only.
A program may use at most 64 MiB of HBM per device.

v0:
```python
import jax
import jax.numpy as jnp
from jax import lax
from jax.sharding import PartitionSpec as P

H = 64
KVH = 8
HD = 128
BLK = 16
SPAN = 128
KVW = 1024
G = 8
NB = 16
CAP = 4


NORM_EPSILON = 1e-06
ROPE_BASE = 1000000.0
MASKED_SCORE = -1e30


def from_root(block, axis, holder):
    block = jnp.where(lax.axis_index(axis) == holder, block, jnp.zeros_like(block))
    return lax.psum(block, axis)


def joined(value, axis, join):
    pieces = jax.tree.map(lambda part: lax.all_gather(part, axis), value)
    head = jax.tree.map(lambda part: part[0], pieces)
    tail = jax.tree.map(lambda part: part[1:], pieces)
    running, _ = lax.scan(lambda running, share: (join(running, share), None), head, tail)
    return running


def positions_of(prompt_blocks, token_count):
    prompt_ends = jnp.cumsum(prompt_blocks)
    prompt_starts = prompt_ends - prompt_blocks
    token_ids = jnp.arange(token_count, dtype=jnp.int32)
    block_index = token_ids // BLK
    prompt_index = jnp.sum((block_index[:, None] >= prompt_ends[None, :]).astype(jnp.int32), axis=1)
    chosen = prompt_index[:, None] == jnp.arange(prompt_ends.shape[0], dtype=jnp.int32)[None, :]
    first_block = jnp.sum(jnp.where(chosen, prompt_starts[None, :], 0), axis=1)
    return token_ids - first_block * BLK


def finish_keys(projected, positions, key_gain):
    token_count = projected.shape[0]
    key_heads = projected[:, :KVW].reshape(token_count, KVH, HD)
    inv_root = lax.rsqrt(jnp.mean(key_heads * key_heads, axis=-1, keepdims=True) + NORM_EPSILON)
    key_heads = key_heads * inv_root * key_gain
    half_dim = HD // 2
    frequency = ROPE_BASE ** (jnp.arange(half_dim, dtype=jnp.float32) * (-2.0 / HD))
    angles = positions.astype(jnp.float32)[:, None, None] * frequency[None, None, :]
    cosine = jnp.cos(angles)
    sine_part = jnp.sin(angles)
    lower_half = key_heads[..., :half_dim]
    upper_half = key_heads[..., half_dim:]
    rotated = jnp.concatenate(
        [
            lower_half * cosine - upper_half * sine_part,
            upper_half * cosine + lower_half * sine_part,
        ],
        axis=-1,
    )
    return jnp.concatenate([rotated.reshape(token_count, KVW), projected[:, KVW:]], axis=1).astype(
        jnp.bfloat16
    )


def fill_slots(landed, block_owner, block_slot, group_index):
    blocks = landed.reshape(NB, BLK * landed.shape[1])
    slot_ids = jnp.arange(CAP, dtype=jnp.int32)
    selector = (block_owner[None, :] == group_index) & (block_slot[None, :] == slot_ids[:, None])
    filled = jnp.dot(selector.astype(jnp.bfloat16), blocks, preferred_element_type=jnp.float32)
    return filled.reshape(1, CAP, BLK, landed.shape[1]).astype(jnp.bfloat16)


def partial_attention(queries, cache_keys, cache_values, decode_lengths, first_position):
    row_count = queries.shape[0]
    local_len = cache_keys.shape[1]
    span_count = local_len // SPAN
    query_heads = queries.reshape(row_count, KVH, G, HD)
    key_heads = cache_keys.reshape(row_count, local_len, KVH, HD)
    scores = jnp.einsum(
        "rkgd,rpkd->rkgp", query_heads, key_heads, preferred_element_type=jnp.float32
    ) * HD ** (-0.5)
    live_mask = (first_position + jnp.arange(local_len, dtype=jnp.int32))[None, :] < decode_lengths[
        :, None
    ]
    scores = jnp.where(live_mask[:, None, None, :], scores, MASKED_SCORE)
    spans = scores.reshape(row_count, KVH, G, span_count, SPAN)
    span_max = jnp.max(spans, axis=-1)
    live_spans = live_mask.reshape(row_count, 1, 1, span_count, SPAN)
    weights = jnp.where(live_spans, jnp.exp(spans - span_max[..., None]), 0.0)
    span_sum = jnp.sum(weights, axis=-1)
    value_spans = cache_values.reshape(row_count, span_count, SPAN, KVH, HD)
    span_out = jnp.einsum(
        "rkgns,rnskd->rkgnd",
        weights.astype(jnp.bfloat16),
        value_spans,
        preferred_element_type=jnp.float32,
    )
    row_peak = jnp.max(span_max, axis=-1)
    factor = jnp.exp(span_max - row_peak[..., None])
    partial_out = jnp.sum(span_out * factor[..., None], axis=3)
    partial_sum = jnp.sum(span_sum * factor, axis=-1)
    return (
        partial_out.reshape(row_count, H, HD),
        row_peak.reshape(row_count, H),
        partial_sum.reshape(row_count, H),
    )


def combine_partials(former, latter):
    former_out, former_peak, former_sum = former
    latter_out, latter_peak, latter_sum = latter
    highest = jnp.maximum(former_peak, latter_peak)
    former_factor = jnp.exp(former_peak - highest)
    latter_factor = jnp.exp(latter_peak - highest)
    merged_out = former_out * former_factor[..., None] + latter_out * latter_factor[..., None]
    return (merged_out, highest, former_sum * former_factor + latter_sum * latter_factor)


def finish_heads(
    own_out, own_peak, own_sum, queries, new_keys, new_values, tensor_rank, heads_here
):
    row_count = queries.shape[0]
    own_width = heads_here * HD
    own_queries = (
        lax.dynamic_slice_in_dim(queries, tensor_rank * own_width, own_width, 1)
        .reshape(row_count, heads_here, HD)
        .astype(jnp.float32)
    )
    head_ids = tensor_rank * heads_here + jnp.arange(heads_here, dtype=jnp.int32)
    selector = (head_ids[:, None] // G == jnp.arange(KVH, dtype=jnp.int32)[None, :]).astype(
        jnp.float32
    )
    own_keys = jnp.einsum(
        "jk,rkd->rjd",
        selector,
        new_keys.reshape(row_count, KVH, HD).astype(jnp.float32),
        precision=lax.Precision.HIGHEST,
    )
    own_values = jnp.einsum(
        "jk,rkd->rjd",
        selector,
        new_values.reshape(row_count, KVH, HD).astype(jnp.float32),
        precision=lax.Precision.HIGHEST,
    )
    self_score = jnp.sum(own_queries * own_keys, axis=-1) * HD ** (-0.5)
    row_peak = jnp.maximum(own_peak, self_score)
    factor = jnp.exp(own_peak - row_peak)
    self_weight = jnp.exp(self_score - row_peak)
    numerator = own_out * factor[..., None] + self_weight[..., None] * own_values
    denominator = own_sum * factor + self_weight
    return (numerator / denominator[..., None]).reshape(row_count, own_width).astype(jnp.bfloat16)


def local(
    prompt,
    key_value_weight,
    key_gain,
    prompt_blocks,
    block_owner,
    block_slot,
    queries,
    cache_keys,
    cache_values,
    new_keys,
    new_values,
    decode_lengths,
):
    tensor_count = lax.axis_size("tensor")
    tensor_rank = lax.axis_index("tensor")
    group_index = lax.axis_index("section")
    local_states = prompt[0]
    token_count = local_states.shape[0]
    positions = positions_of(prompt_blocks, token_count)
    partial_terms = jnp.dot(local_states, key_value_weight, preferred_element_type=jnp.float32)
    summed = lax.psum(partial_terms, "tensor")
    prompt_kv = finish_keys(summed, positions, key_gain)
    landed = from_root(prompt_kv, "section", 0)
    block_pool = fill_slots(landed, block_owner, block_slot, group_index)
    local_len = cache_keys.shape[1]
    partial_out, partial_peak, partial_sum = partial_attention(
        queries, cache_keys, cache_values, decode_lengths, tensor_rank * local_len
    )
    heads_here = H // tensor_count
    merged_out, merged_peak, merged_sum = joined(
        (partial_out, partial_peak, partial_sum), "tensor", combine_partials
    )
    own_out = lax.dynamic_slice_in_dim(merged_out, tensor_rank * heads_here, heads_here, 1)
    own_peak = lax.dynamic_slice_in_dim(merged_peak, tensor_rank * heads_here, heads_here, 1)
    own_sum = lax.dynamic_slice_in_dim(merged_sum, tensor_rank * heads_here, heads_here, 1)
    attended = finish_heads(
        own_out, own_peak, own_sum, queries, new_keys, new_values, tensor_rank, heads_here
    )
    return (attended, block_pool)


def solution(mesh):
    in_specs = (
        P(("parts", "section"), None, "tensor"),
        P("tensor", None),
        P(),
        P("parts"),
        P("parts"),
        P("parts"),
        P(("parts", "section"), None),
        P(("parts", "section"), "tensor", None),
        P(("parts", "section"), "tensor", None),
        P(("parts", "section"), None),
        P(("parts", "section"), None),
        P(("parts", "section")),
    )
    out_specs = (P(("parts", "section"), "tensor"), P(("parts", "section"), None, None, None))
    return jax.shard_map(local, mesh=mesh, in_specs=in_specs, out_specs=out_specs, check_vma=False)
```

profile of v0, /device:TPU:0, one launch (start us, length us, event | category | flops | bytes accessed | tf_op | source)
XLA Modules:
  0.0 160.0 jit_solution(5950931711473255107)
XLA Ops:
  7.2 5.6 %fusion.18 = f32[256,2048]{1,0:T(8,128)} fusion(bf16[1280,2048]{1,0:T(8,128)(2,1)} %param.15, bf16[1,256,1280]{2,1,0:T(8,128)(2,1)} %param.14), kind=kOutput, calls=%fused_computation.36 | convolution fusion | flops 1342177280 | bytes 7995392 | tf_op jit(solution)/shard_map/dot_general | solution.py:179
  12.9 0.5 copy-done.7
  13.7 0.7 fusion.48
  14.5 0.2 fusion.20
  14.7 0.4 fusion.6
  15.2 24.0 %all_gather.9 = f32[4,4,64,128]{3,2,1,0:T(8,128)S(1)} all-gather(f32[1,4,64,128]{3,2,1,0:T(8,128)S(1)} %fusion.6), channel_id=1, replica_groups=mesh['parts'=2,'section'=4,'tensor'=4] {'tensor'}, dimensions={0}, use_global_device_ids=true | all-gather | bytes 655360 | tf_op jit(solution)/shard_map/all_gather | solution.py:28
  39.1 13.0 %all_gather.10 = f32[4,4,64]{2,1,0:T(4,128)S(1)} all-gather(f32[1,4,64]{2,1,0:T(4,128)S(1)} %all_gather_reshape.8), channel_id=1, replica_groups=mesh['parts'=2,'section'=4,'tensor'=4] {'tensor'}, dimensions={0}, use_global_device_ids=true | all-gather | bytes 5120 | tf_op jit(solution)/shard_map/all_gather | solution.py:28
  52.7 0.3 fusion.12
  53.0 12.7 %all_gather.11 = f32[4,4,64]{2,1,0:T(4,128)S(1)} all-gather(f32[1,4,64]{2,1,0:T(4,128)S(1)} %exponential_multiply_fusion), channel_id=1, replica_groups=mesh['parts'=2,'section'=4,'tensor'=4] {'tensor'}, dimensions={0}, use_global_device_ids=true | all-gather | bytes 5120 | tf_op jit(solution)/shard_map/all_gather | solution.py:28
  65.8 0.5 multiply_cosine_fusion
  66.3 0.6 while.14
  66.9 42.0 %all-reduce.3.cloned.1.call-done = f32[256,2048]{1,0:T(8,128)} async-done(((f32[256,2048]{1,0:T(8,128)}), f32[256,2048]{1,0:T(8,128)}) %all-reduce.3.cloned.1.call-update) | async-done | bytes 2097168 | tf_op jit(solution)/shard_map/psum | solution.py:180
  109.0 1.3 slice_bitcast_fusion
  110.5 0.3 multiply_reduce_fusion
  111.1 0.3 multiply_multiply_fusion
  111.5 0.4 subtract_convert_fusion
  111.9 0.3 pad_maximum_fusion
  112.3 1.3 slice.60
  113.8 0.5 reshape.323
  114.4 1.1 copy.78
  115.9 0.6 copy.80
  116.5 34.3 %all-reduce.5.cloned.1.call-done = bf16[16,2048,16]{1,2,0:T(8,128)(2,1)} async-done(((bf16[16,2048,16]{1,2,0:T(8,128)(2,1)}), bf16[16,2048,16]{1,2,0:T(8,128)(2,1)}) %all-reduce.5.cloned.1.call-update) | async-done | bytes 1048592 | tf_op jit(solution)/shard_map/psum | solution.py:24
  150.8 1.5 fusion.3
  152.3 0.9 copy.39
  (59 shorter events, 2.6 us)
Async XLA Ops:
  7.2 6.4 %copy-start = (bf16[4,128,1024]{2,1,0:T(8,128)(2,1)S(1)}, bf16[4,128,1024]{2,1,0:T(8,128)(2,1)}, u32[]{:S(2)}) copy-start(bf16[4,128,1024]{2,1,0:T(8,128)(2,1)} %param.21) | copy-start | bytes 3145732
  7.2 101.8 %all-reduce.3.cloned.1.call-start = ((), (), s32[]{:S(2)}) async-start(), calls=%async_computation | async-start | bytes 4194304 | tf_op jit(solution)/shard_map/psum | solution.py:180
  12.8 0.7 copy-start.7
  12.8 0.9 copy-start.2
  12.8 1.9 %copy-start.1 = (bf16[4,128,1024]{2,1,0:T(8,128)(2,1)S(1)}, bf16[4,128,1024]{2,1,0:T(8,128)(2,1)}, u32[]{:S(2)}) copy-start(bf16[4,128,1024]{2,1,0:T(8,128)(2,1)} %param.22) | copy-start | bytes 3145732
  12.8 39.5 %copy-start.8 = (s32[6]{0:T(128)S(1)}, s32[6]{0:T(128)}, u32[]{:S(2)}) copy-start(s32[6]{0:T(128)} %param.17) | copy-start | bytes 76
  12.8 39.8 %copy-start.3 = (bf16[4,1024]{1,0:T(4,128)(2,1)S(1)}, bf16[4,1024]{1,0:T(4,128)(2,1)}, u32[]{:S(2)}) copy-start(bf16[4,1024]{1,0:T(4,128)(2,1)} %param.23) | copy-start | bytes 24580
  12.9 137.9 %all-reduce.5.cloned.1.call-start = ((), (), s32[]{:S(2)}) async-start(), calls=%async_computation.1 | async-start | bytes 2097152 | tf_op jit(solution)/shard_map/psum | solution.py:24
  110.3 0.8 copy-start.4
  114.4 1.3 copy-start.6
  114.4 2.1 %copy-start.9 = (s32[16]{0:T(128)S(1)}, s32[16]{0:T(128)}, u32[]{:S(2)}) copy-start(s32[16]{0:T(128)} %param.18) | copy-start | bytes 196
  114.4 36.4 %copy-start.5 = (s32[16]{0:T(128)S(1)}, s32[16]{0:T(128)}, u32[]{:S(2)}) copy-start(s32[16]{0:T(128)} %param.19) | copy-start | bytes 196
Sparse Core Ops, SparseCore 0:
  13.0 95.9 all-reduce.2
  115.7 35.0 all-reduce.4
where the time goes:
time: 160 us
  waiting for transfers between devices  76.4 us (48%)
  blocking collectives  49.8 us (31%)
  between operations  14.3 us (9%)
  matrix products  8.7 us (5%)
  local copies, waits for them, and re-layouts  7.17 us (4%)
  other arithmetic  3.57 us (2%)
    all_gather x3, blocking collectives, joined(): pieces = jax.tree.map(lambda part: lax.all_gather(part, axis), value)  49.8 us
    psum x1, waiting for transfers between devices, local(): summed = lax.psum(partial_terms, 'tensor')  42 us
    psum x1, waiting for transfers between devices, from_root(): return lax.psum(block, axis)  34.3 us
    dot_general x1, matrix products, local(): jnp.dot(local_states, key_value_weight, preferred_element_type=jnp.float32)  5.58 us
    unnamed x25, local copies, waits for them, and re-layouts  3.8 us
  transfers between devices with their start and end apart: 2, of which 2 were waited for; matrix products, arithmetic and copies ran while one was open for 3% of the time, Pallas kernels for 0%

commit v1 on v0

--- a/solution.py
+++ b/solution.py
@@ -19,28 +19,55 @@
 MASKED_SCORE = -1e30
 
 
-def from_root(block, axis, holder):
-    block = jnp.where(lax.axis_index(axis) == holder, block, jnp.zeros_like(block))
-    return lax.psum(block, axis)
-
-
-def joined(value, axis, join):
-    pieces = jax.tree.map(lambda part: lax.all_gather(part, axis), value)
-    head = jax.tree.map(lambda part: part[0], pieces)
-    tail = jax.tree.map(lambda part: part[1:], pieces)
-    running, _ = lax.scan(lambda running, share: (join(running, share), None), head, tail)
-    return running
-
-
-def positions_of(prompt_blocks, token_count):
+def exchange(pieces, axis):
+    count = lax.axis_size(axis)
+    rank = lax.axis_index(axis)
+    landed = [lax.dynamic_index_in_dim(pieces, rank, 0, keepdims=False)]
+    for step in range(1, count):
+        piece = lax.dynamic_index_in_dim(pieces, rank ^ step, 0, keepdims=False)
+        landed.append(lax.ppermute(piece, axis, [(i, i ^ step) for i in range(count)]))
+    return landed
+
+
+def collected(own, axis):
+    count = lax.axis_size(axis)
+    rank = lax.axis_index(axis)
+    landed = [own]
+    for step in range(1, count):
+        landed.append(lax.ppermute(own, axis, [(i, i ^ step) for i in range(count)]))
+    stacked = jnp.zeros((count,) + own.shape, own.dtype)
+    for step, piece in enumerate(landed):
+        stacked = lax.dynamic_update_index_in_dim(stacked, piece, rank ^ step, 0)
+    return stacked
+
+
+def rows_for_groups(states, block_owner, block_slot, group_count):
+    slot_ids = jnp.arange(group_count * CAP, dtype=jnp.int32)
+    selector = (block_owner * CAP + block_slot)[None, :] == slot_ids[:, None]
+    filled = jnp.any(selector, axis=1)
+    source = jnp.argmax(selector, axis=1)
+    blocks = states.reshape(NB, BLK, states.shape[1])
+    chosen = jnp.where(filled[:, None, None], blocks[source], jnp.zeros((), states.dtype))
+    return chosen.reshape(group_count, CAP * BLK, states.shape[1])
+
+
+def spread(rows, axis):
+    count = lax.axis_size(axis)
+    landed = jnp.where(lax.axis_index(axis) == 0, rows[0], jnp.zeros_like(rows[0]))
+    for k in range(1, count):
+        landed = landed + lax.ppermute(rows[k], axis, [(0, k)])
+    return landed
+
+
+def slot_positions(prompt_blocks, block_owner, block_slot, group_index):
     prompt_ends = jnp.cumsum(prompt_blocks)
     prompt_starts = prompt_ends - prompt_blocks
-    token_ids = jnp.arange(token_count, dtype=jnp.int32)
-    block_index = token_ids // BLK
-    prompt_index = jnp.sum((block_index[:, None] >= prompt_ends[None, :]).astype(jnp.int32), axis=1)
-    chosen = prompt_index[:, None] == jnp.arange(prompt_ends.shape[0], dtype=jnp.int32)[None, :]
-    first_block = jnp.sum(jnp.where(chosen, prompt_starts[None, :], 0), axis=1)
-    return token_ids - first_block * BLK
+    slot_ids = jnp.arange(CAP, dtype=jnp.int32)
+    selector = (block_owner[None, :] == group_index) & (block_slot[None, :] == slot_ids[:, None])
+    block = jnp.sum(jnp.where(selector, jnp.arange(NB, dtype=jnp.int32)[None, :], 0), axis=1)
+    inside = (block[:, None] >= prompt_starts[None, :]) & (block[:, None] < prompt_ends[None, :])
+    first = jnp.sum(jnp.where(inside, prompt_starts[None, :], 0), axis=1)
+    return (((block - first) * BLK)[:, None] + jnp.arange(BLK, dtype=jnp.int32)[None, :]).reshape(-1)
 
 
 def finish_keys(projected, positions, key_gain):
@@ -65,14 +92,6 @@
     return jnp.concatenate([rotated.reshape(token_count, KVW), projected[:, KVW:]], axis=1).astype(
         jnp.bfloat16
     )
-
-
-def fill_slots(landed, block_owner, block_slot, group_index):
-    blocks = landed.reshape(NB, BLK * landed.shape[1])
-    slot_ids = jnp.arange(CAP, dtype=jnp.int32)
-    selector = (block_owner[None, :] == group_index) & (block_slot[None, :] == slot_ids[:, None])
-    filled = jnp.dot(selector.astype(jnp.bfloat16), blocks, preferred_element_type=jnp.float32)
-    return filled.reshape(1, CAP, BLK, landed.shape[1]).astype(jnp.bfloat16)
 
 
 def partial_attention(queries, cache_keys, cache_values, decode_lengths, first_position):
@@ -173,25 +192,33 @@
     tensor_count = lax.axis_size("tensor")
     tensor_rank = lax.axis_index("tensor")
     group_index = lax.axis_index("section")
-    local_states = prompt[0]
-    token_count = local_states.shape[0]
-    positions = positions_of(prompt_blocks, token_count)
-    partial_terms = jnp.dot(local_states, key_value_weight, preferred_element_type=jnp.float32)
-    summed = lax.psum(partial_terms, "tensor")
-    prompt_kv = finish_keys(summed, positions, key_gain)
-    landed = from_root(prompt_kv, "section", 0)
-    block_pool = fill_slots(landed, block_owner, block_slot, group_index)
+    group_count = lax.axis_size("section")
+    slot_rows = CAP * BLK
+    rows_here = slot_rows // tensor_count
+    rows = rows_for_groups(prompt[0], block_owner, block_slot, group_count)
+    own_rows = spread(rows, "section")
     local_len = cache_keys.shape[1]
+    row_count = queries.shape[0]
+    heads_here = H // tensor_count
     partial_out, partial_peak, partial_sum = partial_attention(
         queries, cache_keys, cache_values, decode_lengths, tensor_rank * local_len
     )
-    heads_here = H // tensor_count
-    merged_out, merged_peak, merged_sum = joined(
-        (partial_out, partial_peak, partial_sum), "tensor", combine_partials
-    )
-    own_out = lax.dynamic_slice_in_dim(merged_out, tensor_rank * heads_here, heads_here, 1)
-    own_peak = lax.dynamic_slice_in_dim(merged_peak, tensor_rank * heads_here, heads_here, 1)
-    own_sum = lax.dynamic_slice_in_dim(merged_sum, tensor_rank * heads_here, heads_here, 1)
+    stats = jnp.stack([partial_peak, partial_sum], axis=-1).reshape(row_count, tensor_count, heads_here, 2)
+    outs = partial_out.reshape(row_count, tensor_count, heads_here, HD)
+    packed = jnp.concatenate([outs, jnp.pad(stats, ((0, 0), (0, 0), (0, 0), (0, HD - 2)))], axis=-1)
+    shares = exchange(packed.transpose(1, 0, 2, 3), "tensor")
+    merged = (shares[0][..., :HD], shares[0][..., HD], shares[0][..., HD + 1])
+    for share in shares[1:]:
+        merged = combine_partials(merged, (share[..., :HD], share[..., HD], share[..., HD + 1]))
+    own_out, own_peak, own_sum = merged
+    partial_terms = jnp.dot(own_rows, key_value_weight, preferred_element_type=jnp.float32)
+    terms = exchange(partial_terms.reshape(tensor_count, rows_here, -1), "tensor")
+    summed = sum(terms[1:], terms[0])
+    positions = lax.dynamic_slice_in_dim(
+        slot_positions(prompt_blocks, block_owner, block_slot, group_index), tensor_rank * rows_here, rows_here, 0
+    )
+    prompt_kv = finish_keys(summed, positions, key_gain)
+    block_pool = collected(prompt_kv, "tensor").reshape(1, CAP, BLK, -1)
     attended = finish_heads(
         own_out, own_peak, own_sum, queries, new_keys, new_values, tensor_rank, heads_here
     )

time: 160 us -> 85 us (0.53)
  blocking collectives: 49.8 us -> 0 us
  waiting for transfers between devices: 76.4 us -> 40.8 us
  starting transfers between devices: 0.08 us -> 21.5 us
  between operations: 14.3 us -> 1.07 us
  other arithmetic: 3.57 us -> 9.11 us
  local copies, waits for them, and re-layouts: 7.17 us -> 4.8 us
    psum x2 -> x0, waiting for transfers between devices: 76.4 us -> none  [the longest x1 42 us: local(): summed = lax.psum(partial_terms, 'tensor')]
    all_gather x3 -> x0, blocking collectives: 49.8 us -> none  [joined(): pieces = jax.tree.map(lambda part: lax.all_gather(part, axis), value)]
    ppermute x0 -> x12, waiting for transfers between devices: none -> 40.8 us  [the longest x6 36.6 us: exchange(): lax.ppermute(piece, axis, [(i, i ^ step) for i in range(count)])]
    ppermute x0 -> x12, starting transfers between devices: none -> 21.5 us  [the longest x6 10.2 us: exchange(): lax.ppermute(piece, axis, [(i, i ^ step) for i in range(count)])]
    dot_general x2 -> x1, matrix products: 7.09 us -> 3.53 us  [local(): jnp.dot(own_rows, key_value_weight, preferred_element_type=jnp.float32)]
    mul x0 -> x4, other arithmetic: none -> 2.1 us  [the longest x2 1.36 us: combine_partials(): former_out * former_factor[..., None]]
    unnamed x25 -> x23, local copies, waits for them, and re-layouts: 3.8 us -> 1.89 us
    another operation x1 -> x6, local copies, waits for them, and re-layouts: 0.08 us -> 1.82 us  [joined(): pieces = jax.tree.map(lambda part: lax.all_gather(part, axis), value)]
  transfers between devices with their start and end apart: 2 -> 12, of which waited for: 2 -> 7; matrix products, arithmetic and copies ran while one was open for 3% -> 12% of each run, Pallas kernels for 0% -> 0%
where the time goes in v1:
time: 85 us; the launch traced here: 84.5 us
  waiting for transfers between devices  40.8 us (48%)
  starting transfers between devices  21.5 us (25%)
  other arithmetic  9.11 us (11%)
  matrix products  7.22 us (8%)
  local copies, waits for them, and re-layouts  4.8 us (6%)
  between operations  1.07 us (1%)
    ppermute x6, waiting for transfers between devices, exchange(): lax.ppermute(piece, axis, [(i, i ^ step) for i in range(count)])  36.6 us
    ppermute x6, starting transfers between devices, exchange(): lax.ppermute(piece, axis, [(i, i ^ step) for i in range(count)])  10.2 us
    ppermute x3, starting transfers between devices, spread(): landed = landed + lax.ppermute(rows[k], axis, [(0, k)])  6.88 us
    ppermute x3, starting transfers between devices, collected(): lax.ppermute(own, axis, [(i, i ^ step) for i in range(count)])  4.45 us
    ppermute x3, waiting for transfers between devices, collected(): lax.ppermute(own, axis, [(i, i ^ step) for i in range(count)])  4.15 us
    dot_general x1, matrix products, local(): jnp.dot(own_rows, key_value_weight, preferred_element_type=jnp.float32)  3.53 us
    unnamed x23, local copies, waits for them, and re-layouts  1.89 us
    another operation x5, local copies, waits for them, and re-layouts  1.74 us
  transfers between devices with their start and end apart: 12, of which 7 were waited for; matrix products, arithmetic and copies ran while one was open for 12% of the time, Pallas kernels for 0%

profile of v1, /device:TPU:0, one launch (start us, length us, event | category | flops | bytes accessed | tf_op | source)
XLA Modules:
  0.0 84.5 jit_solution(10822821242439722269)
XLA Ops:
  0.7 0.8 broadcast_compare_fusion
  1.9 1.6 %fusion.60 = (f32[4,8,8]{2,1,0:T(8,128)S(1)}, f32[4,8,8,128]{3,2,1,0:T(8,128)S(1)}) fusion(bf16[1,4,64,128]{3,1,2,0:T(4,128)(2,1)} %bitcast.158, pred[4,128]{1,0:T(4,128)(4,1)S(1)} %broadcast_compare_fusion, bf16[4,128,1024]{2,1,0:T(8,128)(2,1)S(1)} %copy-done), kind=kOutput, calls=%fused_computation.137 | convolution fusion | flops 8486656 | bytes 1246720 | tf_op jit(solution)/shard_map/rkgd,rpkd->rkgp/dot_general | solution.py:103
  4.1 1.7 %fusion.1 = f32[4,8,1,128,8]{3,4,1,0,2:T(8,128)S(1)} fusion(f32[4,8,8,128]{3,2,1,0:T(8,128)S(1)} %get-tuple-element.31, f32[4,8,8]{2,1,0:T(8,128)S(1)} %subtract_exponential_fusion, f32[4,8,8]{2,1,0:T(8,128)S(1)} %get-tuple-element.30, pred[4,128]{1,0:T(4,128)(4,1)S(1)} %broadcast_compare_fusion, bf16[4,128,1024]{2,1,0:T(8,128)(2,1)} %param.20), kind=kOutput, calls=%fused_computation.4 | convolution fusion | flops 8519680 | bytes 1313280 | tf_op jit(solution)/shard_map/rkgns,rnskd->rkgnd/dot_general | solution.py:116
  6.1 5.1 %collective-permute-start.2 = (f32[4,16,256]{1,0,2:T(4,128)S(1)}, f32[4,16,256]{1,0,2:T(4,128)}, u32[]{:S(2)}, u32[]{:S(2)}) collective-permute-start(f32[4,16,256]{1,0,2:T(4,128)S(1)} %bitcast.151), channel_id=1, source_target_pairs={{0,3},{1,2},{2,1},{3,0},{4,7},{5,6},{6,5},{7,4},{8,11},{9,10},{10,... | collective-permute-start | bytes 196616 | tf_op jit(solution)/shard_map/ppermute | solution.py:28
  11.5 1.0 %copy.52 = f32[4,1,16,256]{2,0,3,1:T(4,128)} copy(f32[4,1,16,256]{3,2,1,0:T(8,128)S(1)} %get-tuple-element.23) | data formatting | bytes 131072 | tf_op jit(solution)/shard_map/dynamic-slice.1
  14.6 0.7 slice_select_fusion
  15.3 2.9 %collective-permute-start.5 = (bf16[64,1280]{1,0:T(8,128)(2,1)}, bf16[64,1280]{1,0:T(8,128)(2,1)}, u32[]{:S(2)}, u32[]{:S(2)}) collective-permute-start(bf16[64,1280]{1,0:T(8,128)(2,1)} %bitcast.25), channel_id=1, source_target_pairs={{0,12},{1,13},{2,14},{3,15},{16,28},{17,29},{18,30},{19,31}} | collective-permute-start | bytes 491528 | tf_op jit(solution)/shard_map/ppermute | solution.py:58
  18.3 2.7 %collective-permute-start.4 = (bf16[64,1280]{1,0:T(8,128)(2,1)S(1)}, bf16[64,1280]{1,0:T(8,128)(2,1)}, u32[]{:S(2)}, u32[]{:S(2)}) collective-permute-start(bf16[64,1280]{1,0:T(8,128)(2,1)S(1)} %bitcast.156), channel_id=1, source_target_pairs={{0,8},{1,9},{2,10},{3,11},{16,24},{17,25},{18,26},{19,27}} | collective-permute-start | bytes 491528 | tf_op jit(solution)/shard_map/ppermute | solution.py:58
  21.5 0.7 convert_bitcast_fusion
  23.4 21.6 %collective-permute-done = f32[4,16,256]{1,0,2:T(4,128)} collective-permute-done((f32[4,16,256]{1,0,2:T(4,128)}, f32[4,16,256]{1,0,2:T(4,128)}, u32[]{:S(2)}, u32[]{:S(2)}) %collective-permute-start) | collective-permute-done | bytes 65568 | tf_op jit(solution)/shard_map/ppermute | solution.py:28
  45.0 1.3 %collective-permute-start.3 = (bf16[64,1280]{1,0:T(8,128)(2,1)S(1)}, bf16[64,1280]{1,0:T(8,128)(2,1)S(1)}, u32[]{:S(2)}, u32[]{:S(2)}) collective-permute-start(bf16[64,1280]{1,0:T(8,128)(2,1)S(1)} %bitcast.155), channel_id=1, source_target_pairs={{0,4},{1,5},{2,6},{3,7},{16,20},{17,21},{18,22},{19,23}} | collective-permute-start | bytes 491528 | tf_op jit(solution)/shard_map/ppermute | solution.py:58
  47.0 9.1 %collective-permute-done.1 = f32[4,16,256]{1,0,2:T(4,128)} collective-permute-done((f32[4,16,256]{1,0,2:T(4,128)S(1)}, f32[4,16,256]{1,0,2:T(4,128)}, u32[]{:S(2)}, u32[]{:S(2)}) %collective-permute-start.1) | collective-permute-done | bytes 65568 | tf_op jit(solution)/shard_map/ppermute | solution.py:28
  56.8 0.7 fusion.54
  57.5 1.0 %fusion.18 = bf16[64,1280]{1,0:T(8,128)(2,1)S(1)} fusion(bf16[64,1280]{1,0:T(8,128)(2,1)} %collective-permute-done.5, bf16[64,1280]{1,0:T(8,128)(2,1)} %collective-permute-done.4, bf16[64,1280]{1,0:T(8,128)(2,1)S(1)} %collective-permute-done.3, bf16[4,16,1280]{2,1,0:T(8,128)(2,1)S(1)} %get-tuple-element.8), kind=kLoop, calls=%fused_computation.32 | loop fusion | flops 245760 | bytes 819200 | tf_op jit(solution)/shard_map/add | solution.py:58
  58.6 3.5 %fusion.61 = f32[64,2048]{1,0:T(8,128)S(1)} fusion(bf16[64,1280]{1,0:T(8,128)(2,1)S(1)} %fusion.18, bf16[1280,2048]{1,0:T(8,128)(2,1)} %param.13), kind=kOutput, calls=%fused_computation.139 | convolution fusion | flops 335544320 | bytes 5931008 | tf_op jit(solution)/shard_map/dot_general | solution.py:214
  62.1 2.5 %collective-permute-start.8 = (f32[16,2048]{1,0:T(8,128)S(1)}, f32[16,2048]{1,0:T(8,128)S(1)}, u32[]{:S(2)}, u32[]{:S(2)}) collective-permute-start(f32[16,2048]{1,0:T(8,128)S(1)} %get-tuple-element.18), channel_id=1, source_target_pairs={{0,3},{1,2},{2,1},{3,0},{4,7},{5,6},{6,5},{7,4},{8,11},{9,10},{10,... | collective-permute-start | bytes 393224 | tf_op jit(solution)/shard_map/ppermute | solution.py:28
  64.7 1.9 %collective-permute-start.6 = (f32[16,2048]{1,0:T(8,128)S(1)}, f32[16,2048]{1,0:T(8,128)S(1)}, u32[]{:S(2)}, u32[]{:S(2)}) collective-permute-start(f32[16,2048]{1,0:T(8,128)S(1)} %get-tuple-element.17), channel_id=1, source_target_pairs={{0,1},{1,0},{2,3},{3,2},{4,5},{5,4},{6,7},{7,6},{8,9},{9,8},{10,11... | collective-permute-start | bytes 393224 | tf_op jit(solution)/shard_map/ppermute | solution.py:28
  66.6 1.4 %fusion.16 = bf16[4,16,128]{1,0,2:T(4,128)(2,1)S(1)} fusion(f32[16,4,128]{0,1,2:T(4,128)S(1)} %copy.55, f32[4,16,256]{1,0,2:T(4,128)} %collective-permute-done.2, f32[4,16,256]{1,0,2:T(4,128)} %collective-permute-done.1, f32[4,16,256]{1,0,2:T(4,128)} %collective-permute-done, f32[4,16,256]{1,0,2:T(4,128)S(1)} %bitcast.148, ...), kind=kLoop, calls=%fused_computation.28 | loop fusion | flops 114688 | bytes 182528 | tf_op jit(solution)/shard_map/convert_element_type | solution.py:175
  68.7 1.8 %collective-permute-done.8 = f32[16,2048]{1,0:T(8,128)S(1)} collective-permute-done((f32[16,2048]{1,0:T(8,128)S(1)}, f32[16,2048]{1,0:T(8,128)S(1)}, u32[]{:S(2)}, u32[]{:S(2)}) %collective-permute-start.8) | collective-permute-done | bytes 131104 | tf_op jit(solution)/shard_map/ppermute | solution.py:28
  70.4 4.2 %collective-permute-done.7 = f32[16,2048]{1,0:T(8,128)S(1)} collective-permute-done((f32[16,2048]{1,0:T(8,128)S(1)}, f32[16,2048]{1,0:T(8,128)S(1)}, u32[]{:S(2)}, u32[]{:S(2)}) %collective-permute-start.7) | collective-permute-done | bytes 131104 | tf_op jit(solution)/shard_map/ppermute | solution.py:28
  75.3 2.4 %collective-permute-start.10 = (bf16[16,2048]{1,0:T(8,128)(2,1)S(1)}, bf16[16,2048]{1,0:T(8,128)(2,1)S(1)}, u32[]{:S(2)}, u32[]{:S(2)}) collective-permute-start(bf16[16,2048]{1,0:T(8,128)(2,1)S(1)} %pad_maximum_fusion), channel_id=1, source_target_pairs={{0,2},{1,3},{2,0},{3,1},{4,6},{5,7},{6,4},{7,5},{8,10},{9,11},{10,... | collective-permute-start | bytes 196616 | tf_op jit(solution)/shard_map/ppermute | solution.py:37
  77.7 1.9 %collective-permute-start.11 = (bf16[16,2048]{1,0:T(8,128)(2,1)S(1)}, bf16[16,2048]{1,0:T(8,128)(2,1)S(1)}, u32[]{:S(2)}, u32[]{:S(2)}) collective-permute-start(bf16[16,2048]{1,0:T(8,128)(2,1)S(1)} %pad_maximum_fusion), channel_id=1, source_target_pairs={{0,3},{1,2},{2,1},{3,0},{4,7},{5,6},{6,5},{7,4},{8,11},{9,10},{10,... | collective-permute-start | bytes 196616 | tf_op jit(solution)/shard_map/ppermute | solution.py:37
  80.1 3.0 %collective-permute-done.10 = bf16[16,2048]{1,0:T(8,128)(2,1)S(1)} collective-permute-done((bf16[16,2048]{1,0:T(8,128)(2,1)S(1)}, bf16[16,2048]{1,0:T(8,128)(2,1)S(1)}, u32[]{:S(2)}, u32[]{:S(2)}) %collective-permute-start.10) | collective-permute-done | bytes 65568 | tf_op jit(solution)/shard_map/ppermute | solution.py:37
  83.0 0.8 collective-permute-done.11
  (86 shorter events, 9.2 us)
Async XLA Ops:
  0.6 1.2 %copy-start = (bf16[4,128,1024]{2,1,0:T(8,128)(2,1)S(1)}, bf16[4,128,1024]{2,1,0:T(8,128)(2,1)}, u32[]{:S(2)}) copy-start(bf16[4,128,1024]{2,1,0:T(8,128)(2,1)} %param.19) | copy-start | bytes 3145732
  0.6 12.4 %copy-start.7 = (s32[16]{0:T(128)S(1)}, s32[16]{0:T(128)}, u32[]{:S(2)}) copy-start(s32[16]{0:T(128)} %param.17) | copy-start | bytes 196
  0.7 12.4 %copy-start.6 = (s32[16]{0:T(128)S(1)}, s32[16]{0:T(128)}, u32[]{:S(2)}) copy-start(s32[16]{0:T(128)} %param.16) | copy-start | bytes 196
  0.7 13.2 %copy-start.1 = (bf16[1,256,1280]{2,1,0:T(8,128)(2,1)S(1)}, bf16[1,256,1280]{2,1,0:T(8,128)(2,1)}, u32[]{:S(2)}) copy-start(bf16[1,256,1280]{2,1,0:T(8,128)(2,1)} %param.12) | copy-start | bytes 1966084
  0.7 20.3 %copy-start.3 = (bf16[4,1024]{1,0:T(4,128)(2,1)S(1)}, bf16[4,1024]{1,0:T(4,128)(2,1)}, u32[]{:S(2)}) copy-start(bf16[4,1024]{1,0:T(4,128)(2,1)} %param.22) | copy-start | bytes 24580
  1.9 20.5 %copy-start.8 = (s32[6]{0:T(128)S(1)}, s32[6]{0:T(128)}, u32[]{:S(2)}) copy-start(s32[6]{0:T(128)} %param.15) | copy-start | bytes 76
  1.9 21.2 %copy-start.4 = (bf16[4,1024]{1,0:T(4,128)(2,1)S(1)}, bf16[4,1024]{1,0:T(4,128)(2,1)}, u32[]{:S(2)}) copy-start(bf16[4,1024]{1,0:T(4,128)(2,1)} %param.21) | copy-start | bytes 24580
  6.1 40.9 %collective-permute-start.2 = (f32[4,16,256]{1,0,2:T(4,128)S(1)}, f32[4,16,256]{1,0,2:T(4,128)}, u32[]{:S(2)}, u32[]{:S(2)}) collective-permute-start(f32[4,16,256]{1,0,2:T(4,128)S(1)} %bitcast.151), channel_id=1, source_target_pairs={{0,3},{1,2},{2,1},{3,0},{4,7},{5,6},{6,5},{7,4},{8,11},{9,10},{10,... | collective-permute-start | bytes 196616 | tf_op jit(solution)/shard_map/ppermute | solution.py:28
  11.4 44.6 %collective-permute-start.1 = (f32[4,16,256]{1,0,2:T(4,128)S(1)}, f32[4,16,256]{1,0,2:T(4,128)}, u32[]{:S(2)}, u32[]{:S(2)}) collective-permute-start(f32[4,16,256]{1,0,2:T(4,128)S(1)} %bitcast.152), channel_id=1, source_target_pairs={{0,2},{1,3},{2,0},{3,1},{4,6},{5,7},{6,4},{7,5},{8,10},{9,11},{10,... | collective-permute-start | bytes 196616 | tf_op jit(solution)/shard_map/ppermute | solution.py:28
  12.5 32.5 %collective-permute-start = (f32[4,16,256]{1,0,2:T(4,128)}, f32[4,16,256]{1,0,2:T(4,128)}, u32[]{:S(2)}, u32[]{:S(2)}) collective-permute-start(f32[4,16,256]{1,0,2:T(4,128)} %bitcast.5), channel_id=1, source_target_pairs={{0,1},{1,0},{2,3},{3,2},{4,5},{5,4},{6,7},{7,6},{8,9},{9,8},{10,11... | collective-permute-start | bytes 196616 | tf_op jit(solution)/shard_map/ppermute | solution.py:28
  15.3 42.2 %collective-permute-start.5 = (bf16[64,1280]{1,0:T(8,128)(2,1)}, bf16[64,1280]{1,0:T(8,128)(2,1)}, u32[]{:S(2)}, u32[]{:S(2)}) collective-permute-start(bf16[64,1280]{1,0:T(8,128)(2,1)} %bitcast.25), channel_id=1, source_target_pairs={{0,12},{1,13},{2,14},{3,15},{16,28},{17,29},{18,30},{19,31}} | collective-permute-start | bytes 491528 | tf_op jit(solution)/shard_map/ppermute | solution.py:58
  18.3 39.2 %collective-permute-start.4 = (bf16[64,1280]{1,0:T(8,128)(2,1)S(1)}, bf16[64,1280]{1,0:T(8,128)(2,1)}, u32[]{:S(2)}, u32[]{:S(2)}) collective-permute-start(bf16[64,1280]{1,0:T(8,128)(2,1)S(1)} %bitcast.156), channel_id=1, source_target_pairs={{0,8},{1,9},{2,10},{3,11},{16,24},{17,25},{18,26},{19,27}} | collective-permute-start | bytes 491528 | tf_op jit(solution)/shard_map/ppermute | solution.py:58
  22.8 52.0 %copy-start.5 = (f32[128]{0:T(128)S(1)}, f32[128]{0:T(128)}, u32[]{:S(2)}) copy-start(f32[128]{0:T(128)} %param.14) | copy-start | bytes 1540
  45.0 12.5 %collective-permute-start.3 = (bf16[64,1280]{1,0:T(8,128)(2,1)S(1)}, bf16[64,1280]{1,0:T(8,128)(2,1)S(1)}, u32[]{:S(2)}, u32[]{:S(2)}) collective-permute-start(bf16[64,1280]{1,0:T(8,128)(2,1)S(1)} %bitcast.155), channel_id=1, source_target_pairs={{0,4},{1,5},{2,6},{3,7},{16,20},{17,21},{18,22},{19,23}} | collective-permute-start | bytes 491528 | tf_op jit(solution)/shard_map/ppermute | solution.py:58
  62.1 8.3 %collective-permute-start.8 = (f32[16,2048]{1,0:T(8,128)S(1)}, f32[16,2048]{1,0:T(8,128)S(1)}, u32[]{:S(2)}, u32[]{:S(2)}) collective-permute-start(f32[16,2048]{1,0:T(8,128)S(1)} %get-tuple-element.18), channel_id=1, source_target_pairs={{0,3},{1,2},{2,1},{3,0},{4,7},{5,6},{6,5},{7,4},{8,11},{9,10},{10,... | collective-permute-start | bytes 393224 | tf_op jit(solution)/shard_map/ppermute | solution.py:28
  64.7 9.9 %collective-permute-start.7 = (f32[16,2048]{1,0:T(8,128)S(1)}, f32[16,2048]{1,0:T(8,128)S(1)}, u32[]{:S(2)}, u32[]{:S(2)}) collective-permute-start(f32[16,2048]{1,0:T(8,128)S(1)} %get-tuple-element.19), channel_id=1, source_target_pairs={{0,2},{1,3},{2,0},{3,1},{4,6},{5,7},{6,4},{7,5},{8,10},{9,11},{10,... | collective-permute-start | bytes 393224 | tf_op jit(solution)/shard_map/ppermute | solution.py:28
  64.7 9.9 %collective-permute-start.6 = (f32[16,2048]{1,0:T(8,128)S(1)}, f32[16,2048]{1,0:T(8,128)S(1)}, u32[]{:S(2)}, u32[]{:S(2)}) collective-permute-start(f32[16,2048]{1,0:T(8,128)S(1)} %get-tuple-element.17), channel_id=1, source_target_pairs={{0,1},{1,0},{2,3},{3,2},{4,5},{5,4},{6,7},{7,6},{8,9},{9,8},{10,11... | collective-permute-start | bytes 393224 | tf_op jit(solution)/shard_map/ppermute | solution.py:28
  75.1 4.9 %collective-permute-start.9 = (bf16[16,2048]{1,0:T(8,128)(2,1)S(1)}, bf16[16,2048]{1,0:T(8,128)(2,1)S(1)}, u32[]{:S(2)}, u32[]{:S(2)}) collective-permute-start(bf16[16,2048]{1,0:T(8,128)(2,1)S(1)} %pad_maximum_fusion), channel_id=1, source_target_pairs={{0,1},{1,0},{2,3},{3,2},{4,5},{5,4},{6,7},{7,6},{8,9},{9,8},{10,11... | collective-permute-start | bytes 196616 | tf_op jit(solution)/shard_map/ppermute | solution.py:37
  75.3 7.7 %collective-permute-start.10 = (bf16[16,2048]{1,0:T(8,128)(2,1)S(1)}, bf16[16,2048]{1,0:T(8,128)(2,1)S(1)}, u32[]{:S(2)}, u32[]{:S(2)}) collective-permute-start(bf16[16,2048]{1,0:T(8,128)(2,1)S(1)} %pad_maximum_fusion), channel_id=1, source_target_pairs={{0,2},{1,3},{2,0},{3,1},{4,6},{5,7},{6,4},{7,5},{8,10},{9,11},{10,... | collective-permute-start | bytes 196616 | tf_op jit(solution)/shard_map/ppermute | solution.py:37
  77.7 6.1 %collective-permute-start.11 = (bf16[16,2048]{1,0:T(8,128)(2,1)S(1)}, bf16[16,2048]{1,0:T(8,128)(2,1)S(1)}, u32[]{:S(2)}, u32[]{:S(2)}) collective-permute-start(bf16[16,2048]{1,0:T(8,128)(2,1)S(1)} %pad_maximum_fusion), channel_id=1, source_target_pairs={{0,3},{1,2},{2,1},{3,0},{4,7},{5,6},{6,5},{7,4},{8,11},{9,10},{10,... | collective-permute-start | bytes 196616 | tf_op jit(solution)/shard_map/ppermute | solution.py:37
  83.8 0.7 copy-start.2

commit v2 on v1

--- a/solution.py
+++ b/solution.py
@@ -1,6 +1,8 @@
 import jax
 import jax.numpy as jnp
 from jax import lax
+from jax.experimental import pallas as pl
+from jax.experimental.pallas import tpu as pltpu
 from jax.sharding import PartitionSpec as P
 
 H = 64
@@ -175,7 +177,7 @@
     return (numerator / denominator[..., None]).reshape(row_count, own_width).astype(jnp.bfloat16)
 
 
-def local(
+def local_small_shares(
     prompt,
     key_value_weight,
     key_gain,
@@ -225,6 +227,296 @@
     return (attended, block_pool)
 
 
+VMEM = pl.BlockSpec(memory_space=pltpu.VMEM)
+SMEM = pl.BlockSpec(memory_space=pltpu.SMEM)
+ANY = pl.BlockSpec(memory_space=pl.ANY)
+F32 = jnp.float32
+BF16 = jnp.bfloat16
+
+
+def on_chip(kernel, operands, in_specs, out_shapes, scratch=(), flops=0, moved=0):
+    return pl.pallas_call(
+        kernel,
+        out_shape=out_shapes,
+        in_specs=in_specs,
+        out_specs=[VMEM] * len(out_shapes),
+        scratch_shapes=list(scratch),
+        compiler_params=pltpu.CompilerParams(vmem_limit_bytes=40 * 1024 * 1024),
+        cost_estimate=pl.CostEstimate(flops=flops, bytes_accessed=moved, transcendentals=0),
+    )(*operands)
+
+
+def place_rows(states, block_owner, block_slot, group_count):
+    width = states.shape[1]
+    slot_count = group_count * CAP
+
+    def kernel(owner_ref, slot_ref, states_ref, *refs):
+        row_refs, source_ref, sems = refs[:group_count], refs[group_count], refs[group_count + 1]
+        for j in range(slot_count):
+            source_ref[j] = -1
+        for b in range(NB):
+            source_ref[owner_ref[b] * CAP + slot_ref[b]] = b
+
+        def copy_of(j, b):
+            start = pl.multiple_of(b * BLK, BLK)
+            target = row_refs[j // CAP].at[pl.ds((j % CAP) * BLK, BLK)]
+            return pltpu.make_async_copy(states_ref.at[pl.ds(start, BLK)], target, sems.at[j])
+
+        for j in range(slot_count):
+            b = source_ref[j]
+
+            @pl.when(b >= 0)
+            def _():
+                copy_of(j, b).start()
+
+            @pl.when(b < 0)
+            def _():
+                row_refs[j // CAP][pl.ds((j % CAP) * BLK, BLK), :] = jnp.zeros((BLK, width), BF16)
+
+        for j in range(slot_count):
+            b = source_ref[j]
+
+            @pl.when(b >= 0)
+            def _():
+                copy_of(j, b).wait()
+
+    return on_chip(
+        kernel,
+        (block_owner, block_slot, states),
+        [SMEM, SMEM, ANY],
+        [jax.ShapeDtypeStruct((CAP * BLK, width), BF16)] * group_count,
+        [pltpu.SMEM((slot_count,), jnp.int32), pltpu.SemaphoreType.DMA((slot_count,))],
+        moved=states.size * 4,
+    )
+
+
+def attend_span(queries, cache_keys, cache_values, decode_lengths, tensor_count):
+    row_count, local_len = cache_keys.shape[0], cache_keys.shape[1]
+    heads_here = H // tensor_count
+    out_rows = row_count * heads_here
+
+    def kernel(length_ref, query_ref, key_ref, value_ref, *refs):
+        share_refs, held = refs[:tensor_count], refs[tensor_count]
+        rank = lax.axis_index("tensor")
+        first = rank * local_len
+        place = lax.broadcasted_iota(jnp.int32, (1, local_len), 1) + first
+        lane = lax.broadcasted_iota(jnp.int32, (G, HD), 1)
+        stats = jnp.zeros((G, HD), F32)
+        for r in range(row_count):
+            live = place < length_ref[r]
+            for pair in range(KVH // 2):
+                pair_queries = query_ref[r, pl.ds(pair * 2 * G, 2 * G), :]
+                weights = []
+                for half in range(2):
+                    n = pair * 2 + half
+                    scores = lax.dot_general(
+                        pair_queries,
+                        key_ref[r, :, n * HD : (n + 1) * HD],
+                        (((1,), (1,)), ((), ())),
+                        preferred_element_type=F32,
+                    )[half * G : (half + 1) * G] * HD ** (-0.5)
+                    scores = jnp.where(live, scores, MASKED_SCORE)
+                    peak = jnp.max(scores, axis=1, keepdims=True)
+                    weight = jnp.where(live, jnp.exp(scores - peak), 0.0)
+                    total = jnp.sum(weight, axis=1, keepdims=True)
+                    stats = jnp.where(lane == 2 * KVH * r + n, peak, stats)
+                    stats = jnp.where(lane == 2 * KVH * r + KVH + n, total, stats)
+                    weights.append(weight)
+                rounded = jnp.concatenate(weights, axis=0).astype(BF16)
+                for half in range(2):
+                    n = pair * 2 + half
+                    out = jnp.dot(rounded, value_ref[r, :, n * HD : (n + 1) * HD], preferred_element_type=F32)
+                    held[r, pl.ds(n * G, G), :] = out[half * G : (half + 1) * G]
+        for step in range(tensor_count):
+            start = pl.multiple_of((rank ^ step) * heads_here, heads_here)
+            for r in range(row_count):
+                share_refs[step][pl.ds(r * heads_here, heads_here), :] = held[r, pl.ds(start, heads_here), :]
+            share_refs[step][pl.ds(out_rows, G), :] = stats
+
+    return on_chip(
+        kernel,
+        (decode_lengths, queries.reshape(row_count, H, HD), cache_keys, cache_values),
+        [SMEM, VMEM, VMEM, VMEM],
+        [jax.ShapeDtypeStruct((out_rows + G, HD), F32)] * tensor_count,
+        [pltpu.VMEM((row_count, H, HD), F32)],
+        flops=4 * row_count * H * HD * local_len,
+        moved=4 * cache_keys.size,
+    )
+
+
+def merge_spans(shares, queries, new_keys, new_values, heads_here):
+    row_count = queries.shape[0]
+    share_count = len(shares)
+    keys_here = heads_here // G
+    out_rows = row_count * heads_here
+
+    def kernel(*refs):
+        share_refs = refs[:share_count]
+        query_ref, key_ref, value_ref, out_ref = refs[share_count:]
+        rank = lax.axis_index("tensor")
+        lane = lax.broadcasted_iota(jnp.int32, (G, HD), 1)
+        stats = [ref[pl.ds(out_rows, G), :] for ref in share_refs]
+        for r in range(row_count):
+            for kk in range(keys_here):
+                n = rank * keys_here + kk
+
+                def column(tile, index):
+                    return jnp.sum(jnp.where(lane == index, tile, 0.0), axis=1, keepdims=True)
+
+                query = query_ref[r, pl.ds(pl.multiple_of(n * G, G), G), :]
+                column_start = pl.multiple_of(n * HD, HD)
+                new_key = key_ref[pl.ds(r, 1), pl.ds(column_start, HD)]
+                new_value = value_ref[pl.ds(r, 1), pl.ds(column_start, HD)]
+                self_score = jnp.sum(query * new_key, axis=1, keepdims=True) * HD ** (-0.5)
+                peaks = [column(tile, 2 * KVH * r + n) for tile in stats]
+                sums = [column(tile, 2 * KVH * r + KVH + n) for tile in stats]
+                row_peak = self_score
+                for peak in peaks:
+                    row_peak = jnp.maximum(row_peak, peak)
+                self_weight = jnp.exp(self_score - row_peak)
+                numerator = self_weight * new_value
+                denominator = self_weight
+                for ref, peak, total in zip(share_refs, peaks, sums):
+                    factor = jnp.exp(peak - row_peak)
+                    numerator += factor * ref[pl.ds(r * heads_here + kk * G, G), :]
+                    denominator += factor * total
+                out_ref[r, pl.ds(kk * G, G), :] = numerator / denominator
+
+    attended = on_chip(
+        kernel,
+        (*shares, queries.reshape(row_count, H, HD).astype(F32), new_keys.astype(F32), new_values.astype(F32)),
+        [VMEM] * (share_count + 3),
+        [jax.ShapeDtypeStruct((row_count, heads_here, HD), F32)],
+    )[0]
+    return attended.astype(BF16).reshape(row_count, heads_here * HD)
+
+
+def project_rows(candidates, weight, tensor_count):
+    slot_rows, depth = candidates[0].shape
+    width = weight.shape[1]
+    rows_here = slot_rows // tensor_count
+    count = len(candidates)
+    step_width = 512
+
+    def kernel(*refs):
+        candidate_refs, weight_ref = refs[:count], refs[count]
+        share_refs, rows_ref, held = refs[count + 1 : count + 1 + tensor_count], refs[-2], refs[-1]
+        group = lax.axis_index("section")
+        rank = lax.axis_index("tensor")
+        for k in range(count):
+
+            @pl.when(group == k)
+            def _():
+                rows_ref[...] = candidate_refs[k][...]
+
+        for c in range(width // step_width):
+            columns = pl.ds(c * step_width, step_width)
+            held[:, columns] = jnp.dot(rows_ref[...], weight_ref[:, columns], preferred_element_type=F32)
+        for step in range(tensor_count):
+            start = pl.multiple_of((rank ^ step) * rows_here, rows_here)
+            share_refs[step][...] = held[pl.ds(start, rows_here), :]
+
+    return on_chip(
+        kernel,
+        (*candidates, weight),
+        [VMEM] * (count + 1),
+        [jax.ShapeDtypeStruct((rows_here, width), F32)] * tensor_count,
+        [pltpu.VMEM((slot_rows, depth), BF16), pltpu.VMEM((slot_rows, width), F32)],
+        flops=2 * slot_rows * depth * width,
+        moved=2 * weight.size,
+    )
+
+
+def finish_rows(shares, cosine, sine, gain):
+    share_count = len(shares)
+    rows, width = shares[0].shape
+
+    def kernel(*refs):
+        share_refs = refs[:share_count]
+        cosine_ref, sine_ref, gain_ref, out_ref = refs[share_count:]
+        for n in range(width // HD):
+            columns = pl.ds(n * HD, HD)
+            total = share_refs[0][:, columns]
+            for ref in share_refs[1:]:
+                total = total + ref[:, columns]
+            if n < KVH:
+                mean = jnp.sum(total * total, axis=1, keepdims=True) * (1.0 / HD)
+                total = total * lax.rsqrt(mean + NORM_EPSILON) * gain_ref[...]
+                total = total * cosine_ref[...] + pltpu.roll(total, HD // 2, 1) * sine_ref[...]
+            out_ref[:, columns] = total.astype(BF16)
+
+    return on_chip(
+        kernel,
+        (*shares, cosine, sine, gain),
+        [VMEM] * (share_count + 3),
+        [jax.ShapeDtypeStruct((rows, width), BF16)],
+    )[0]
+
+
+def join_rows(pieces):
+    count = len(pieces)
+    rows, width = pieces[0].shape
+
+    def kernel(*refs):
+        piece_refs, out_ref = refs[:count], refs[count]
+        rank = lax.axis_index("tensor")
+        for step in range(count):
+            out_ref[pl.ds(pl.multiple_of((rank ^ step) * rows, rows), rows), :] = piece_refs[step][...]
+
+    return on_chip(
+        kernel, pieces, [VMEM] * count, [jax.ShapeDtypeStruct((count * rows, width), BF16)]
+    )[0]
+
+
+def rotation_tables(positions):
+    frequency = ROPE_BASE ** (jnp.arange(HD // 2, dtype=F32) * (-2.0 / HD))
+    angles = positions.astype(F32)[:, None] * frequency[None, :]
+    cosine, sine = jnp.cos(angles), jnp.sin(angles)
+    return jnp.concatenate([cosine, cosine], axis=1), jnp.concatenate([-sine, sine], axis=1)
+
+
+def swapped(pieces, axis):
+    count = lax.axis_size(axis)
+    return [pieces[0]] + [
+        lax.ppermute(pieces[k], axis, [(i, i ^ k) for i in range(count)]) for k in range(1, count)
+    ]
+
+
+def local(
+    prompt,
+    key_value_weight,
+    key_gain,
+    prompt_blocks,
+    block_owner,
+    block_slot,
+    queries,
+    cache_keys,
+    cache_values,
+    new_keys,
+    new_values,
+    decode_lengths,
+):
+    tensor_count = lax.axis_size("tensor")
+    tensor_rank = lax.axis_index("tensor")
+    group_count = lax.axis_size("section")
+    group_index = lax.axis_index("section")
+    rows_here = CAP * BLK // tensor_count
+    heads_here = H // tensor_count
+    rows = place_rows(prompt[0], block_owner, block_slot, group_count)
+    candidates = [rows[0]] + [lax.ppermute(rows[k], "section", [(0, k)]) for k in range(1, group_count)]
+    span_shares = attend_span(queries, cache_keys, cache_values, decode_lengths, tensor_count)
+    span_shares = swapped(span_shares, "tensor")
+    positions = lax.dynamic_slice_in_dim(
+        slot_positions(prompt_blocks, block_owner, block_slot, group_index), tensor_rank * rows_here, rows_here, 0
+    )
+    cosine, sine = rotation_tables(positions)
+    terms = swapped(project_rows(candidates, key_value_weight, tensor_count), "tensor")
+    finished = finish_rows(terms, cosine, sine, key_gain[None, :])
+    block_pool = join_rows(swapped([finished] * tensor_count, "tensor"))
+    attended = merge_spans(span_shares, queries, new_keys, new_values, heads_here)
+    return (attended, block_pool.reshape(1, CAP, BLK, -1))
+
+
 def solution(mesh):
     in_specs = (
         P(("parts", "section"), None, "tensor"),
@@ -241,4 +533,7 @@
         P(("parts", "section")),
     )
     out_specs = (P(("parts", "section"), "tensor"), P(("parts", "section"), None, None, None))
-    return jax.shard_map(local, mesh=mesh, in_specs=in_specs, out_specs=out_specs, check_vma=False)
+    tensor_count = mesh.shape["tensor"]
+    whole_tiles = (CAP * BLK) % (16 * tensor_count) == 0 and H % (G * tensor_count) == 0
+    program = local if whole_tiles else local_small_shares
+    return jax.shard_map(program, mesh=mesh, in_specs=in_specs, out_specs=out_specs, check_vma=False)

time: 85 us -> 53.7 us (0.63)
  waiting for transfers between devices: 40.8 us -> 9.8 us
  Pallas kernels: 0 us -> 8.38 us
  matrix products: 7.22 us -> 0 us
  other arithmetic: 9.11 us -> 4.34 us
  local copies, waits for them, and re-layouts: 4.8 us -> 8.68 us
    ppermute x12, waiting for transfers between devices: 40.8 us -> 9.8 us  [the longest x9 9.78 us: swapped(): lax.ppermute(pieces[k], axis, [(i, i ^ k) for i in range(count)])]
    pallas_call x0 -> x6, Pallas kernels: none -> 8.38 us  [on_chip(): pl.pallas_call(kernel, out_shape=out_shapes, in_specs=in_specs, out_specs...]
    dot_general x5 -> x0, matrix products: 7.22 us -> none  [the longest x1 3.53 us: local(): jnp.dot(own_rows, key_value_weight, preferred_element_type=jnp.float32)]
    unnamed x23 -> x21, local copies, waits for them, and re-layouts: 1.89 us -> 8.6 us
    mul x5 -> x0, other arithmetic: 2.18 us -> none  [the longest x2 1.36 us: combine_partials(): former_out * former_factor[..., None]]
    another operation x6 -> x0, local copies, waits for them, and re-layouts: 1.82 us -> none
    add x4 -> x0, other arithmetic: 1.07 us -> none  [the longest x1 1.04 us: spread(): landed = landed + lax.ppermute(rows[k], axis, [(0, k)])]
  transfers between devices with their start and end apart: 12 -> 12, of which waited for: 7 -> 4; matrix products, arithmetic and copies ran while one was open for 12% -> 9% of each run, Pallas kernels for 0% -> 11%
where the time goes in v2:
time: 53.7 us; the launch traced here: 53.3 us
  starting transfers between devices  21.3 us (40%)
  waiting for transfers between devices  9.8 us (18%)
  local copies, waits for them, and re-layouts  8.68 us (16%)
  Pallas kernels  8.38 us (16%)
  other arithmetic  4.34 us (8%)
  between operations  0.81 us (2%)
    ppermute x9, starting transfers between devices, swapped(): lax.ppermute(pieces[k], axis, [(i, i ^ k) for i in range(count)])  14.5 us
    ppermute x9, waiting for transfers between devices, swapped(): lax.ppermute(pieces[k], axis, [(i, i ^ k) for i in range(count)])  9.78 us
    unnamed x21, local copies, waits for them, and re-layouts  8.6 us
    pallas_call x6, Pallas kernels, on_chip(): pl.pallas_call(kernel, out_shape=out_shapes, in_specs=in_specs, out_specs...  8.38 us
    ppermute x3, starting transfers between devices, local(): lax.ppermute(rows[k], 'section', [(0, k)])  6.82 us
  transfers between devices with their start and end apart: 12, of which 4 were waited for; matrix products, arithmetic and copies ran while one was open for 9% of the time, Pallas kernels for 11%

profile of v2, /device:TPU:0, one launch (start us, length us, event | category | flops | bytes accessed | tf_op | source)
XLA Modules:
  0.0 53.3 jit_solution(6869994464980816531)
XLA Ops:
  0.7 1.1 %copy-done.3 = bf16[1,256,1280]{2,1,0:T(8,128)(2,1)S(1)} copy-done((bf16[1,256,1280]{2,1,0:T(8,128)(2,1)S(1)}, bf16[1,256,1280]{2,1,0:T(8,128)(2,1)}, u32[]{:S(2)}) %copy-start.3) | copy-done | bytes 655384
  3.1 1.8 %shard_map.133 = (bf16[64,1280]{1,0:T(8,128)(2,1)S(1)}, bf16[64,1280]{1,0:T(8,128)(2,1)S(1)}, bf16[64,1280]{1,0:T(8,128)(2,1)S(1)}, bf16[64,1280]{1,0:T(8,128)(2,1)S(1)}) custom-call(s32[16]{0:T(128)S(1)} %copy-done.5, s32[16]{0:T(128)S(1)} %copy-done.6, bf16[256,1280]{1,0:T(8,128)(2,1)S(1)} %bitcast.16), custom_call_target="tpu_custom_call" | custom-call | bytes 1310720 | tf_op jit(solution)/shard_map/pallas_call | solution.py:238
  4.9 2.4 %collective-permute-start.3 = (bf16[64,1280]{1,0:T(8,128)(2,1)S(1)}, bf16[64,1280]{1,0:T(8,128)(2,1)S(1)}, u32[]{:S(2)}, u32[]{:S(2)}) collective-permute-start(bf16[64,1280]{1,0:T(8,128)(2,1)S(1)} %get-tuple-element.19), channel_id=1, source_target_pairs={{0,4},{1,5},{2,6},{3,7},{16,20},{17,21},{18,22},{19,23}} | collective-permute-start | bytes 491528 | tf_op jit(solution)/shard_map/ppermute | solution.py:506
  7.3 3.2 %collective-permute-start.4 = (bf16[64,1280]{1,0:T(8,128)(2,1)S(1)}, bf16[64,1280]{1,0:T(8,128)(2,1)S(1)}, u32[]{:S(2)}, u32[]{:S(2)}) collective-permute-start(bf16[64,1280]{1,0:T(8,128)(2,1)S(1)} %get-tuple-element.20), channel_id=1, source_target_pairs={{0,8},{1,9},{2,10},{3,11},{16,24},{17,25},{18,26},{19,27}} | collective-permute-start | bytes 491528 | tf_op jit(solution)/shard_map/ppermute | solution.py:506
  10.4 1.3 %collective-permute-start.5 = (bf16[64,1280]{1,0:T(8,128)(2,1)S(1)}, bf16[64,1280]{1,0:T(8,128)(2,1)S(1)}, u32[]{:S(2)}, u32[]{:S(2)}) collective-permute-start(bf16[64,1280]{1,0:T(8,128)(2,1)S(1)} %get-tuple-element.21), channel_id=1, source_target_pairs={{0,12},{1,13},{2,14},{3,15},{16,28},{17,29},{18,30},{19,31}} | collective-permute-start | bytes 491528 | tf_op jit(solution)/shard_map/ppermute | solution.py:506
  11.7 0.9 %fusion.2 = (f32[4,64,128]{2,1,0:T(8,128)S(1)}, bf16[4,64,128]{2,1,0:T(8,128)(2,1)S(1)}) fusion(bf16[1,4,64,128]{3,1,2,0:T(4,128)(2,1)} %bitcast.19), kind=kLoop, calls=%fused_computation.18 | loop fusion | flops 32768 | bytes 262144 | tf_op jit(solution)/shard_map/convert_element_type | solution.py:387
  12.6 1.2 %copy-done.1 = bf16[4,128,1024]{2,1,0:T(8,128)(2,1)S(1)} copy-done((bf16[4,128,1024]{2,1,0:T(8,128)(2,1)S(1)}, bf16[4,128,1024]{2,1,0:T(8,128)(2,1)}, u32[]{:S(2)}) %copy-start.1) | copy-done | bytes 1048600
  13.8 1.2 %copy-done.2 = bf16[4,128,1024]{2,1,0:T(8,128)(2,1)S(1)} copy-done((bf16[4,128,1024]{2,1,0:T(8,128)(2,1)S(1)}, bf16[4,128,1024]{2,1,0:T(8,128)(2,1)}, u32[]{:S(2)}) %copy-start.2) | copy-done | bytes 1048600
  15.7 4.4 %shard_map.131 = (f32[72,128]{1,0:T(8,128)S(1)}, f32[72,128]{1,0:T(8,128)S(1)}, f32[72,128]{1,0:T(8,128)S(1)}, f32[72,128]{1,0:T(8,128)S(1)}) custom-call(s32[4]{0:T(128)S(1)} %copy-done.4, bf16[4,64,128]{2,1,0:T(8,128)(2,1)S(1)} %get-tuple-element.27.query_ref, bf16[4,128,1024]{2,1,0:T(8,128)(2,1)S(1)} %copy-done.1, bf16[4,128,1024]{2,1,0:T(8,128)(2,1)S(1)} %copy-done.2), custom_call_target="tpu_custom_call" | custom-call | flops 16777216 | bytes 2097152 | tf_op jit(solution)/shard_map/pallas_call | solution.py:238
  20.1 1.6 %collective-permute-start = (f32[72,128]{1,0:T(8,128)S(1)}, f32[72,128]{1,0:T(8,128)S(1)}, u32[]{:S(2)}, u32[]{:S(2)}) collective-permute-start(f32[72,128]{1,0:T(8,128)S(1)} %get-tuple-element.15), channel_id=1, source_target_pairs={{0,1},{1,0},{2,3},{3,2},{4,5},{5,4},{6,7},{7,6},{8,9},{9,8},{10,11... | collective-permute-start | bytes 110600 | tf_op jit(solution)/shard_map/ppermute | solution.py:481
  21.7 2.6 %collective-permute-start.1 = (f32[72,128]{1,0:T(8,128)S(1)}, f32[72,128]{1,0:T(8,128)S(1)}, u32[]{:S(2)}, u32[]{:S(2)}) collective-permute-start(f32[72,128]{1,0:T(8,128)S(1)} %get-tuple-element.16), channel_id=1, source_target_pairs={{0,2},{1,3},{2,0},{3,1},{4,6},{5,7},{6,4},{7,5},{8,10},{9,11},{10,... | collective-permute-start | bytes 110600 | tf_op jit(solution)/shard_map/ppermute | solution.py:481
  24.3 0.7 %broadcast_compare_fusion = pred[16]{0:T(512)(128)(4,1)S(1)} fusion(s32[16]{0:T(128)} %owner_ref.1, s32[]{:T(128)S(6)} %axis_index.23), kind=kLoop, calls=%fused_computation.16 | loop fusion | flops 16 | bytes 84 | tf_op jit(solution)/shard_map/eq | solution.py:68
  25.0 0.8 %select_reduce_fusion.1 = s32[4]{0:T(128)S(1)} fusion(s32[16]{0:T(128)} %slot_ref.1, pred[16]{0:T(512)(128)(4,1)S(1)} %broadcast_compare_fusion), kind=kLoop, calls=%fused_computation.10 | loop fusion | flops 252 | bytes 96 | tf_op jit(solution)/shard_map/reduce_sum | solution.py:69
  25.8 0.8 %reduce-window.8 = s32[6,1]{0,1:T(1,128)S(1)} reduce-window(s32[6,1]{0,1:T(1,128)} %bitcast.22, s32[]{:T(128)} %constant.5.clone.1), window={size=6x1 pad=5_0x0_0}, to_apply=%region_1.2 | reduce-window | flops 30 | bytes 52 | tf_op jit(solution)/shard_map/reduce-window.3
  26.6 0.7 %bitcast_subtract_fusion = s32[6]{0:T(128)S(1)} fusion(s32[6]{0:T(128)} %param.15, s32[6,1]{0,1:T(1,128)S(1)} %reduce-window.8), kind=kLoop, calls=%fused_computation.17 | loop fusion | flops 6 | bytes 72 | tf_op jit(solution)/shard_map/sub | solution.py:66
  27.7 2.5 %copy-done = bf16[1280,2048]{1,0:T(8,128)(2,1)S(1)} copy-done((bf16[1280,2048]{1,0:T(8,128)(2,1)S(1)}, bf16[1280,2048]{1,0:T(8,128)(2,1)}, u32[]{:S(2)}) %copy-start) | copy-done | bytes 5242904
  30.2 1.1 %shard_map.134 = (f32[16,2048]{1,0:T(8,128)S(1)}, f32[16,2048]{1,0:T(8,128)S(1)}, f32[16,2048]{1,0:T(8,128)S(1)}, f32[16,2048]{1,0:T(8,128)S(1)}) custom-call(bf16[64,1280]{1,0:T(8,128)(2,1)S(1)} %get-tuple-element.18.refs_0_, bf16[64,1280]{1,0:T(8,128)(2,1)S(1)} %collective-permute-done.3.refs_1_, bf16[64,1280]{1,0:T(8,128)(2,1)S(1)} %collective-permute-done.4.refs_2_, ...), custom_call_target="tpu_custom_call" | custom-call | flops 335544320 | bytes 5242880 | tf_op jit(solution)/shard_map/pallas_call | solution.py:238
  32.2 3.6 %collective-permute-start.8 = (f32[16,2048]{1,0:T(8,128)S(1)}, f32[16,2048]{1,0:T(8,128)S(1)}, u32[]{:S(2)}, u32[]{:S(2)}) collective-permute-start(f32[16,2048]{1,0:T(8,128)S(1)} %get-tuple-element.25), channel_id=1, source_target_pairs={{0,3},{1,2},{2,1},{3,0},{4,7},{5,6},{6,5},{7,4},{8,11},{9,10},{10,... | collective-permute-start | bytes 393224 | tf_op jit(solution)/shard_map/ppermute | solution.py:481
  36.3 5.5 %collective-permute-done.2.refs_3_ = f32[72,128]{1,0:T(8,128)S(1)} collective-permute-done((f32[72,128]{1,0:T(8,128)S(1)}, f32[72,128]{1,0:T(8,128)S(1)}, u32[]{:S(2)}, u32[]{:S(2)}) %collective-permute-start.2) | collective-permute-done | bytes 36896 | tf_op jit(solution)/shard_map/ppermute | solution.py:481
  42.8 2.5 %collective-permute-start.10 = (bf16[16,2048]{1,0:T(8,128)(2,1)S(1)}, bf16[16,2048]{1,0:T(8,128)(2,1)S(1)}, u32[]{:S(2)}, u32[]{:S(2)}) collective-permute-start(bf16[16,2048]{1,0:T(8,128)(2,1)S(1)} %shard_map.135.refs_0_), channel_id=1, source_target_pairs={{0,2},{1,3},{2,0},{3,1},{4,6},{5,7},{6,4},{7,5},{8,10},{9,11},{10,... | collective-permute-start | bytes 196616 | tf_op jit(solution)/shard_map/ppermute | solution.py:481
  45.3 3.0 %collective-permute-start.11 = (bf16[16,2048]{1,0:T(8,128)(2,1)S(1)}, bf16[16,2048]{1,0:T(8,128)(2,1)S(1)}, u32[]{:S(2)}, u32[]{:S(2)}) collective-permute-start(bf16[16,2048]{1,0:T(8,128)(2,1)S(1)} %shard_map.135.refs_0_), channel_id=1, source_target_pairs={{0,3},{1,2},{2,1},{3,0},{4,7},{5,6},{6,5},{7,4},{8,11},{9,10},{10,... | collective-permute-start | bytes 196616 | tf_op jit(solution)/shard_map/ppermute | solution.py:481
  48.9 2.4 %collective-permute-done.11.refs_3_ = bf16[16,2048]{1,0:T(8,128)(2,1)S(1)} collective-permute-done((bf16[16,2048]{1,0:T(8,128)(2,1)S(1)}, bf16[16,2048]{1,0:T(8,128)(2,1)S(1)}, u32[]{:S(2)}, u32[]{:S(2)}) %collective-permute-start.11) | collective-permute-done | bytes 65568 | tf_op jit(solution)/shard_map/ppermute | solution.py:481
  51.4 1.2 %collective-permute-done.9.refs_1_ = bf16[16,2048]{1,0:T(8,128)(2,1)S(1)} collective-permute-done((bf16[16,2048]{1,0:T(8,128)(2,1)S(1)}, bf16[16,2048]{1,0:T(8,128)(2,1)S(1)}, u32[]{:S(2)}, u32[]{:S(2)}) %collective-permute-start.9) | collective-permute-done | bytes 65568 | tf_op jit(solution)/shard_map/ppermute | solution.py:481
  52.6 0.7 %shard_map.136 = bf16[64,2048]{1,0:T(8,128)(2,1)} custom-call(bf16[16,2048]{1,0:T(8,128)(2,1)S(1)} %shard_map.135.refs_0_, bf16[16,2048]{1,0:T(8,128)(2,1)S(1)} %collective-permute-done.9.refs_1_, bf16[16,2048]{1,0:T(8,128)(2,1)S(1)} %collective-permute-done.10.refs_2_, bf16[16,2048]{1,0:T(8,128)(2,1)S(1)} %collective-permute-done.11.refs_3_), custom_call_target="tpu_custom_call" | custom-call | tf_op jit(solution)/shard_map/pallas_call | solution.py:238
  (43 shorter events, 5.4 us)
Async XLA Ops:
  0.6 42.0 %copy-start.7 = (f32[128]{0:T(128)S(1)}, f32[128]{0:T(128)}, u32[]{:S(2)}) copy-start(f32[128]{0:T(128)} %param.14) | copy-start | bytes 1540
  0.6 1.1 %copy-start.3 = (bf16[1,256,1280]{2,1,0:T(8,128)(2,1)S(1)}, bf16[1,256,1280]{2,1,0:T(8,128)(2,1)}, u32[]{:S(2)}) copy-start(bf16[1,256,1280]{2,1,0:T(8,128)(2,1)} %param.12) | copy-start | bytes 1966084
  1.7 0.7 %copy-start.5 = (s32[16]{0:T(128)S(1)}, s32[16]{0:T(128)}, u32[]{:S(2)}) copy-start(s32[16]{0:T(128)} %owner_ref.1) | copy-start | bytes 196
  2.4 0.7 %copy-start.6 = (s32[16]{0:T(128)S(1)}, s32[16]{0:T(128)}, u32[]{:S(2)}) copy-start(s32[16]{0:T(128)} %slot_ref.1) | copy-start | bytes 196
  3.0 33.2 %copy-start.8 = (bf16[4,1024]{1,0:T(4,128)(2,1)S(1)}, bf16[4,1024]{1,0:T(4,128)(2,1)}, u32[]{:S(2)}) copy-start(bf16[4,1024]{1,0:T(4,128)(2,1)} %param.21) | copy-start | bytes 24580
  3.0 33.2 %copy-start.9 = (bf16[4,1024]{1,0:T(4,128)(2,1)S(1)}, bf16[4,1024]{1,0:T(4,128)(2,1)}, u32[]{:S(2)}) copy-start(bf16[4,1024]{1,0:T(4,128)(2,1)} %param.22) | copy-start | bytes 24580
  4.9 22.8 %collective-permute-start.3 = (bf16[64,1280]{1,0:T(8,128)(2,1)S(1)}, bf16[64,1280]{1,0:T(8,128)(2,1)S(1)}, u32[]{:S(2)}, u32[]{:S(2)}) collective-permute-start(bf16[64,1280]{1,0:T(8,128)(2,1)S(1)} %get-tuple-element.19), channel_id=1, source_target_pairs={{0,4},{1,5},{2,6},{3,7},{16,20},{17,21},{18,22},{19,23}} | collective-permute-start | bytes 491528 | tf_op jit(solution)/shard_map/ppermute | solution.py:506
  7.3 20.4 %collective-permute-start.4 = (bf16[64,1280]{1,0:T(8,128)(2,1)S(1)}, bf16[64,1280]{1,0:T(8,128)(2,1)S(1)}, u32[]{:S(2)}, u32[]{:S(2)}) collective-permute-start(bf16[64,1280]{1,0:T(8,128)(2,1)S(1)} %get-tuple-element.20), channel_id=1, source_target_pairs={{0,8},{1,9},{2,10},{3,11},{16,24},{17,25},{18,26},{19,27}} | collective-permute-start | bytes 491528 | tf_op jit(solution)/shard_map/ppermute | solution.py:506
  10.4 17.3 %collective-permute-start.5 = (bf16[64,1280]{1,0:T(8,128)(2,1)S(1)}, bf16[64,1280]{1,0:T(8,128)(2,1)S(1)}, u32[]{:S(2)}, u32[]{:S(2)}) collective-permute-start(bf16[64,1280]{1,0:T(8,128)(2,1)S(1)} %get-tuple-element.21), channel_id=1, source_target_pairs={{0,12},{1,13},{2,14},{3,15},{16,28},{17,29},{18,30},{19,31}} | collective-permute-start | bytes 491528 | tf_op jit(solution)/shard_map/ppermute | solution.py:506
  12.6 1.2 %copy-start.1 = (bf16[4,128,1024]{2,1,0:T(8,128)(2,1)S(1)}, bf16[4,128,1024]{2,1,0:T(8,128)(2,1)}, u32[]{:S(2)}) copy-start(bf16[4,128,1024]{2,1,0:T(8,128)(2,1)} %key_ref.1) | copy-start | bytes 3145732
  13.8 1.2 %copy-start.2 = (bf16[4,128,1024]{2,1,0:T(8,128)(2,1)S(1)}, bf16[4,128,1024]{2,1,0:T(8,128)(2,1)}, u32[]{:S(2)}) copy-start(bf16[4,128,1024]{2,1,0:T(8,128)(2,1)} %value_ref.1) | copy-start | bytes 3145732
  15.0 0.7 %copy-start.4 = (s32[4]{0:T(128)S(1)}, s32[4]{0:T(128)}, u32[]{:S(2)}) copy-start(s32[4]{0:T(128)} %length_ref.1) | copy-start | bytes 52
  20.1 15.8 %collective-permute-start = (f32[72,128]{1,0:T(8,128)S(1)}, f32[72,128]{1,0:T(8,128)S(1)}, u32[]{:S(2)}, u32[]{:S(2)}) collective-permute-start(f32[72,128]{1,0:T(8,128)S(1)} %get-tuple-element.15), channel_id=1, source_target_pairs={{0,1},{1,0},{2,3},{3,2},{4,5},{5,4},{6,7},{7,6},{8,9},{9,8},{10,11... | collective-permute-start | bytes 110600 | tf_op jit(solution)/shard_map/ppermute | solution.py:481
  21.7 14.5 %collective-permute-start.1 = (f32[72,128]{1,0:T(8,128)S(1)}, f32[72,128]{1,0:T(8,128)S(1)}, u32[]{:S(2)}, u32[]{:S(2)}) collective-permute-start(f32[72,128]{1,0:T(8,128)S(1)} %get-tuple-element.16), channel_id=1, source_target_pairs={{0,2},{1,3},{2,0},{3,1},{4,6},{5,7},{6,4},{7,5},{8,10},{9,11},{10,... | collective-permute-start | bytes 110600 | tf_op jit(solution)/shard_map/ppermute | solution.py:481
  27.7 2.5 %copy-start = (bf16[1280,2048]{1,0:T(8,128)(2,1)S(1)}, bf16[1280,2048]{1,0:T(8,128)(2,1)}, u32[]{:S(2)}) copy-start(bf16[1280,2048]{1,0:T(8,128)(2,1)} %refs_4_.1) | copy-start | bytes 15728644
  31.3 10.7 %collective-permute-start.6 = (f32[16,2048]{1,0:T(8,128)S(1)}, f32[16,2048]{1,0:T(8,128)S(1)}, u32[]{:S(2)}, u32[]{:S(2)}) collective-permute-start(f32[16,2048]{1,0:T(8,128)S(1)} %get-tuple-element.23), channel_id=1, source_target_pairs={{0,1},{1,0},{2,3},{3,2},{4,5},{5,4},{6,7},{7,6},{8,9},{9,8},{10,11... | collective-permute-start | bytes 393224 | tf_op jit(solution)/shard_map/ppermute | solution.py:481
  31.8 10.8 %collective-permute-start.7 = (f32[16,2048]{1,0:T(8,128)S(1)}, f32[16,2048]{1,0:T(8,128)S(1)}, u32[]{:S(2)}, u32[]{:S(2)}) collective-permute-start(f32[16,2048]{1,0:T(8,128)S(1)} %get-tuple-element.24), channel_id=1, source_target_pairs={{0,2},{1,3},{2,0},{3,1},{4,6},{5,7},{6,4},{7,5},{8,10},{9,11},{10,... | collective-permute-start | bytes 393224 | tf_op jit(solution)/shard_map/ppermute | solution.py:481
  32.2 10.5 %collective-permute-start.8 = (f32[16,2048]{1,0:T(8,128)S(1)}, f32[16,2048]{1,0:T(8,128)S(1)}, u32[]{:S(2)}, u32[]{:S(2)}) collective-permute-start(f32[16,2048]{1,0:T(8,128)S(1)} %get-tuple-element.25), channel_id=1, source_target_pairs={{0,3},{1,2},{2,1},{3,0},{4,7},{5,6},{6,5},{7,4},{8,11},{9,10},{10,... | collective-permute-start | bytes 393224 | tf_op jit(solution)/shard_map/ppermute | solution.py:481
  35.9 5.9 %collective-permute-start.2 = (f32[72,128]{1,0:T(8,128)S(1)}, f32[72,128]{1,0:T(8,128)S(1)}, u32[]{:S(2)}, u32[]{:S(2)}) collective-permute-start(f32[72,128]{1,0:T(8,128)S(1)} %get-tuple-element.17), channel_id=1, source_target_pairs={{0,3},{1,2},{2,1},{3,0},{4,7},{5,6},{6,5},{7,4},{8,11},{9,10},{10,... | collective-permute-start | bytes 110600 | tf_op jit(solution)/shard_map/ppermute | solution.py:481
  42.8 6.1 %collective-permute-start.10 = (bf16[16,2048]{1,0:T(8,128)(2,1)S(1)}, bf16[16,2048]{1,0:T(8,128)(2,1)S(1)}, u32[]{:S(2)}, u32[]{:S(2)}) collective-permute-start(bf16[16,2048]{1,0:T(8,128)(2,1)S(1)} %shard_map.135.refs_0_), channel_id=1, source_target_pairs={{0,2},{1,3},{2,0},{3,1},{4,6},{5,7},{6,4},{7,5},{8,10},{9,11},{10,... | collective-permute-start | bytes 196616 | tf_op jit(solution)/shard_map/ppermute | solution.py:481
  45.3 6.1 %collective-permute-start.11 = (bf16[16,2048]{1,0:T(8,128)(2,1)S(1)}, bf16[16,2048]{1,0:T(8,128)(2,1)S(1)}, u32[]{:S(2)}, u32[]{:S(2)}) collective-permute-start(bf16[16,2048]{1,0:T(8,128)(2,1)S(1)} %shard_map.135.refs_0_), channel_id=1, source_target_pairs={{0,3},{1,2},{2,1},{3,0},{4,7},{5,6},{6,5},{7,4},{8,11},{9,10},{10,... | collective-permute-start | bytes 196616 | tf_op jit(solution)/shard_map/ppermute | solution.py:481
  48.3 4.3 %collective-permute-start.9 = (bf16[16,2048]{1,0:T(8,128)(2,1)S(1)}, bf16[16,2048]{1,0:T(8,128)(2,1)S(1)}, u32[]{:S(2)}, u32[]{:S(2)}) collective-permute-start(bf16[16,2048]{1,0:T(8,128)(2,1)S(1)} %shard_map.135.refs_0_), channel_id=1, source_target_pairs={{0,1},{1,0},{2,3},{3,2},{4,5},{5,4},{6,7},{7,6},{8,9},{9,8},{10,11... | collective-permute-start | bytes 196616 | tf_op jit(solution)/shard_map/ppermute | solution.py:481

commit v3 on v1

--- a/solution.py
+++ b/solution.py
@@ -1,6 +1,10 @@
+import math
+
 import jax
 import jax.numpy as jnp
 from jax import lax
+from jax.experimental import pallas as pl
+from jax.experimental.pallas import tpu as pltpu
 from jax.sharding import PartitionSpec as P
 
 H = 64
@@ -175,7 +179,7 @@
     return (numerator / denominator[..., None]).reshape(row_count, own_width).astype(jnp.bfloat16)
 
 
-def local(
+def local_small_shares(
     prompt,
     key_value_weight,
     key_gain,
@@ -225,6 +229,420 @@
     return (attended, block_pool)
 
 
+VMEM = pl.BlockSpec(memory_space=pltpu.VMEM)
+HBM = pl.BlockSpec(memory_space=pltpu.HBM)
+F32 = jnp.float32
+BF16 = jnp.bfloat16
+I16 = jnp.int16
+TOP = 32000.0
+OCTAVE = 256.0
+LN2 = math.log(2.0)
+TINY = 1e-30
+
+
+def on_chip(kernel, operands, in_specs, out_shapes, scratch=(), out_specs=None, flops=0, moved=0):
+    return pl.pallas_call(
+        kernel,
+        out_shape=out_shapes,
+        in_specs=in_specs,
+        out_specs=out_specs or [VMEM] * len(out_shapes),
+        scratch_shapes=list(scratch),
+        compiler_params=pltpu.CompilerParams(vmem_limit_bytes=40 * 1024 * 1024),
+        cost_estimate=pl.CostEstimate(flops=flops, bytes_accessed=moved, transcendentals=0),
+    )(*operands)
+
+
+def stays(array):
+    return pltpu.with_memory_space_constraint(array, pltpu.HBM)
+
+
+def level_of(peak):
+    return jnp.ceil(jnp.log(jnp.maximum(peak, TINY)) * (OCTAVE / LN2))
+
+
+def as_int16(value):
+    return jnp.round(value).astype(jnp.int32).astype(I16)
+
+
+def as_float(value):
+    return value.astype(jnp.int32).astype(F32)
+
+
+def table_of(block_owner, block_slot, prompt_blocks, decode_lengths):
+    arrays = [block_owner, block_slot, prompt_blocks, decode_lengths]
+    joined_up = jnp.concatenate(arrays)
+    return jnp.pad(joined_up, (0, HD - joined_up.shape[0]))
+
+
+def place_rows(own_states, near_states, table):
+    width = own_states.shape[1]
+
+    def kernel(table_ref, own_hbm, near_ref, keep_ref, send_ref, table, source, held, sems):
+        core = lax.rem(lax.axis_index("section"), 2)
+        large = pltpu.make_async_copy(own_hbm, held, sems.at[1])
+        large.start()
+        small = pltpu.make_async_copy(table_ref, table, sems.at[0])
+        small.start()
+        for j in range(2 * CAP):
+            source[j] = -1
+        small.wait()
+        for b in range(NB):
+            owner_b = table[b]
+
+            @pl.when(lax.rem(owner_b, 2) == core)
+            def _():
+                source[(owner_b // 2) * CAP + table[NB + b]] = b
+
+        large.wait()
+
+        def place(states):
+            for j in range(2 * CAP):
+                b = source[j]
+                start = pl.multiple_of(jnp.maximum(b, 0) * BLK, BLK)
+                target = (keep_ref, send_ref)[j // CAP]
+                target[pl.ds((j % CAP) * BLK, BLK), :] = states[pl.ds(start, BLK), :]
+
+                @pl.when(b < 0)
+                def _():
+                    target[pl.ds((j % CAP) * BLK, BLK), :] = jnp.zeros((BLK, width), BF16)
+
+        @pl.when(core == 0)
+        def _():
+            place(held)
+
+        @pl.when(core == 1)
+        def _():
+            place(near_ref)
+
+    return on_chip(
+        kernel,
+        (table, stays(own_states), near_states),
+        [VMEM, HBM, VMEM],
+        [jax.ShapeDtypeStruct((CAP * BLK, width), BF16)] * 2,
+        [
+            pltpu.SMEM((HD,), jnp.int32),
+            pltpu.SMEM((2 * CAP,), jnp.int32),
+            pltpu.VMEM(own_states.shape, BF16),
+            pltpu.SemaphoreType.DMA((2,)),
+        ],
+        moved=own_states.size * 2,
+    )
+
+
+def attend_span(queries, cache_keys, cache_values, weight, table, prompt_count):
+    row_count, local_len = cache_keys.shape[0], cache_keys.shape[1]
+    tensor_count = lax.axis_size("tensor")
+    rows_here = CAP * BLK // tensor_count
+    slots_here = rows_here // BLK
+    width = row_count * HD
+
+    def kernel(
+        table_ref, key_hbm, value_hbm, weight_hbm, query_ref,
+        float_ref, code_ref, cosine_ref, sine_ref, weight_ref,
+        table, keys, values, scores, weights, sems,
+    ):
+        pairs = [(table_ref, table), (key_hbm, keys), (value_hbm, values), (weight_hbm, weight_ref)]
+        copies = [pltpu.make_async_copy(s, d, sems.at[i]) for i, (s, d) in enumerate(pairs)]
+        for copy in copies:
+            copy.start()
+        group = lax.axis_index("section")
+        rank = lax.axis_index("tensor")
+        copies[0].wait()
+
+        lane = lax.broadcasted_iota(jnp.int32, (BLK, HD), 1)
+        row = lax.broadcasted_iota(jnp.int32, (BLK, HD), 0)
+        half = lax.rem(lane, HD // 2).astype(F32)
+        frequency = jnp.exp(half * (-2.0 / HD * math.log(ROPE_BASE)))
+        for s in range(slots_here):
+            block = 0
+            for b in range(NB):
+                block = jnp.where((table[b] == group) & (table[NB + b] == rank * slots_here + s), b, block)
+            first, begin = 0, 0
+            for j in range(prompt_count):
+                first = jnp.where(block >= begin, begin, first)
+                begin = begin + table[2 * NB + j]
+            angles = ((block - first) * BLK + row).astype(F32) * frequency
+            cosine_ref[pl.ds(s * BLK, BLK), :] = jnp.cos(angles)
+            sine = jnp.sin(angles)
+            sine_ref[pl.ds(s * BLK, BLK), :] = jnp.where(lane < HD // 2, -sine, sine)
+
+        copies[1].wait()
+        for r in range(row_count):
+            for pair in range(KVH // 2):
+                pair_queries = query_ref[r, pl.ds(pair * 2 * G, 2 * G), :]
+                for n in (2 * pair, 2 * pair + 1):
+                    both = lax.dot_general(
+                        pair_queries,
+                        keys[r, :, n * HD : (n + 1) * HD],
+                        (((1,), (1,)), ((), ())),
+                        preferred_element_type=F32,
+                    )
+                    scores[r, pl.ds(n * G, G), :] = both[(n % 2) * G : (n % 2 + 1) * G]
+        place = lax.broadcasted_iota(jnp.int32, (H, local_len), 1) + rank * local_len
+        column = lax.broadcasted_iota(jnp.int32, (H, HD), 1)
+        stats = jnp.zeros((H, HD), F32)
+        for r in range(row_count):
+            live = place < table[2 * NB + prompt_count + r]
+            row_scores = jnp.where(live, scores[r] * HD ** (-0.5), MASKED_SCORE)
+            peak = jnp.max(row_scores, axis=1, keepdims=True)
+            weight = jnp.where(live, jnp.exp(row_scores - peak), 0.0)
+            total = jnp.sum(weight, axis=1, keepdims=True)
+            weights[r] = weight.astype(BF16)
+            stats = jnp.where(column == r, peak, stats)
+            stats = jnp.where(column == row_count + r, total, stats)
+        float_ref[:, pl.ds(width, HD)] = stats
+        copies[2].wait()
+        levels = jnp.zeros((H, HD), F32)
+        for r in range(row_count):
+            for pair in range(KVH // 2):
+                pair_weights = weights[r, pl.ds(pair * 2 * G, 2 * G), :]
+                for n in (2 * pair, 2 * pair + 1):
+                    both = jnp.dot(
+                        pair_weights, values[r, :, n * HD : (n + 1) * HD], preferred_element_type=F32
+                    )
+                    float_ref[pl.ds(n * G, G), pl.ds(r * HD, HD)] = both[(n % 2) * G : (n % 2 + 1) * G]
+        for r in range(row_count):
+            peak = jnp.max(jnp.abs(float_ref[:, pl.ds(r * HD, HD)]), axis=1, keepdims=True)
+            levels = jnp.where(column == r, peak, levels)
+        levels = level_of(levels)
+        scale = TOP * jnp.exp(levels * (-LN2 / OCTAVE))
+        for r in range(row_count):
+            out = float_ref[:, pl.ds(r * HD, HD)]
+            code_ref[:, pl.ds(r * HD, HD)] = as_int16(out * scale[:, r : r + 1])
+        peaks = jnp.maximum(stats, -TOP)
+        fine = jnp.where(column < row_count, peaks, stats * HD)
+        whole = jnp.floor(fine)
+        part = (fine - whole) * TOP
+        packed = jnp.where(column < 2 * row_count, whole, 0.0)
+        shifted = pltpu.roll(jnp.where(column < 2 * row_count, part, 0.0), 2 * row_count, 1)
+        moved = pltpu.roll(jnp.where(column < row_count, levels, 0.0), 4 * row_count, 1)
+        code_ref[:, pl.ds(width, HD)] = as_int16(packed + shifted + moved)
+        copies[3].wait()
+
+    return on_chip(
+        kernel,
+        (table, stays(cache_keys), stays(cache_values), stays(weight), queries.reshape(row_count, H, HD)),
+        [VMEM, HBM, HBM, HBM, VMEM],
+        [
+            jax.ShapeDtypeStruct((H, width + HD), F32),
+            jax.ShapeDtypeStruct((H, width + HD), I16),
+            jax.ShapeDtypeStruct((rows_here, HD), F32),
+            jax.ShapeDtypeStruct((rows_here, HD), F32),
+            jax.ShapeDtypeStruct(weight.shape, BF16),
+        ],
+        [
+            pltpu.SMEM((HD,), jnp.int32),
+            pltpu.VMEM(cache_keys.shape, BF16),
+            pltpu.VMEM(cache_values.shape, BF16),
+            pltpu.VMEM((row_count, H, local_len), F32),
+            pltpu.VMEM((row_count, H, local_len), BF16),
+            pltpu.SemaphoreType.DMA((4,)),
+        ],
+        flops=4 * row_count * H * HD * local_len,
+        moved=4 * cache_keys.size + 2 * weight.size,
+    )
+
+
+def project_rows(kept, landed, weight, span_code, tensor_count):
+    slot_rows, depth = kept.shape
+    width = weight.shape[1]
+    rows_here = slot_rows // tensor_count
+    span_width = span_code.shape[1]
+    heads_here = H // tensor_count
+    share_width = width + span_width + HD
+    step_width = 512
+
+    def kernel(kept_ref, landed_ref, weight_ref, span_ref, own_ref, *refs):
+        share_refs, rows_ref, held = refs[: tensor_count - 1], refs[-2], refs[-1]
+        far = lax.axis_index("section") >= 2
+        rank = lax.axis_index("tensor")
+        rows_ref[...] = jnp.where(far, landed_ref[...], kept_ref[...])
+        for c in range(width // step_width):
+            columns = pl.ds(c * step_width, step_width)
+            held[:, columns] = jnp.dot(rows_ref[...], weight_ref[:, columns], preferred_element_type=F32)
+        own_ref[...] = held[pl.ds(pl.multiple_of(rank * rows_here, rows_here), rows_here), :]
+        lane = lax.broadcasted_iota(jnp.int32, (rows_here, HD), 1)
+        for step in range(1, tensor_count):
+            share_ref = share_refs[step - 1]
+            rows = pl.ds(pl.multiple_of((rank ^ step) * rows_here, rows_here), rows_here)
+            heads = pl.ds(pl.multiple_of((rank ^ step) * heads_here, heads_here), heads_here)
+            levels = jnp.zeros((rows_here, HD), F32)
+            for n in range(width // HD):
+                peak = jnp.max(jnp.abs(held[rows, pl.ds(n * HD, HD)]), axis=1, keepdims=True)
+                levels = jnp.where(lane == n, peak, levels)
+            levels = level_of(levels)
+            scale = TOP * jnp.exp(levels * (-LN2 / OCTAVE))
+            for n in range(width // HD):
+                columns = pl.ds(n * HD, HD)
+                share_ref[:, columns] = as_int16(held[rows, columns] * scale[:, n : n + 1])
+            share_ref[:, pl.ds(width, span_width)] = span_ref[heads, :]
+            share_ref[:, pl.ds(width + span_width, HD)] = as_int16(levels)
+
+    return on_chip(
+        kernel,
+        (kept, landed, weight, span_code),
+        [VMEM] * 4,
+        [jax.ShapeDtypeStruct((rows_here, width), F32)]
+        + [jax.ShapeDtypeStruct((rows_here, share_width), I16)] * (tensor_count - 1),
+        [pltpu.VMEM((slot_rows, depth), BF16), pltpu.VMEM((slot_rows, width), F32)],
+        flops=2 * slot_rows * depth * width,
+        moved=2 * weight.size,
+    )
+
+
+def finish_rows(own, shares, cosine, sine, gain):
+    rows, width = own.shape
+    share_count = len(shares)
+    share_width = shares[0].shape[1]
+
+    def kernel(own_ref, *refs):
+        share_refs = refs[:share_count]
+        cosine_ref, sine_ref, gain_ref, out_ref = refs[share_count:]
+        scales = [
+            jnp.exp(as_float(ref[:, pl.ds(share_width - HD, HD)]) * (LN2 / OCTAVE)) * (1.0 / TOP)
+            for ref in share_refs
+        ]
+        for n in range(width // HD):
+            columns = pl.ds(n * HD, HD)
+            total = own_ref[:, columns]
+            for ref, scale in zip(share_refs, scales):
+                total = total + as_float(ref[:, columns]) * scale[:, n : n + 1]
+            if n < KVH:
+                mean = jnp.sum(total * total, axis=1, keepdims=True) * (1.0 / HD)
+                total = total * lax.rsqrt(mean + NORM_EPSILON) * gain_ref[...]
+                total = total * cosine_ref[...] + pltpu.roll(total, HD // 2, 1) * sine_ref[...]
+            out_ref[:, columns] = total.astype(BF16)
+
+    return on_chip(
+        kernel,
+        (own, *shares, cosine, sine, gain),
+        [VMEM] * (share_count + 4),
+        [jax.ShapeDtypeStruct((rows, width), BF16)],
+    )[0]
+
+
+def merge_spans(span_float, shares, queries, new_keys, new_values, width):
+    row_count = queries.shape[0]
+    share_count = len(shares)
+    heads_here = shares[0].shape[0]
+    keys_here = heads_here // G
+    span_width = row_count * HD
+
+    def kernel(own_ref, *refs):
+        share_refs = refs[:share_count]
+        query_ref, key_ref, value_ref, out_ref = refs[share_count:]
+        rank = lax.axis_index("tensor")
+        heads = pl.ds(pl.multiple_of(rank * heads_here, heads_here), heads_here)
+        columns = pl.ds(pl.multiple_of(rank * keys_here * HD, HD), keys_here * HD)
+        new_key, new_value = key_ref[:, columns].astype(F32), value_ref[:, columns].astype(F32)
+
+        def spread(tile, r):
+            return jnp.concatenate(
+                [
+                    jnp.broadcast_to(tile[r : r + 1, kk * HD : (kk + 1) * HD], (G, HD))
+                    for kk in range(keys_here)
+                ],
+                axis=0,
+            )
+
+        stats = [own_ref[heads, pl.ds(span_width, HD)]]
+        scales = [None]
+        for ref in share_refs:
+            code = as_float(ref[:, pl.ds(width + span_width, HD)])
+            fine = code + pltpu.roll(code, HD - 2 * row_count, 1) * (1.0 / TOP)
+            column = lax.broadcasted_iota(jnp.int32, code.shape, 1)
+            stats.append(jnp.where(column < row_count, fine, fine * (1.0 / HD)))
+            scales.append(jnp.exp(code * (LN2 / OCTAVE)) * (1.0 / TOP))
+        for r in range(row_count):
+            query = query_ref[r, heads, :].astype(F32)
+            self_score = jnp.sum(query * spread(new_key, r), axis=1, keepdims=True) * HD ** (-0.5)
+            row_peak = self_score
+            for tile in stats:
+                row_peak = jnp.maximum(row_peak, tile[:, r : r + 1])
+            self_weight = jnp.exp(self_score - row_peak)
+            numerator = self_weight * spread(new_value, r)
+            denominator = self_weight
+            for k, tile in enumerate(stats):
+                factor = jnp.exp(tile[:, r : r + 1] - row_peak)
+                if k == 0:
+                    out = own_ref[heads, pl.ds(r * HD, HD)]
+                else:
+                    out = as_float(share_refs[k - 1][:, pl.ds(width + r * HD, HD)])
+                    out = out * scales[k][:, 4 * row_count + r : 4 * row_count + r + 1]
+                numerator += factor * out
+                denominator += factor * tile[:, row_count + r : row_count + r + 1]
+            out_ref[r] = (numerator / denominator).astype(BF16)
+
+    attended = on_chip(
+        kernel,
+        (span_float, *shares, queries.reshape(row_count, H, HD), new_keys, new_values),
+        [VMEM] * (share_count + 4),
+        [jax.ShapeDtypeStruct((row_count, heads_here, HD), BF16)],
+    )[0]
+    return attended.reshape(row_count, heads_here * HD)
+
+
+def join_rows(pieces):
+    count = len(pieces)
+    rows, width = pieces[0].shape
+
+    def kernel(*refs):
+        piece_refs, out_hbm, sems = refs[:count], refs[count], refs[count + 1]
+        rank = lax.axis_index("tensor")
+        copies = []
+        for step in range(count):
+            place = pl.ds(pl.multiple_of((rank ^ step) * rows, rows), rows)
+            copies.append(pltpu.make_async_copy(piece_refs[step], out_hbm.at[place], sems.at[step]))
+        for copy in copies:
+            copy.start()
+        for copy in copies:
+            copy.wait()
+
+    return on_chip(
+        kernel,
+        pieces,
+        [VMEM] * count,
+        [jax.ShapeDtypeStruct((count * rows, width), BF16)],
+        [pltpu.SemaphoreType.DMA((count,))],
+        out_specs=[HBM],
+    )[0]
+
+
+def swap(piece, axis, step):
+    return lax.ppermute(piece, axis, [(i, i ^ step) for i in range(lax.axis_size(axis))])
+
+
+def local(
+    prompt,
+    key_value_weight,
+    key_gain,
+    prompt_blocks,
+    block_owner,
+    block_slot,
+    queries,
+    cache_keys,
+    cache_values,
+    new_keys,
+    new_values,
+    decode_lengths,
+):
+    tensor_count = lax.axis_size("tensor")
+    near_states = swap(prompt[0], "section", 1)
+    table = table_of(block_owner, block_slot, prompt_blocks, decode_lengths)
+    kept, sent = place_rows(prompt[0], near_states, table)
+    landed = swap(sent, "section", 2)
+    span_float, span_code, cosine, sine, weight = attend_span(
+        queries, cache_keys, cache_values, key_value_weight, table, prompt_blocks.shape[0]
+    )
+    own, *shares = project_rows(kept, landed, weight, span_code, tensor_count)
+    shares = [swap(share, "tensor", k + 1) for k, share in enumerate(shares)]
+    finished = finish_rows(own, shares, cosine, sine, key_gain[None, :])
+    pieces = [finished] + [swap(finished, "tensor", k) for k in range(1, tensor_count)]
+    block_pool = join_rows(pieces)
+    attended = merge_spans(span_float, shares, queries, new_keys, new_values, key_value_weight.shape[1])
+    return (attended, block_pool.reshape(1, CAP, BLK, -1))
+
+
 def solution(mesh):
     in_specs = (
         P(("parts", "section"), None, "tensor"),
@@ -241,4 +659,7 @@
         P(("parts", "section")),
     )
     out_specs = (P(("parts", "section"), "tensor"), P(("parts", "section"), None, None, None))
-    return jax.shard_map(local, mesh=mesh, in_specs=in_specs, out_specs=out_specs, check_vma=False)
+    tensor_count = mesh.shape["tensor"]
+    whole_tiles = tensor_count == 4 and mesh.shape["section"] == 4
+    program = local if whole_tiles else local_small_shares
+    return jax.shard_map(program, mesh=mesh, in_specs=in_specs, out_specs=out_specs, check_vma=False)

time: 85 us -> 34.6 us (0.41)
  waiting for transfers between devices: 40.8 us -> 11.2 us
  starting transfers between devices: 21.5 us -> 12.4 us
  other arithmetic: 9.11 us -> 0.78 us
  Pallas kernels: 0 us -> 7.8 us
  matrix products: 7.22 us -> 0 us
  local copies, waits for them, and re-layouts: 4.8 us -> 1.49 us
    ppermute x12 -> x8, waiting for transfers between devices: 40.8 us -> 11.2 us  [swap(): lax.ppermute(piece, axis, [(i, i ^ step) for i in range(lax.axis_size(axi...]
    ppermute x12 -> x8, starting transfers between devices: 21.5 us -> 12.4 us  [swap(): lax.ppermute(piece, axis, [(i, i ^ step) for i in range(lax.axis_size(axi...]
    pallas_call x0 -> x6, Pallas kernels: none -> 7.8 us  [on_chip(): pl.pallas_call(kernel, out_shape=out_shapes, in_specs=in_specs, out_specs...]
    dot_general x5 -> x0, matrix products: 7.22 us -> none  [the longest x1 3.53 us: local(): jnp.dot(own_rows, key_value_weight, preferred_element_type=jnp.float32)]
    mul x6 -> x0, other arithmetic: 2.19 us -> none  [the longest x2 1.36 us: combine_partials(): former_out * former_factor[..., None]]
    another operation x6 -> x0, local copies, waits for them, and re-layouts: 1.82 us -> none
    convert_element_type x2 -> x0, other arithmetic: 1.43 us -> none  [the longest x1 1.36 us: finish_heads(): (numerator / denominator[..., None]).reshape(row_count, own_width)]
    add x5 -> x0, other arithmetic: 1.15 us -> none  [the longest x1 1.04 us: spread(): landed = landed + lax.ppermute(rows[k], axis, [(0, k)])]
  transfers between devices with their start and end apart: 12 -> 8, of which waited for: 7 -> 6; matrix products, arithmetic and copies ran while one was open for 12% -> 7% of each run, Pallas kernels for 0% -> 10%
where the time goes in v3:
time: 34.6 us; the launch traced here: 34.3 us
  starting transfers between devices  12.4 us (36%)
  waiting for transfers between devices  11.2 us (32%)
  Pallas kernels  7.8 us (23%)
  local copies, waits for them, and re-layouts  1.49 us (4%)
  other arithmetic  0.78 us (2%)
  between operations  0.7 us (2%)
    ppermute x8, starting transfers between devices, swap(): lax.ppermute(piece, axis, [(i, i ^ step) for i in range(lax.axis_size(axi...  12.4 us
    ppermute x8, waiting for transfers between devices, swap(): lax.ppermute(piece, axis, [(i, i ^ step) for i in range(lax.axis_size(axi...  11.2 us
    pallas_call x6, Pallas kernels, on_chip(): pl.pallas_call(kernel, out_shape=out_shapes, in_specs=in_specs, out_specs...  7.8 us
    unnamed x8, local copies, waits for them, and re-layouts  1.49 us
    concatenate x1, other arithmetic, table_of(): joined_up = jnp.concatenate(arrays)  0.78 us
  transfers between devices with their start and end apart: 8, of which 6 were waited for; matrix products, arithmetic and copies ran while one was open for 7% of the time, Pallas kernels for 10%

profile of v3, /device:TPU:0, one launch (start us, length us, event | category | flops | bytes accessed | tf_op | source)
XLA Modules:
  0.0 34.3 jit_solution(3119789551085422709)
XLA Ops:
  0.6 0.5 %collective-permute-start = (bf16[256,1280]{1,0:T(8,128)(2,1)}, bf16[256,1280]{1,0:T(8,128)(2,1)S(1)}, u32[]{:S(2)}, u32[]{:S(2)}) collective-permute-start(bf16[256,1280]{1,0:T(8,128)(2,1)} %bitcast.15), channel_id=1, source_target_pairs={{0,4},{4,0},{8,12},{12,8},{1,5},{5,1},{9,13},{13,9},{2,6},{6,2},{1... | collective-permute-start | bytes 1966088 | tf_op jit(solution)/shard_map/ppermute | solution.py:612
  1.1 0.8 %pad_add_fusion = s32[42]{0:T(128)S(1)} fusion(s32[4]{0:T(128)} %param.23, s32[6]{0:T(128)} %param.15, s32[16]{0:T(128)} %param.17, s32[16]{0:T(128)} %param.16), kind=kLoop, calls=%fused_computation.2 | loop fusion | flops 126 | bytes 336 | tf_op jit(solution)/shard_map/concatenate | solution.py:273
  1.9 1.1 %collective-permute-done.near_ref = bf16[256,1280]{1,0:T(8,128)(2,1)S(1)} collective-permute-done((bf16[256,1280]{1,0:T(8,128)(2,1)}, bf16[256,1280]{1,0:T(8,128)(2,1)S(1)}, u32[]{:S(2)}, u32[]{:S(2)}) %collective-permute-start) | collective-permute-done | bytes 655392 | tf_op jit(solution)/shard_map/ppermute | solution.py:612
  3.1 1.2 %shard_map.132 = (bf16[64,1280]{1,0:T(8,128)(2,1)S(1)}, bf16[64,1280]{1,0:T(8,128)(2,1)S(1)}) custom-call(s32[128]{0:T(128)S(1)} %pad.4.table_ref, bf16[256,1280]{1,0:T(8,128)(2,1)} %bitcast.16, bf16[256,1280]{1,0:T(8,128)(2,1)S(1)} %collective-permute-done.near_ref), custom_call_target="tpu_custom_call" | custom-call | bytes 655360 | tf_op jit(solution)/shard_map/pallas_call | solution.py:244
  4.3 2.9 %collective-permute-start.1 = (bf16[64,1280]{1,0:T(8,128)(2,1)S(1)}, bf16[64,1280]{1,0:T(8,128)(2,1)S(1)}, u32[]{:S(2)}, u32[]{:S(2)}) collective-permute-start(bf16[64,1280]{1,0:T(8,128)(2,1)S(1)} %get-tuple-element.15), channel_id=1, source_target_pairs={{0,8},{4,12},{8,0},{12,4},{1,9},{5,13},{9,1},{13,5},{2,10},{6,14},... | collective-permute-start | bytes 491528 | tf_op jit(solution)/shard_map/ppermute | solution.py:612
  7.2 0.8 %copy.18 = bf16[1,4,64,128]{3,2,1,0:T(8,128)(2,1)S(1)} copy(bf16[1,4,64,128]{3,1,2,0:T(4,128)(2,1)} %bitcast.18) | data formatting | bytes 131072
  8.0 0.0 copy-start
  8.1 0.0 copy-start.1
  8.1 3.2 %shard_map.131 = (f32[64,640]{1,0:T(8,128)S(1)}, s16[64,640]{1,0:T(8,128)(2,1)S(1)}, f32[16,128]{1,0:T(8,128)S(1)}, f32[16,128]{1,0:T(8,128)S(1)}, bf16[1280,2048]{1,0:T(8,128)(2,1)S(1)}) custom-call(s32[128]{0:T(128)S(1)} %pad.4.table_ref, bf16[4,128,1024]{2,1,0:T(8,128)(2,1)} %key_hbm.1, bf16[4,128,1024]{2,1,0:T(8,128)(2,1)} %value_hbm.1, ...), custom_call_target="tpu_custom_call" | custom-call | flops 16777216 | bytes 7340032 | tf_op jit(solution)/shard_map/pallas_call | solution.py:244
  11.3 0.4 %collective-permute-done.1.landed_ref = bf16[64,1280]{1,0:T(8,128)(2,1)S(1)} collective-permute-done((bf16[64,1280]{1,0:T(8,128)(2,1)S(1)}, bf16[64,1280]{1,0:T(8,128)(2,1)S(1)}, u32[]{:S(2)}, u32[]{:S(2)}) %collective-permute-start.1) | collective-permute-done | bytes 163872 | tf_op jit(solution)/shard_map/ppermute | solution.py:612
  11.7 1.4 %shard_map.133 = (f32[16,2048]{1,0:T(8,128)S(1)}, s16[16,2816]{1,0:T(8,128)(2,1)S(1)}, s16[16,2816]{1,0:T(8,128)(2,1)S(1)}, s16[16,2816]{1,0:T(8,128)(2,1)S(1)}) custom-call(bf16[64,1280]{1,0:T(8,128)(2,1)S(1)} %get-tuple-element.14.kept_ref, bf16[64,1280]{1,0:T(8,128)(2,1)S(1)} %collective-permute-done.1.landed_ref, ...), custom_call_target="tpu_custom_call" | custom-call | flops 335544320 | bytes 5242880 | tf_op jit(solution)/shard_map/pallas_call | solution.py:244
  13.1 1.9 %collective-permute-start.2 = (s16[16,2816]{1,0:T(8,128)(2,1)S(1)}, s16[16,2816]{1,0:T(8,128)(2,1)S(1)}, u32[]{:S(2)}, u32[]{:S(2)}) collective-permute-start(s16[16,2816]{1,0:T(8,128)(2,1)S(1)} %get-tuple-element.18), channel_id=1, source_target_pairs={{0,1},{1,0},{2,3},{3,2},{4,5},{5,4},{6,7},{7,6},{8,9},{9,8},{10,11... | collective-permute-start | bytes 270344 | tf_op jit(solution)/shard_map/ppermute | solution.py:612
  15.0 2.6 %collective-permute-start.3 = (s16[16,2816]{1,0:T(8,128)(2,1)S(1)}, s16[16,2816]{1,0:T(8,128)(2,1)S(1)}, u32[]{:S(2)}, u32[]{:S(2)}) collective-permute-start(s16[16,2816]{1,0:T(8,128)(2,1)S(1)} %get-tuple-element.19), channel_id=1, source_target_pairs={{0,2},{1,3},{2,0},{3,1},{4,6},{5,7},{6,4},{7,5},{8,10},{9,11},{10,... | collective-permute-start | bytes 270344 | tf_op jit(solution)/shard_map/ppermute | solution.py:612
  17.6 1.0 %collective-permute-done.2.refs_0_ = s16[16,2816]{1,0:T(8,128)(2,1)S(1)} collective-permute-done((s16[16,2816]{1,0:T(8,128)(2,1)S(1)}, s16[16,2816]{1,0:T(8,128)(2,1)S(1)}, u32[]{:S(2)}, u32[]{:S(2)}) %collective-permute-start.2) | collective-permute-done | bytes 90144 | tf_op jit(solution)/shard_map/ppermute | solution.py:612
  18.6 5.7 %collective-permute-done.3.refs_1_ = s16[16,2816]{1,0:T(8,128)(2,1)S(1)} collective-permute-done((s16[16,2816]{1,0:T(8,128)(2,1)S(1)}, s16[16,2816]{1,0:T(8,128)(2,1)S(1)}, u32[]{:S(2)}, u32[]{:S(2)}) %collective-permute-start.3) | collective-permute-done | bytes 90144 | tf_op jit(solution)/shard_map/ppermute | solution.py:612
  24.3 0.9 %shard_map.135.refs_0_ = bf16[16,2048]{1,0:T(8,128)(2,1)S(1)} custom-call(f32[16,2048]{1,0:T(8,128)S(1)} %get-tuple-element.21.own_ref, s16[16,2816]{1,0:T(8,128)(2,1)S(1)} %collective-permute-done.2.refs_0_, s16[16,2816]{1,0:T(8,128)(2,1)S(1)} %collective-permute-done.3.refs_1_, s16[16,2816]{1,0:T(8,128)(2,1)S(1)} %collective-permute-done.4.refs_2_, ...), custom_call_target="tpu_custom_call" | custom-call | tf_op jit(solution)/shard_map/pallas_call | solution.py:244
  25.2 2.5 %collective-permute-start.7 = (bf16[16,2048]{1,0:T(8,128)(2,1)S(1)}, bf16[16,2048]{1,0:T(8,128)(2,1)S(1)}, u32[]{:S(2)}, u32[]{:S(2)}) collective-permute-start(bf16[16,2048]{1,0:T(8,128)(2,1)S(1)} %shard_map.135.refs_0_), channel_id=1, source_target_pairs={{0,3},{1,2},{2,1},{3,0},{4,7},{5,6},{6,5},{7,4},{8,11},{9,10},{10,... | collective-permute-start | bytes 196616 | tf_op jit(solution)/shard_map/ppermute | solution.py:612
  27.7 0.5 %collective-permute-start.6 = (bf16[16,2048]{1,0:T(8,128)(2,1)S(1)}, bf16[16,2048]{1,0:T(8,128)(2,1)S(1)}, u32[]{:S(2)}, u32[]{:S(2)}) collective-permute-start(bf16[16,2048]{1,0:T(8,128)(2,1)S(1)} %shard_map.135.refs_0_), channel_id=1, source_target_pairs={{0,2},{1,3},{2,0},{3,1},{4,6},{5,7},{6,4},{7,5},{8,10},{9,11},{10,... | collective-permute-start | bytes 196616 | tf_op jit(solution)/shard_map/ppermute | solution.py:612
  28.2 1.4 %collective-permute-start.5 = (bf16[16,2048]{1,0:T(8,128)(2,1)S(1)}, bf16[16,2048]{1,0:T(8,128)(2,1)S(1)}, u32[]{:S(2)}, u32[]{:S(2)}) collective-permute-start(bf16[16,2048]{1,0:T(8,128)(2,1)S(1)} %shard_map.135.refs_0_), channel_id=1, source_target_pairs={{0,1},{1,0},{2,3},{3,2},{4,5},{5,4},{6,7},{7,6},{8,9},{9,8},{10,11... | collective-permute-start | bytes 196616 | tf_op jit(solution)/shard_map/ppermute | solution.py:612
  29.7 0.4 %shard_map.134 = bf16[4,16,128]{2,1,0:T(8,128)(2,1)S(1)} custom-call(f32[64,640]{1,0:T(8,128)S(1)} %get-tuple-element.13.own_ref, s16[16,2816]{1,0:T(8,128)(2,1)S(1)} %collective-permute-done.2.refs_0_, s16[16,2816]{1,0:T(8,128)(2,1)S(1)} %collective-permute-done.3.refs_1_, s16[16,2816]{1,0:T(8,128)(2,1)S(1)} %collective-permute-done.4.refs_2_, ...), custom_call_target="tpu_custom_call" | custom-call | tf_op jit(solution)/shard_map/pallas_call | solution.py:244
  30.0 0.6 %copy.19 = bf16[1,4,16,128]{3,1,2,0:T(4,128)(2,1)} copy(bf16[1,4,16,128]{3,2,1,0:T(8,128)(2,1)S(1)} %bitcast.13) | data formatting | bytes 32768
  30.7 0.9 %collective-permute-done.7.refs_3_ = bf16[16,2048]{1,0:T(8,128)(2,1)S(1)} collective-permute-done((bf16[16,2048]{1,0:T(8,128)(2,1)S(1)}, bf16[16,2048]{1,0:T(8,128)(2,1)S(1)}, u32[]{:S(2)}, u32[]{:S(2)}) %collective-permute-start.7) | collective-permute-done | bytes 65568 | tf_op jit(solution)/shard_map/ppermute | solution.py:612
  31.6 2.0 %collective-permute-done.6.refs_2_ = bf16[16,2048]{1,0:T(8,128)(2,1)S(1)} collective-permute-done((bf16[16,2048]{1,0:T(8,128)(2,1)S(1)}, bf16[16,2048]{1,0:T(8,128)(2,1)S(1)}, u32[]{:S(2)}, u32[]{:S(2)}) %collective-permute-start.6) | collective-permute-done | bytes 65568 | tf_op jit(solution)/shard_map/ppermute | solution.py:612
  33.6 0.7 %shard_map.136 = bf16[64,2048]{1,0:T(8,128)(2,1)} custom-call(bf16[16,2048]{1,0:T(8,128)(2,1)S(1)} %shard_map.135.refs_0_, bf16[16,2048]{1,0:T(8,128)(2,1)S(1)} %collective-permute-done.5.refs_1_, bf16[16,2048]{1,0:T(8,128)(2,1)S(1)} %collective-permute-done.6.refs_2_, bf16[16,2048]{1,0:T(8,128)(2,1)S(1)} %collective-permute-done.7.refs_3_), custom_call_target="tpu_custom_call" | custom-call | tf_op jit(solution)/shard_map/pallas_call | solution.py:244
  (8 shorter events, 0.0 us)
Async XLA Ops:
  0.6 2.5 %collective-permute-start = (bf16[256,1280]{1,0:T(8,128)(2,1)}, bf16[256,1280]{1,0:T(8,128)(2,1)S(1)}, u32[]{:S(2)}, u32[]{:S(2)}) collective-permute-start(bf16[256,1280]{1,0:T(8,128)(2,1)} %bitcast.15), channel_id=1, source_target_pairs={{0,4},{4,0},{8,12},{12,8},{1,5},{5,1},{9,13},{13,9},{2,6},{6,2},{1... | collective-permute-start | bytes 1966088 | tf_op jit(solution)/shard_map/ppermute | solution.py:612
  4.3 7.4 %collective-permute-start.1 = (bf16[64,1280]{1,0:T(8,128)(2,1)S(1)}, bf16[64,1280]{1,0:T(8,128)(2,1)S(1)}, u32[]{:S(2)}, u32[]{:S(2)}) collective-permute-start(bf16[64,1280]{1,0:T(8,128)(2,1)S(1)} %get-tuple-element.15), channel_id=1, source_target_pairs={{0,8},{4,12},{8,0},{12,4},{1,9},{5,13},{9,1},{13,5},{2,10},{6,14},... | collective-permute-start | bytes 491528 | tf_op jit(solution)/shard_map/ppermute | solution.py:612
  8.0 16.2 %copy-start.2 = (f32[128]{0:T(128)S(1)}, f32[128]{0:T(128)}, u32[]{:S(2)}) copy-start(f32[128]{0:T(128)} %param.14) | copy-start | bytes 1540
  8.0 21.6 %copy-start = (bf16[4,1024]{1,0:T(4,128)(2,1)S(1)}, bf16[4,1024]{1,0:T(4,128)(2,1)}, u32[]{:S(2)}) copy-start(bf16[4,1024]{1,0:T(4,128)(2,1)} %refs_4_.1) | copy-start | bytes 24580
  8.1 21.6 %copy-start.1 = (bf16[4,1024]{1,0:T(4,128)(2,1)S(1)}, bf16[4,1024]{1,0:T(4,128)(2,1)}, u32[]{:S(2)}) copy-start(bf16[4,1024]{1,0:T(4,128)(2,1)} %refs_5_.1) | copy-start | bytes 24580
  13.1 5.5 %collective-permute-start.2 = (s16[16,2816]{1,0:T(8,128)(2,1)S(1)}, s16[16,2816]{1,0:T(8,128)(2,1)S(1)}, u32[]{:S(2)}, u32[]{:S(2)}) collective-permute-start(s16[16,2816]{1,0:T(8,128)(2,1)S(1)} %get-tuple-element.18), channel_id=1, source_target_pairs={{0,1},{1,0},{2,3},{3,2},{4,5},{5,4},{6,7},{7,6},{8,9},{9,8},{10,11... | collective-permute-start | bytes 270344 | tf_op jit(solution)/shard_map/ppermute | solution.py:612
  15.0 9.3 %collective-permute-start.3 = (s16[16,2816]{1,0:T(8,128)(2,1)S(1)}, s16[16,2816]{1,0:T(8,128)(2,1)S(1)}, u32[]{:S(2)}, u32[]{:S(2)}) collective-permute-start(s16[16,2816]{1,0:T(8,128)(2,1)S(1)} %get-tuple-element.19), channel_id=1, source_target_pairs={{0,2},{1,3},{2,0},{3,1},{4,6},{5,7},{6,4},{7,5},{8,10},{9,11},{10,... | collective-permute-start | bytes 270344 | tf_op jit(solution)/shard_map/ppermute | solution.py:612
  17.6 6.7 %collective-permute-start.4 = (s16[16,2816]{1,0:T(8,128)(2,1)S(1)}, s16[16,2816]{1,0:T(8,128)(2,1)S(1)}, u32[]{:S(2)}, u32[]{:S(2)}) collective-permute-start(s16[16,2816]{1,0:T(8,128)(2,1)S(1)} %get-tuple-element.20), channel_id=1, source_target_pairs={{0,3},{1,2},{2,1},{3,0},{4,7},{5,6},{6,5},{7,4},{8,11},{9,10},{10,... | collective-permute-start | bytes 270344 | tf_op jit(solution)/shard_map/ppermute | solution.py:612
  25.2 6.4 %collective-permute-start.7 = (bf16[16,2048]{1,0:T(8,128)(2,1)S(1)}, bf16[16,2048]{1,0:T(8,128)(2,1)S(1)}, u32[]{:S(2)}, u32[]{:S(2)}) collective-permute-start(bf16[16,2048]{1,0:T(8,128)(2,1)S(1)} %shard_map.135.refs_0_), channel_id=1, source_target_pairs={{0,3},{1,2},{2,1},{3,0},{4,7},{5,6},{6,5},{7,4},{8,11},{9,10},{10,... | collective-permute-start | bytes 196616 | tf_op jit(solution)/shard_map/ppermute | solution.py:612
  27.7 5.9 %collective-permute-start.6 = (bf16[16,2048]{1,0:T(8,128)(2,1)S(1)}, bf16[16,2048]{1,0:T(8,128)(2,1)S(1)}, u32[]{:S(2)}, u32[]{:S(2)}) collective-permute-start(bf16[16,2048]{1,0:T(8,128)(2,1)S(1)} %shard_map.135.refs_0_), channel_id=1, source_target_pairs={{0,2},{1,3},{2,0},{3,1},{4,6},{5,7},{6,4},{7,5},{8,10},{9,11},{10,... | collective-permute-start | bytes 196616 | tf_op jit(solution)/shard_map/ppermute | solution.py:612
  28.2 5.4 %collective-permute-start.5 = (bf16[16,2048]{1,0:T(8,128)(2,1)S(1)}, bf16[16,2048]{1,0:T(8,128)(2,1)S(1)}, u32[]{:S(2)}, u32[]{:S(2)}) collective-permute-start(bf16[16,2048]{1,0:T(8,128)(2,1)S(1)} %shard_map.135.refs_0_), channel_id=1, source_target_pairs={{0,1},{1,0},{2,3},{3,2},{4,5},{5,4},{6,7},{7,6},{8,9},{9,8},{10,11... | collective-permute-start | bytes 196616 | tf_op jit(solution)/shard_map/ppermute | solution.py:612

commit v4 on v3

--- a/solution.py
+++ b/solution.py
@@ -238,6 +238,7 @@
 OCTAVE = 256.0
 LN2 = math.log(2.0)
 TINY = 1e-30
+LEVELS = 64
 
 
 def on_chip(kernel, operands, in_specs, out_shapes, scratch=(), out_specs=None, flops=0, moved=0):
@@ -268,108 +269,148 @@
     return value.astype(jnp.int32).astype(F32)
 
 
-def table_of(block_owner, block_slot, prompt_blocks, decode_lengths):
-    arrays = [block_owner, block_slot, prompt_blocks, decode_lengths]
-    joined_up = jnp.concatenate(arrays)
-    return jnp.pad(joined_up, (0, HD - joined_up.shape[0]))
-
-
-def place_rows(own_states, near_states, table):
-    width = own_states.shape[1]
-
-    def kernel(table_ref, own_hbm, near_ref, keep_ref, send_ref, table, source, held, sems):
-        core = lax.rem(lax.axis_index("section"), 2)
-        large = pltpu.make_async_copy(own_hbm, held, sems.at[1])
-        large.start()
-        small = pltpu.make_async_copy(table_ref, table, sems.at[0])
-        small.start()
-        for j in range(2 * CAP):
-            source[j] = -1
-        small.wait()
-        for b in range(NB):
-            owner_b = table[b]
-
-            @pl.when(lax.rem(owner_b, 2) == core)
-            def _():
-                source[(owner_b // 2) * CAP + table[NB + b]] = b
-
-        large.wait()
-
-        def place(states):
-            for j in range(2 * CAP):
-                b = source[j]
-                start = pl.multiple_of(jnp.maximum(b, 0) * BLK, BLK)
-                target = (keep_ref, send_ref)[j // CAP]
-                target[pl.ds((j % CAP) * BLK, BLK), :] = states[pl.ds(start, BLK), :]
-
-                @pl.when(b < 0)
-                def _():
-                    target[pl.ds((j % CAP) * BLK, BLK), :] = jnp.zeros((BLK, width), BF16)
-
-        @pl.when(core == 0)
-        def _():
-            place(held)
-
-        @pl.when(core == 1)
-        def _():
-            place(near_ref)
-
-    return on_chip(
-        kernel,
-        (table, stays(own_states), near_states),
-        [VMEM, HBM, VMEM],
-        [jax.ShapeDtypeStruct((CAP * BLK, width), BF16)] * 2,
-        [
-            pltpu.SMEM((HD,), jnp.int32),
-            pltpu.SMEM((2 * CAP,), jnp.int32),
-            pltpu.VMEM(own_states.shape, BF16),
-            pltpu.SemaphoreType.DMA((2,)),
-        ],
-        moved=own_states.size * 2,
-    )
-
-
-def attend_span(queries, cache_keys, cache_values, weight, table, prompt_count):
-    row_count, local_len = cache_keys.shape[0], cache_keys.shape[1]
-    tensor_count = lax.axis_size("tensor")
-    rows_here = CAP * BLK // tensor_count
+def prepare(states, key_gain, block_owner, block_slot, prompt_blocks):
+    rows_here = CAP * BLK // lax.axis_size("tensor")
     slots_here = rows_here // BLK
-    width = row_count * HD
-
-    def kernel(
-        table_ref, key_hbm, value_hbm, weight_hbm, query_ref,
-        float_ref, code_ref, cosine_ref, sine_ref, weight_ref,
-        table, keys, values, scores, weights, sems,
-    ):
-        pairs = [(table_ref, table), (key_hbm, keys), (value_hbm, values), (weight_hbm, weight_ref)]
-        copies = [pltpu.make_async_copy(s, d, sems.at[i]) for i, (s, d) in enumerate(pairs)]
+    prompt_count = prompt_blocks.shape[0]
+    fetched = [block_owner, block_slot, prompt_blocks, key_gain[None, :]]
+    count = len(fetched)
+
+    def kernel(*refs):
+        sources, states_hbm = refs[:count], refs[count]
+        cosine_ref, sine_ref, states_ref, table_ref = refs[count + 1 : count + 5]
+        held, (source, sems) = refs[count + 5 : 2 * count + 5], refs[2 * count + 5 :]
+        owner, slot, prompts, gain = held
+        copies = [pltpu.make_async_copy(s, d, sems.at[i]) for i, (s, d) in enumerate(zip(sources, held))]
+        copies.append(pltpu.make_async_copy(states_hbm, states_ref, sems.at[count]))
         for copy in copies:
             copy.start()
         group = lax.axis_index("section")
         rank = lax.axis_index("tensor")
-        copies[0].wait()
+        core = lax.rem(group, 2)
+        for copy in copies[:count]:
+            copy.wait()
+
+        for j in range(2 * CAP):
+            source[j] = -1
+        for b in range(NB):
+
+            @pl.when(owner[b] == core)
+            def _():
+                source[slot[b]] = b
+
+            @pl.when(owner[b] == 3 - core)
+            def _():
+                source[CAP + slot[b]] = b
+
+        column = lax.broadcasted_iota(jnp.int32, (8, HD), 1)
+        table = jnp.zeros((8, HD), jnp.int32)
+        for j in range(2 * CAP):
+            table = jnp.where(column == j, source[j], table)
+        table_ref[...] = table
 
         lane = lax.broadcasted_iota(jnp.int32, (BLK, HD), 1)
         row = lax.broadcasted_iota(jnp.int32, (BLK, HD), 0)
         half = lax.rem(lane, HD // 2).astype(F32)
         frequency = jnp.exp(half * (-2.0 / HD * math.log(ROPE_BASE)))
+        far_gain = pltpu.roll(jnp.broadcast_to(gain[...], (8, HD)), HD // 2, 1)[0:1]
         for s in range(slots_here):
             block = 0
             for b in range(NB):
-                block = jnp.where((table[b] == group) & (table[NB + b] == rank * slots_here + s), b, block)
+                block = jnp.where((owner[b] == group) & (slot[b] == rank * slots_here + s), b, block)
             first, begin = 0, 0
             for j in range(prompt_count):
                 first = jnp.where(block >= begin, begin, first)
-                begin = begin + table[2 * NB + j]
+                begin = begin + prompts[j]
             angles = ((block - first) * BLK + row).astype(F32) * frequency
-            cosine_ref[pl.ds(s * BLK, BLK), :] = jnp.cos(angles)
-            sine = jnp.sin(angles)
+            cosine_ref[pl.ds(s * BLK, BLK), :] = jnp.cos(angles) * gain[...]
+            sine = jnp.sin(angles) * far_gain
             sine_ref[pl.ds(s * BLK, BLK), :] = jnp.where(lane < HD // 2, -sine, sine)
-
+        copies[count].wait()
+
+    return on_chip(
+        kernel,
+        [stays(array) for array in (*fetched, states)],
+        [HBM] * (count + 1),
+        [
+            jax.ShapeDtypeStruct((rows_here, HD), F32),
+            jax.ShapeDtypeStruct((rows_here, HD), F32),
+            jax.ShapeDtypeStruct(states.shape, BF16),
+            jax.ShapeDtypeStruct((8, HD), jnp.int32),
+        ],
+        [pltpu.SMEM(array.shape, jnp.int32) for array in fetched[:3]]
+        + [
+            pltpu.VMEM((1, HD), F32),
+            pltpu.SMEM((2 * CAP,), jnp.int32),
+            pltpu.SemaphoreType.DMA((count + 1,)),
+        ],
+        moved=2 * states.size,
+    )
+
+
+def place_rows(own_states, near_states, table):
+    width = own_states.shape[1]
+
+    def kernel(own_ref, near_ref, table_ref, keep_ref, send_ref, source, sem):
+        core = lax.rem(lax.axis_index("section"), 2)
+        copy = pltpu.make_async_copy(table_ref, source, sem)
+        copy.start()
+        copy.wait()
+
+        def place(states):
+            for j in range(2 * CAP):
+                b = source[0, j]
+                start = pl.multiple_of(jnp.maximum(b, 0) * BLK, BLK)
+                target = (keep_ref, send_ref)[j // CAP]
+                target[pl.ds((j % CAP) * BLK, BLK), :] = states[pl.ds(start, BLK), :]
+
+                @pl.when(b < 0)
+                def _():
+                    target[pl.ds((j % CAP) * BLK, BLK), :] = jnp.zeros((BLK, width), BF16)
+
+        @pl.when(core == 0)
+        def _():
+            place(own_ref)
+
+        @pl.when(core == 1)
+        def _():
+            place(near_ref)
+
+    return on_chip(
+        kernel,
+        (own_states, near_states, table),
+        [VMEM] * 3,
+        [jax.ShapeDtypeStruct((CAP * BLK, width), BF16)] * 2,
+        [pltpu.SMEM((8, HD), jnp.int32), pltpu.SemaphoreType.DMA(())],
+        moved=own_states.size * 2,
+    )
+
+
+def attend_span(queries, cache_keys, cache_values, decode_lengths, weight, after):
+    row_count, local_len = cache_keys.shape[0], cache_keys.shape[1]
+    width = row_count * HD
+    fetched = [decode_lengths, queries, cache_keys, cache_values]
+    count = len(fetched)
+
+    def kernel(*refs):
+        sources, weight_hbm = refs[:count], refs[count]
+        span_ref, code_ref, query_ref, weight_ref = refs[count + 2 : count + 6]
+        held, (scores, weights, sems) = refs[count + 6 : 2 * count + 6], refs[2 * count + 6 :]
+        length, packed, keys, values = held
+        copies = [pltpu.make_async_copy(s, d, sems.at[i]) for i, (s, d) in enumerate(zip(sources, held))]
+        copies.append(pltpu.make_async_copy(weight_hbm, weight_ref, sems.at[count]))
+        for copy in copies:
+            copy.start()
+        rank = lax.axis_index("tensor")
+        copies[0].wait()
         copies[1].wait()
+        for h in range(H):
+            piece = packed[:, pl.ds(h * HD, HD)].astype(F32)
+            query_ref[pl.ds(h, row_count, stride=H), :] = piece
+        copies[2].wait()
         for r in range(row_count):
             for pair in range(KVH // 2):
-                pair_queries = query_ref[r, pl.ds(pair * 2 * G, 2 * G), :]
+                pair_queries = query_ref[pl.ds(r * H + pair * 2 * G, 2 * G), :].astype(BF16)
                 for n in (2 * pair, 2 * pair + 1):
                     both = lax.dot_general(
                         pair_queries,
@@ -382,7 +423,7 @@
         column = lax.broadcasted_iota(jnp.int32, (H, HD), 1)
         stats = jnp.zeros((H, HD), F32)
         for r in range(row_count):
-            live = place < table[2 * NB + prompt_count + r]
+            live = place < length[r]
             row_scores = jnp.where(live, scores[r] * HD ** (-0.5), MASKED_SCORE)
             peak = jnp.max(row_scores, axis=1, keepdims=True)
             weight = jnp.where(live, jnp.exp(row_scores - peak), 0.0)
@@ -390,8 +431,8 @@
             weights[r] = weight.astype(BF16)
             stats = jnp.where(column == r, peak, stats)
             stats = jnp.where(column == row_count + r, total, stats)
-        float_ref[:, pl.ds(width, HD)] = stats
-        copies[2].wait()
+        span_ref[:, pl.ds(width, HD)] = stats
+        copies[3].wait()
         levels = jnp.zeros((H, HD), F32)
         for r in range(row_count):
             for pair in range(KVH // 2):
@@ -400,104 +441,106 @@
                     both = jnp.dot(
                         pair_weights, values[r, :, n * HD : (n + 1) * HD], preferred_element_type=F32
                     )
-                    float_ref[pl.ds(n * G, G), pl.ds(r * HD, HD)] = both[(n % 2) * G : (n % 2 + 1) * G]
+                    span_ref[pl.ds(n * G, G), pl.ds(r * HD, HD)] = both[(n % 2) * G : (n % 2 + 1) * G]
         for r in range(row_count):
-            peak = jnp.max(jnp.abs(float_ref[:, pl.ds(r * HD, HD)]), axis=1, keepdims=True)
+            peak = jnp.max(jnp.abs(span_ref[:, pl.ds(r * HD, HD)]), axis=1, keepdims=True)
             levels = jnp.where(column == r, peak, levels)
         levels = level_of(levels)
         scale = TOP * jnp.exp(levels * (-LN2 / OCTAVE))
         for r in range(row_count):
-            out = float_ref[:, pl.ds(r * HD, HD)]
+            out = span_ref[:, pl.ds(r * HD, HD)]
             code_ref[:, pl.ds(r * HD, HD)] = as_int16(out * scale[:, r : r + 1])
         peaks = jnp.maximum(stats, -TOP)
         fine = jnp.where(column < row_count, peaks, stats * HD)
         whole = jnp.floor(fine)
         part = (fine - whole) * TOP
-        packed = jnp.where(column < 2 * row_count, whole, 0.0)
+        coded = jnp.where(column < 2 * row_count, whole, 0.0)
         shifted = pltpu.roll(jnp.where(column < 2 * row_count, part, 0.0), 2 * row_count, 1)
         moved = pltpu.roll(jnp.where(column < row_count, levels, 0.0), 4 * row_count, 1)
-        code_ref[:, pl.ds(width, HD)] = as_int16(packed + shifted + moved)
-        copies[3].wait()
+        code_ref[:, pl.ds(width, HD)] = as_int16(coded + shifted + moved)
+        copies[count].wait()
 
     return on_chip(
         kernel,
-        (table, stays(cache_keys), stays(cache_values), stays(weight), queries.reshape(row_count, H, HD)),
-        [VMEM, HBM, HBM, HBM, VMEM],
+        [stays(array) for array in (*fetched, weight)] + [after],
+        [HBM] * (count + 1) + [pl.BlockSpec(memory_space=pl.ANY)],
         [
             jax.ShapeDtypeStruct((H, width + HD), F32),
             jax.ShapeDtypeStruct((H, width + HD), I16),
-            jax.ShapeDtypeStruct((rows_here, HD), F32),
-            jax.ShapeDtypeStruct((rows_here, HD), F32),
+            jax.ShapeDtypeStruct((row_count * H, HD), F32),
             jax.ShapeDtypeStruct(weight.shape, BF16),
         ],
-        [
-            pltpu.SMEM((HD,), jnp.int32),
-            pltpu.VMEM(cache_keys.shape, BF16),
-            pltpu.VMEM(cache_values.shape, BF16),
+        [pltpu.SMEM((row_count,), jnp.int32)]
+        + [pltpu.VMEM(array.shape, array.dtype) for array in fetched[1:]]
+        + [
             pltpu.VMEM((row_count, H, local_len), F32),
             pltpu.VMEM((row_count, H, local_len), BF16),
-            pltpu.SemaphoreType.DMA((4,)),
+            pltpu.SemaphoreType.DMA((count + 1,)),
         ],
         flops=4 * row_count * H * HD * local_len,
         moved=4 * cache_keys.size + 2 * weight.size,
     )
 
 
-def project_rows(kept, landed, weight, span_code, tensor_count):
+def project_rows(kept, landed, weight, span_code, steps):
     slot_rows, depth = kept.shape
     width = weight.shape[1]
-    rows_here = slot_rows // tensor_count
-    span_width = span_code.shape[1]
-    heads_here = H // tensor_count
+    rows_here = slot_rows // len(steps)
+    heads_here = H // len(steps)
+    span_width = span_code.shape[1] - HD
     share_width = width + span_width + HD
-    step_width = 512
+    step_width = 256
 
     def kernel(kept_ref, landed_ref, weight_ref, span_ref, own_ref, *refs):
-        share_refs, rows_ref, held = refs[: tensor_count - 1], refs[-2], refs[-1]
+        share_refs, (held, code) = refs[:-2], refs[-2:]
         far = lax.axis_index("section") >= 2
         rank = lax.axis_index("tensor")
-        rows_ref[...] = jnp.where(far, landed_ref[...], kept_ref[...])
-        for c in range(width // step_width):
-            columns = pl.ds(c * step_width, step_width)
-            held[:, columns] = jnp.dot(rows_ref[...], weight_ref[:, columns], preferred_element_type=F32)
-        own_ref[...] = held[pl.ds(pl.multiple_of(rank * rows_here, rows_here), rows_here), :]
-        lane = lax.broadcasted_iota(jnp.int32, (rows_here, HD), 1)
-        for step in range(1, tensor_count):
-            share_ref = share_refs[step - 1]
-            rows = pl.ds(pl.multiple_of((rank ^ step) * rows_here, rows_here), rows_here)
+        rows = jnp.where(far, landed_ref[...], kept_ref[...])
+        lane = lax.broadcasted_iota(jnp.int32, (slot_rows, HD), 1)
+        levels = jnp.zeros((slot_rows, HD), F32)
+        for c in range(0, width, step_width):
+            product = jnp.dot(rows, weight_ref[:, c : c + step_width], preferred_element_type=F32)
+            held[:, c : c + step_width] = product
+            for m in range(0, step_width, HD):
+                tile = product[:, m : m + HD]
+                level = level_of(jnp.max(jnp.abs(tile), axis=1, keepdims=True))
+                levels = jnp.where(lane == LEVELS + (c + m) // HD, level, levels)
+                scaled = tile * (TOP * jnp.exp(level * (-LN2 / OCTAVE)))
+                code[:, c + m : c + m + HD] = as_int16(scaled)
+        code[:, width:] = as_int16(levels)
+
+        def rows_of(step):
+            return pl.ds(pl.multiple_of((rank ^ step) * rows_here, rows_here), rows_here)
+
+        own_ref[...] = held[rows_of(0), :]
+        for k, step in enumerate(steps[1:]):
             heads = pl.ds(pl.multiple_of((rank ^ step) * heads_here, heads_here), heads_here)
-            levels = jnp.zeros((rows_here, HD), F32)
-            for n in range(width // HD):
-                peak = jnp.max(jnp.abs(held[rows, pl.ds(n * HD, HD)]), axis=1, keepdims=True)
-                levels = jnp.where(lane == n, peak, levels)
-            levels = level_of(levels)
-            scale = TOP * jnp.exp(levels * (-LN2 / OCTAVE))
-            for n in range(width // HD):
-                columns = pl.ds(n * HD, HD)
-                share_ref[:, columns] = as_int16(held[rows, columns] * scale[:, n : n + 1])
-            share_ref[:, pl.ds(width, span_width)] = span_ref[heads, :]
-            share_ref[:, pl.ds(width + span_width, HD)] = as_int16(levels)
+            share_refs[k][:, pl.ds(0, width)] = code[rows_of(step), pl.ds(0, width)]
+            share_refs[k][:, pl.ds(width, span_width)] = span_ref[heads, pl.ds(0, span_width)]
+            stats = as_float(span_ref[heads, pl.ds(span_width, HD)])
+            both = jnp.where(lane[:rows_here] < LEVELS, stats, as_float(code[rows_of(step), pl.ds(width, HD)]))
+            share_refs[k][:, pl.ds(width + span_width, HD)] = as_int16(both)
 
     return on_chip(
         kernel,
         (kept, landed, weight, span_code),
         [VMEM] * 4,
         [jax.ShapeDtypeStruct((rows_here, width), F32)]
-        + [jax.ShapeDtypeStruct((rows_here, share_width), I16)] * (tensor_count - 1),
-        [pltpu.VMEM((slot_rows, depth), BF16), pltpu.VMEM((slot_rows, width), F32)],
+        + [jax.ShapeDtypeStruct((rows_here, share_width), I16)] * (len(steps) - 1),
+        [pltpu.VMEM((slot_rows, width), F32), pltpu.VMEM((slot_rows, width + HD), I16)],
         flops=2 * slot_rows * depth * width,
         moved=2 * weight.size,
     )
 
 
-def finish_rows(own, shares, cosine, sine, gain):
+def finish_rows(own, shares, cosine, sine):
     rows, width = own.shape
     share_count = len(shares)
     share_width = shares[0].shape[1]
 
     def kernel(own_ref, *refs):
         share_refs = refs[:share_count]
-        cosine_ref, sine_ref, gain_ref, out_ref = refs[share_count:]
+        cosine_ref, sine_ref, out_ref = refs[share_count:]
         scales = [
             jnp.exp(as_float(ref[:, pl.ds(share_width - HD, HD)]) * (LN2 / OCTAVE)) * (1.0 / TOP)
             for ref in share_refs
@@ -506,29 +549,29 @@
             columns = pl.ds(n * HD, HD)
             total = own_ref[:, columns]
             for ref, scale in zip(share_refs, scales):
-                total = total + as_float(ref[:, columns]) * scale[:, n : n + 1]
+                total = total + as_float(ref[:, columns]) * scale[:, LEVELS + n : LEVELS + n + 1]
             if n < KVH:
                 mean = jnp.sum(total * total, axis=1, keepdims=True) * (1.0 / HD)
-                total = total * lax.rsqrt(mean + NORM_EPSILON) * gain_ref[...]
                 total = total * cosine_ref[...] + pltpu.roll(total, HD // 2, 1) * sine_ref[...]
+                total = total * lax.rsqrt(mean + NORM_EPSILON)
             out_ref[:, columns] = total.astype(BF16)
 
     return on_chip(
         kernel,
-        (own, *shares, cosine, sine, gain),
-        [VMEM] * (share_count + 4),
+        (own, *shares, cosine, sine),
+        [VMEM] * (share_count + 3),
         [jax.ShapeDtypeStruct((rows, width), BF16)],
     )[0]
 
 
-def merge_spans(span_float, shares, queries, new_keys, new_values, width):
-    row_count = queries.shape[0]
+def merge_spans(span, shares, queries, new_keys, new_values, begin):
+    row_count = new_keys.shape[0]
     share_count = len(shares)
     heads_here = shares[0].shape[0]
     keys_here = heads_here // G
-    span_width = row_count * HD
-
-    def kernel(own_ref, *refs):
+    width = row_count * HD
+
+    def kernel(span_ref, *refs):
         share_refs = refs[:share_count]
         query_ref, key_ref, value_ref, out_ref = refs[share_count:]
         rank = lax.axis_index("tensor")
@@ -545,16 +588,22 @@
                 axis=0,
             )
 
-        stats = [own_ref[heads, pl.ds(span_width, HD)]]
-        scales = [None]
+        stats, scales = [span_ref[heads, pl.ds(width, HD)]], []
         for ref in share_refs:
-            code = as_float(ref[:, pl.ds(width + span_width, HD)])
+            code = as_float(ref[:, pl.ds(begin + width, HD)])
+            column = lax.broadcasted_iota(jnp.int32, code.shape, 1)
             fine = code + pltpu.roll(code, HD - 2 * row_count, 1) * (1.0 / TOP)
-            column = lax.broadcasted_iota(jnp.int32, code.shape, 1)
             stats.append(jnp.where(column < row_count, fine, fine * (1.0 / HD)))
             scales.append(jnp.exp(code * (LN2 / OCTAVE)) * (1.0 / TOP))
+
+        def part(k, r):
+            if k == 0:
+                return span_ref[heads, pl.ds(r * HD, HD)]
+            coded = as_float(share_refs[k - 1][:, pl.ds(begin + r * HD, HD)])
+            return coded * scales[k - 1][:, 4 * row_count + r : 4 * row_count + r + 1]
+
         for r in range(row_count):
-            query = query_ref[r, heads, :].astype(F32)
+            query = query_ref[pl.ds(pl.multiple_of(r * H + rank * heads_here, heads_here), heads_here), :]
             self_score = jnp.sum(query * spread(new_key, r), axis=1, keepdims=True) * HD ** (-0.5)
             row_peak = self_score
             for tile in stats:
@@ -564,25 +613,20 @@
             denominator = self_weight
             for k, tile in enumerate(stats):
                 factor = jnp.exp(tile[:, r : r + 1] - row_peak)
-                if k == 0:
-                    out = own_ref[heads, pl.ds(r * HD, HD)]
-                else:
-                    out = as_float(share_refs[k - 1][:, pl.ds(width + r * HD, HD)])
-                    out = out * scales[k][:, 4 * row_count + r : 4 * row_count + r + 1]
-                numerator += factor * out
+                numerator += factor * part(k, r)
                 denominator += factor * tile[:, row_count + r : row_count + r + 1]
             out_ref[r] = (numerator / denominator).astype(BF16)
 
     attended = on_chip(
         kernel,
-        (span_float, *shares, queries.reshape(row_count, H, HD), new_keys, new_values),
+        (span, *shares, queries, new_keys, new_values),
         [VMEM] * (share_count + 4),
         [jax.ShapeDtypeStruct((row_count, heads_here, HD), BF16)],
     )[0]
     return attended.reshape(row_count, heads_here * HD)
 
 
-def join_rows(pieces):
+def join_rows(pieces, steps):
     count = len(pieces)
     rows, width = pieces[0].shape
 
@@ -591,7 +635,7 @@
         rank = lax.axis_index("tensor")
         copies = []
         for step in range(count):
-            place = pl.ds(pl.multiple_of((rank ^ step) * rows, rows), rows)
+            place = pl.ds(pl.multiple_of(lax.rem(rank + count - steps[step], count) * rows, rows), rows)
             copies.append(pltpu.make_async_copy(piece_refs[step], out_hbm.at[place], sems.at[step]))
         for copy in copies:
             copy.start()
@@ -610,6 +654,11 @@
 
 def swap(piece, axis, step):
     return lax.ppermute(piece, axis, [(i, i ^ step) for i in range(lax.axis_size(axis))])
+
+
+def turn(piece, axis, step):
+    count = lax.axis_size(axis)
+    return lax.ppermute(piece, axis, [(i, (i + step) % count) for i in range(count)])
 
 
 def local(
@@ -628,18 +677,19 @@
 ):
     tensor_count = lax.axis_size("tensor")
     near_states = swap(prompt[0], "section", 1)
-    table = table_of(block_owner, block_slot, prompt_blocks, decode_lengths)
-    kept, sent = place_rows(prompt[0], near_states, table)
-    landed = swap(sent, "section", 2)
-    span_float, span_code, cosine, sine, weight = attend_span(
-        queries, cache_keys, cache_values, key_value_weight, table, prompt_blocks.shape[0]
-    )
-    own, *shares = project_rows(kept, landed, weight, span_code, tensor_count)
-    shares = [swap(share, "tensor", k + 1) for k, share in enumerate(shares)]
-    finished = finish_rows(own, shares, cosine, sine, key_gain[None, :])
-    pieces = [finished] + [swap(finished, "tensor", k) for k in range(1, tensor_count)]
-    block_pool = join_rows(pieces)
-    attended = merge_spans(span_float, shares, queries, new_keys, new_values, key_value_weight.shape[1])
+    cosine, sine, states, table = prepare(prompt[0], key_gain, block_owner, block_slot, prompt_blocks)
+    kept, sent = place_rows(states, near_states, table)
+    landed = swap(sent, "section", 3)
+    span, span_code, row_queries, weight = attend_span(
+        queries, cache_keys, cache_values, decode_lengths, key_value_weight, kept
+    )
+    steps = (0,) + tuple(range(tensor_count - 1, 0, -1))
+    own, *shares = project_rows(kept, landed, weight, span_code, steps)
+    shares = [swap(share, "tensor", step) for share, step in zip(shares, steps[1:])]
+    finished = finish_rows(own, shares, cosine, sine)
+    pieces = [finished] + [turn(finished, "tensor", step) for step in steps[1:]]
+    block_pool = join_rows(pieces, steps)
+    attended = merge_spans(span, shares, row_queries, new_keys, new_values, key_value_weight.shape[1])
     return (attended, block_pool.reshape(1, CAP, BLK, -1))
 
 

time: 34.6 us -> 33.6 us (0.971)
  local copies, waits for them, and re-layouts: 1.49 us -> 0.63 us
  waiting for transfers between devices: 11.2 us -> 12 us
  other arithmetic: 0.78 us -> 0 us
  starting transfers between devices: 12.4 us -> 12 us
    ppermute x8 -> x5, starting transfers between devices: 12.4 us -> 8.17 us  [swap(): lax.ppermute(piece, axis, [(i, i ^ step) for i in range(lax.axis_size(axi...]
    ppermute x0 -> x3, starting transfers between devices: none -> 3.88 us  [turn(): lax.ppermute(piece, axis, [(i, (i + step) % count) for i in range(count)])]
    ppermute x0 -> x3, waiting for transfers between devices: none -> 3.28 us  [turn(): lax.ppermute(piece, axis, [(i, (i + step) % count) for i in range(count)])]
    ppermute x8 -> x5, waiting for transfers between devices: 11.2 us -> 8.69 us  [swap(): lax.ppermute(piece, axis, [(i, i ^ step) for i in range(lax.axis_size(axi...]
    unnamed x8 -> x5, local copies, waits for them, and re-layouts: 1.49 us -> 0.63 us
    concatenate x1 -> x0, other arithmetic: 0.78 us -> none  [table_of(): joined_up = jnp.concatenate(arrays)]
    pallas_call x6 -> x7, Pallas kernels: 7.8 us -> 8.12 us  [on_chip(): pl.pallas_call(kernel, out_shape=out_shapes, in_specs=in_specs, out_specs...]
  transfers between devices with their start and end apart: 8 -> 8, of which waited for: 6 -> 6; matrix products, arithmetic and copies ran while one was open for 7% -> 2% of each run, Pallas kernels for 10% -> 14%
where the time goes in v4:
time: 33.6 us; the launch traced here: 33.4 us
  starting transfers between devices  12 us (36%)
  waiting for transfers between devices  12 us (36%)
  Pallas kernels  8.12 us (24%)
  between operations  0.68 us (2%)
  local copies, waits for them, and re-layouts  0.63 us (2%)
    ppermute x5, waiting for transfers between devices, swap(): lax.ppermute(piece, axis, [(i, i ^ step) for i in range(lax.axis_size(axi...  8.69 us
    ppermute x5, starting transfers between devices, swap(): lax.ppermute(piece, axis, [(i, i ^ step) for i in range(lax.axis_size(axi...  8.17 us
    pallas_call x7, Pallas kernels, on_chip(): pl.pallas_call(kernel, out_shape=out_shapes, in_specs=in_specs, out_specs...  8.12 us
    ppermute x3, starting transfers between devices, turn(): lax.ppermute(piece, axis, [(i, (i + step) % count) for i in range(count)])  3.88 us
    ppermute x3, waiting for transfers between devices, turn(): lax.ppermute(piece, axis, [(i, (i + step) % count) for i in range(count)])  3.28 us
  transfers between devices with their start and end apart: 8, of which 6 were waited for; matrix products, arithmetic and copies ran while one was open for 2% of the time, Pallas kernels for 14%

profile of v4, /device:TPU:0, one launch (start us, length us, event | category | flops | bytes accessed | tf_op | source)
XLA Modules:
  0.0 33.4 jit_solution(15212463913479851199)
XLA Ops:
  0.6 0.5 %collective-permute-start = (bf16[256,1280]{1,0:T(8,128)(2,1)}, bf16[256,1280]{1,0:T(8,128)(2,1)S(1)}, u32[]{:S(2)}, u32[]{:S(2)}) collective-permute-start(bf16[256,1280]{1,0:T(8,128)(2,1)} %bitcast.8), channel_id=1, source_target_pairs={{0,4},{4,0},{8,12},{12,8},{1,5},{5,1},{9,13},{13,9},{2,6},{6,2},{1... | collective-permute-start | bytes 1966088 | tf_op jit(solution)/shard_map/ppermute | solution.py:656
  1.1 1.1 %shard_map.131 = (f32[16,128]{1,0:T(8,128)S(1)}, f32[16,128]{1,0:T(8,128)S(1)}, bf16[256,1280]{1,0:T(8,128)(2,1)S(1)}, s32[8,128]{1,0:T(8,128)S(1)}) custom-call(s32[16]{0:T(128)} %refs_0_.2, s32[16]{0:T(128)} %refs_1_.2, s32[6]{0:T(128)} %refs_2_.2, f32[1,128]{1,0:T(1,128)} %bitcast.12, bf16[256,1280]{1,0:T(8,128)(2,1)} %bitcast.9), custom_call_target="tpu_custom_call" | custom-call | bytes 655360 | tf_op jit(solution)/shard_map/pallas_call | solution.py:245
  2.3 0.8 %collective-permute-done.near_ref = bf16[256,1280]{1,0:T(8,128)(2,1)S(1)} collective-permute-done((bf16[256,1280]{1,0:T(8,128)(2,1)}, bf16[256,1280]{1,0:T(8,128)(2,1)S(1)}, u32[]{:S(2)}, u32[]{:S(2)}) %collective-permute-start) | collective-permute-done | bytes 655392 | tf_op jit(solution)/shard_map/ppermute | solution.py:656
  3.1 0.7 %shard_map.132 = (bf16[64,1280]{1,0:T(8,128)(2,1)S(1)}, bf16[64,1280]{1,0:T(8,128)(2,1)S(1)}) custom-call(bf16[256,1280]{1,0:T(8,128)(2,1)S(1)} %get-tuple-element.16.own_ref, bf16[256,1280]{1,0:T(8,128)(2,1)S(1)} %collective-permute-done.near_ref, s32[8,128]{1,0:T(8,128)S(1)} %get-tuple-element.17.table_ref), custom_call_target="tpu_custom_call" | custom-call | bytes 655360 | tf_op jit(solution)/shard_map/pallas_call | solution.py:245
  3.8 2.7 %collective-permute-start.1 = (bf16[64,1280]{1,0:T(8,128)(2,1)S(1)}, bf16[64,1280]{1,0:T(8,128)(2,1)S(1)}, u32[]{:S(2)}, u32[]{:S(2)}) collective-permute-start(bf16[64,1280]{1,0:T(8,128)(2,1)S(1)} %get-tuple-element.20), channel_id=1, source_target_pairs={{0,12},{4,8},{8,4},{12,0},{1,13},{5,9},{9,5},{13,1},{2,14},{6,10},... | collective-permute-start | bytes 491528 | tf_op jit(solution)/shard_map/ppermute | solution.py:656
  6.5 3.2 %shard_map.133 = (f32[64,640]{1,0:T(8,128)S(1)}, s16[64,640]{1,0:T(8,128)(2,1)S(1)}, f32[256,128]{1,0:T(8,128)S(1)}, bf16[1280,2048]{1,0:T(8,128)(2,1)S(1)}) custom-call(s32[4]{0:T(128)} %refs_0_.3, bf16[4,8192]{1,0:T(4,128)(2,1)} %refs_1_.3, bf16[4,128,1024]{2,1,0:T(8,128)(2,1)} %refs_2_.3, bf16[4,128,1024]{2,1,0:T(8,128)(2,1)} %refs_3_.1, ...), custom_call_target="tpu_custom_call" | custom-call | flops 16777216 | bytes 7340032 | tf_op jit(solution)/shard_map/pallas_call | solution.py:245
  9.7 1.0 %collective-permute-done.1.landed_ref = bf16[64,1280]{1,0:T(8,128)(2,1)S(1)} collective-permute-done((bf16[64,1280]{1,0:T(8,128)(2,1)S(1)}, bf16[64,1280]{1,0:T(8,128)(2,1)S(1)}, u32[]{:S(2)}, u32[]{:S(2)}) %collective-permute-start.1) | collective-permute-done | bytes 163872 | tf_op jit(solution)/shard_map/ppermute | solution.py:656
  10.7 1.2 %shard_map.134 = (f32[16,2048]{1,0:T(8,128)S(1)}, s16[16,2688]{1,0:T(8,128)(2,1)S(1)}, s16[16,2688]{1,0:T(8,128)(2,1)S(1)}, s16[16,2688]{1,0:T(8,128)(2,1)S(1)}) custom-call(bf16[64,1280]{1,0:T(8,128)(2,1)S(1)} %get-tuple-element.18.refs_5_.kept_ref, bf16[64,1280]{1,0:T(8,128)(2,1)S(1)} %collective-permute-done.1.landed_ref, ...), custom_call_target="tpu_custom_call" | custom-call | flops 335544320 | bytes 5242880 | tf_op jit(solution)/shard_map/pallas_call | solution.py:245
  12.0 4.3 %collective-permute-start.2 = (s16[16,2688]{1,0:T(8,128)(2,1)S(1)}, s16[16,2688]{1,0:T(8,128)(2,1)S(1)}, u32[]{:S(2)}, u32[]{:S(2)}) collective-permute-start(s16[16,2688]{1,0:T(8,128)(2,1)S(1)} %get-tuple-element.23), channel_id=1, source_target_pairs={{0,3},{1,2},{2,1},{3,0},{4,7},{5,6},{6,5},{7,4},{8,11},{9,10},{10,... | collective-permute-start | bytes 258056 | tf_op jit(solution)/shard_map/ppermute | solution.py:656
  16.3 0.0 collective-permute-start.3
  16.3 0.6 %collective-permute-start.4 = (s16[16,2688]{1,0:T(8,128)(2,1)S(1)}, s16[16,2688]{1,0:T(8,128)(2,1)S(1)}, u32[]{:S(2)}, u32[]{:S(2)}) collective-permute-start(s16[16,2688]{1,0:T(8,128)(2,1)S(1)} %get-tuple-element.25), channel_id=1, source_target_pairs={{0,1},{1,0},{2,3},{3,2},{4,5},{5,4},{6,7},{7,6},{8,9},{9,8},{10,11... | collective-permute-start | bytes 258056 | tf_op jit(solution)/shard_map/ppermute | solution.py:656
  17.0 2.8 %collective-permute-done.2.refs_0_ = s16[16,2688]{1,0:T(8,128)(2,1)S(1)} collective-permute-done((s16[16,2688]{1,0:T(8,128)(2,1)S(1)}, s16[16,2688]{1,0:T(8,128)(2,1)S(1)}, u32[]{:S(2)}, u32[]{:S(2)}) %collective-permute-start.2) | collective-permute-done | bytes 86048 | tf_op jit(solution)/shard_map/ppermute | solution.py:656
  19.7 4.1 %collective-permute-done.3.refs_1_ = s16[16,2688]{1,0:T(8,128)(2,1)S(1)} collective-permute-done((s16[16,2688]{1,0:T(8,128)(2,1)S(1)}, s16[16,2688]{1,0:T(8,128)(2,1)S(1)}, u32[]{:S(2)}, u32[]{:S(2)}) %collective-permute-start.3) | collective-permute-done | bytes 86048 | tf_op jit(solution)/shard_map/ppermute | solution.py:656
  23.8 0.0 collective-permute-done.4.refs_2_
  23.8 0.7 %shard_map.136.refs_0_ = bf16[16,2048]{1,0:T(8,128)(2,1)S(1)} custom-call(f32[16,2048]{1,0:T(8,128)S(1)} %get-tuple-element.27.own_ref, s16[16,2688]{1,0:T(8,128)(2,1)S(1)} %collective-permute-done.2.refs_0_, s16[16,2688]{1,0:T(8,128)(2,1)S(1)} %collective-permute-done.3.refs_1_, s16[16,2688]{1,0:T(8,128)(2,1)S(1)} %collective-permute-done.4.refs_2_, ...), custom_call_target="tpu_custom_call" | custom-call | tf_op jit(solution)/shard_map/pallas_call | solution.py:245
  24.5 0.8 %collective-permute-start.7 = (bf16[16,2048]{1,0:T(8,128)(2,1)S(1)}, bf16[16,2048]{1,0:T(8,128)(2,1)S(1)}, u32[]{:S(2)}, u32[]{:S(2)}) collective-permute-start(bf16[16,2048]{1,0:T(8,128)(2,1)S(1)} %shard_map.136.refs_0_), channel_id=1, source_target_pairs={{0,1},{1,2},{2,3},{3,0},{4,5},{5,6},{6,7},{7,4},{8,9},{9,10},{10,1... | collective-permute-start | bytes 196616 | tf_op jit(solution)/shard_map/ppermute | solution.py:661
  25.4 2.3 %collective-permute-start.6 = (bf16[16,2048]{1,0:T(8,128)(2,1)S(1)}, bf16[16,2048]{1,0:T(8,128)(2,1)S(1)}, u32[]{:S(2)}, u32[]{:S(2)}) collective-permute-start(bf16[16,2048]{1,0:T(8,128)(2,1)S(1)} %shard_map.136.refs_0_), channel_id=1, source_target_pairs={{0,2},{1,3},{2,0},{3,1},{4,6},{5,7},{6,4},{7,5},{8,10},{9,11},{10,... | collective-permute-start | bytes 196616 | tf_op jit(solution)/shard_map/ppermute | solution.py:661
  27.6 0.8 %collective-permute-start.5 = (bf16[16,2048]{1,0:T(8,128)(2,1)S(1)}, bf16[16,2048]{1,0:T(8,128)(2,1)S(1)}, u32[]{:S(2)}, u32[]{:S(2)}) collective-permute-start(bf16[16,2048]{1,0:T(8,128)(2,1)S(1)} %shard_map.136.refs_0_), channel_id=1, source_target_pairs={{0,3},{1,0},{2,1},{3,2},{4,7},{5,4},{6,5},{7,6},{8,11},{9,8},{10,9... | collective-permute-start | bytes 196616 | tf_op jit(solution)/shard_map/ppermute | solution.py:661
  28.4 0.4 %shard_map.135 = bf16[4,16,128]{2,1,0:T(8,128)(2,1)S(1)} custom-call(f32[64,640]{1,0:T(8,128)S(1)} %get-tuple-element.19.span_ref, s16[16,2688]{1,0:T(8,128)(2,1)S(1)} %collective-permute-done.2.refs_0_, s16[16,2688]{1,0:T(8,128)(2,1)S(1)} %collective-permute-done.3.refs_1_, s16[16,2688]{1,0:T(8,128)(2,1)S(1)} %collective-permute-done.4.refs_2_, ...), custom_call_target="tpu_custom_call" | custom-call | tf_op jit(solution)/shard_map/pallas_call | solution.py:245
  28.8 0.6 %copy.16 = bf16[1,4,16,128]{3,1,2,0:T(4,128)(2,1)} copy(bf16[1,4,16,128]{3,2,1,0:T(8,128)(2,1)S(1)} %bitcast.7) | data formatting | bytes 32768
  29.4 1.7 %collective-permute-done.7.refs_3_ = bf16[16,2048]{1,0:T(8,128)(2,1)S(1)} collective-permute-done((bf16[16,2048]{1,0:T(8,128)(2,1)S(1)}, bf16[16,2048]{1,0:T(8,128)(2,1)S(1)}, u32[]{:S(2)}, u32[]{:S(2)}) %collective-permute-start.7) | collective-permute-done | bytes 65568 | tf_op jit(solution)/shard_map/ppermute | solution.py:661
  31.1 1.6 %collective-permute-done.6.refs_2_ = bf16[16,2048]{1,0:T(8,128)(2,1)S(1)} collective-permute-done((bf16[16,2048]{1,0:T(8,128)(2,1)S(1)}, bf16[16,2048]{1,0:T(8,128)(2,1)S(1)}, u32[]{:S(2)}, u32[]{:S(2)}) %collective-permute-start.6) | collective-permute-done | bytes 65568 | tf_op jit(solution)/shard_map/ppermute | solution.py:661
  32.7 0.0 collective-permute-done.5.refs_1_
  32.7 0.7 %shard_map.137 = bf16[64,2048]{1,0:T(8,128)(2,1)} custom-call(bf16[16,2048]{1,0:T(8,128)(2,1)S(1)} %shard_map.136.refs_0_, bf16[16,2048]{1,0:T(8,128)(2,1)S(1)} %collective-permute-done.5.refs_1_, bf16[16,2048]{1,0:T(8,128)(2,1)S(1)} %collective-permute-done.6.refs_2_, bf16[16,2048]{1,0:T(8,128)(2,1)S(1)} %collective-permute-done.7.refs_3_), custom_call_target="tpu_custom_call" | custom-call | tf_op jit(solution)/shard_map/pallas_call | solution.py:245
  (4 shorter events, 0.0 us)
Async XLA Ops:
  0.6 2.5 %collective-permute-start = (bf16[256,1280]{1,0:T(8,128)(2,1)}, bf16[256,1280]{1,0:T(8,128)(2,1)S(1)}, u32[]{:S(2)}, u32[]{:S(2)}) collective-permute-start(bf16[256,1280]{1,0:T(8,128)(2,1)} %bitcast.8), channel_id=1, source_target_pairs={{0,4},{4,0},{8,12},{12,8},{1,5},{5,1},{9,13},{13,9},{2,6},{6,2},{1... | collective-permute-start | bytes 1966088 | tf_op jit(solution)/shard_map/ppermute | solution.py:656
  3.8 6.9 %collective-permute-start.1 = (bf16[64,1280]{1,0:T(8,128)(2,1)S(1)}, bf16[64,1280]{1,0:T(8,128)(2,1)S(1)}, u32[]{:S(2)}, u32[]{:S(2)}) collective-permute-start(bf16[64,1280]{1,0:T(8,128)(2,1)S(1)} %get-tuple-element.20), channel_id=1, source_target_pairs={{0,12},{4,8},{8,4},{12,0},{1,13},{5,9},{9,5},{13,1},{2,14},{6,10},... | collective-permute-start | bytes 491528 | tf_op jit(solution)/shard_map/ppermute | solution.py:656
  6.5 22.0 %copy-start = (bf16[4,1024]{1,0:T(4,128)(2,1)S(1)}, bf16[4,1024]{1,0:T(4,128)(2,1)}, u32[]{:S(2)}) copy-start(bf16[4,1024]{1,0:T(4,128)(2,1)} %refs_4_.3) | copy-start | bytes 24580
  6.5 22.0 %copy-start.1 = (bf16[4,1024]{1,0:T(4,128)(2,1)S(1)}, bf16[4,1024]{1,0:T(4,128)(2,1)}, u32[]{:S(2)}) copy-start(bf16[4,1024]{1,0:T(4,128)(2,1)} %refs_5_.1) | copy-start | bytes 24580
  12.0 7.8 %collective-permute-start.2 = (s16[16,2688]{1,0:T(8,128)(2,1)S(1)}, s16[16,2688]{1,0:T(8,128)(2,1)S(1)}, u32[]{:S(2)}, u32[]{:S(2)}) collective-permute-start(s16[16,2688]{1,0:T(8,128)(2,1)S(1)} %get-tuple-element.23), channel_id=1, source_target_pairs={{0,3},{1,2},{2,1},{3,0},{4,7},{5,6},{6,5},{7,4},{8,11},{9,10},{10,... | collective-permute-start | bytes 258056 | tf_op jit(solution)/shard_map/ppermute | solution.py:656
  16.3 7.5 %collective-permute-start.3 = (s16[16,2688]{1,0:T(8,128)(2,1)S(1)}, s16[16,2688]{1,0:T(8,128)(2,1)S(1)}, u32[]{:S(2)}, u32[]{:S(2)}) collective-permute-start(s16[16,2688]{1,0:T(8,128)(2,1)S(1)} %get-tuple-element.24), channel_id=1, source_target_pairs={{0,2},{1,3},{2,0},{3,1},{4,6},{5,7},{6,4},{7,5},{8,10},{9,11},{10,... | collective-permute-start | bytes 258056 | tf_op jit(solution)/shard_map/ppermute | solution.py:656
  16.3 7.5 %collective-permute-start.4 = (s16[16,2688]{1,0:T(8,128)(2,1)S(1)}, s16[16,2688]{1,0:T(8,128)(2,1)S(1)}, u32[]{:S(2)}, u32[]{:S(2)}) collective-permute-start(s16[16,2688]{1,0:T(8,128)(2,1)S(1)} %get-tuple-element.25), channel_id=1, source_target_pairs={{0,1},{1,0},{2,3},{3,2},{4,5},{5,4},{6,7},{7,6},{8,9},{9,8},{10,11... | collective-permute-start | bytes 258056 | tf_op jit(solution)/shard_map/ppermute | solution.py:656
  24.5 6.6 %collective-permute-start.7 = (bf16[16,2048]{1,0:T(8,128)(2,1)S(1)}, bf16[16,2048]{1,0:T(8,128)(2,1)S(1)}, u32[]{:S(2)}, u32[]{:S(2)}) collective-permute-start(bf16[16,2048]{1,0:T(8,128)(2,1)S(1)} %shard_map.136.refs_0_), channel_id=1, source_target_pairs={{0,1},{1,2},{2,3},{3,0},{4,5},{5,6},{6,7},{7,4},{8,9},{9,10},{10,1... | collective-permute-start | bytes 196616 | tf_op jit(solution)/shard_map/ppermute | solution.py:661
  25.4 7.3 %collective-permute-start.6 = (bf16[16,2048]{1,0:T(8,128)(2,1)S(1)}, bf16[16,2048]{1,0:T(8,128)(2,1)S(1)}, u32[]{:S(2)}, u32[]{:S(2)}) collective-permute-start(bf16[16,2048]{1,0:T(8,128)(2,1)S(1)} %shard_map.136.refs_0_), channel_id=1, source_target_pairs={{0,2},{1,3},{2,0},{3,1},{4,6},{5,7},{6,4},{7,5},{8,10},{9,11},{10,... | collective-permute-start | bytes 196616 | tf_op jit(solution)/shard_map/ppermute | solution.py:661
  27.6 5.1 %collective-permute-start.5 = (bf16[16,2048]{1,0:T(8,128)(2,1)S(1)}, bf16[16,2048]{1,0:T(8,128)(2,1)S(1)}, u32[]{:S(2)}, u32[]{:S(2)}) collective-permute-start(bf16[16,2048]{1,0:T(8,128)(2,1)S(1)} %shard_map.136.refs_0_), channel_id=1, source_target_pairs={{0,3},{1,0},{2,1},{3,2},{4,7},{5,4},{6,5},{7,6},{8,11},{9,8},{10,9... | collective-permute-start | bytes 196616 | tf_op jit(solution)/shard_map/ppermute | solution.py:661

commit v5 on v4

--- a/solution.py
+++ b/solution.py
@@ -270,6 +270,7 @@
 
 
 def prepare(states, key_gain, block_owner, block_slot, prompt_blocks):
+    token_count = states.shape[0]
     rows_here = CAP * BLK // lax.axis_size("tensor")
     slots_here = rows_here // BLK
     prompt_count = prompt_blocks.shape[0]
@@ -303,11 +304,11 @@
             def _():
                 source[CAP + slot[b]] = b
 
-        column = lax.broadcasted_iota(jnp.int32, (8, HD), 1)
-        table = jnp.zeros((8, HD), jnp.int32)
+        token = lax.broadcasted_iota(jnp.int32, (BLK, token_count), 1)
+        inner = lax.broadcasted_iota(jnp.int32, (BLK, token_count), 0)
         for j in range(2 * CAP):
-            table = jnp.where(column == j, source[j], table)
-        table_ref[...] = table
+            chosen = token == source[j] * BLK + inner
+            table_ref[pl.ds(j * BLK, BLK), :] = jnp.where(chosen, 1.0, 0.0).astype(BF16)
 
         lane = lax.broadcasted_iota(jnp.int32, (BLK, HD), 1)
         row = lax.broadcasted_iota(jnp.int32, (BLK, HD), 0)
@@ -336,7 +337,7 @@
             jax.ShapeDtypeStruct((rows_here, HD), F32),
             jax.ShapeDtypeStruct((rows_here, HD), F32),
             jax.ShapeDtypeStruct(states.shape, BF16),
-            jax.ShapeDtypeStruct((8, HD), jnp.int32),
+            jax.ShapeDtypeStruct((2 * CAP * BLK, token_count), BF16),
         ],
         [pltpu.SMEM(array.shape, jnp.int32) for array in fetched[:3]]
         + [
@@ -350,23 +351,15 @@
 
 def place_rows(own_states, near_states, table):
     width = own_states.shape[1]
-
-    def kernel(own_ref, near_ref, table_ref, keep_ref, send_ref, source, sem):
+    rows = CAP * BLK
+
+    def kernel(own_ref, near_ref, table_ref, keep_ref, send_ref):
         core = lax.rem(lax.axis_index("section"), 2)
-        copy = pltpu.make_async_copy(table_ref, source, sem)
-        copy.start()
-        copy.wait()
 
         def place(states):
-            for j in range(2 * CAP):
-                b = source[0, j]
-                start = pl.multiple_of(jnp.maximum(b, 0) * BLK, BLK)
-                target = (keep_ref, send_ref)[j // CAP]
-                target[pl.ds((j % CAP) * BLK, BLK), :] = states[pl.ds(start, BLK), :]
-
-                @pl.when(b < 0)
-                def _():
-                    target[pl.ds((j % CAP) * BLK, BLK), :] = jnp.zeros((BLK, width), BF16)
+            placed = jnp.dot(table_ref[...], states[...], preferred_element_type=F32).astype(BF16)
+            keep_ref[...] = placed[:rows]
+            send_ref[...] = placed[rows:]
 
         @pl.when(core == 0)
         def _():
@@ -380,8 +373,7 @@
         kernel,
         (own_states, near_states, table),
         [VMEM] * 3,
-        [jax.ShapeDtypeStruct((CAP * BLK, width), BF16)] * 2,
-        [pltpu.SMEM((8, HD), jnp.int32), pltpu.SemaphoreType.DMA(())],
+        [jax.ShapeDtypeStruct((rows, width), BF16)] * 2,
         moved=own_states.size * 2,
     )
 
@@ -533,6 +525,29 @@
     )
 
 
+def add_shares(total, shares):
+    rows, width = total.shape
+    count = len(shares)
+    share_width = shares[0].shape[1]
+
+    def kernel(total_ref, *refs):
+        share_refs, out_ref = refs[:count], refs[count]
+        scales = [
+            jnp.exp(as_float(ref[:, pl.ds(share_width - HD, HD)]) * (LN2 / OCTAVE)) * (1.0 / TOP)
+            for ref in share_refs
+        ]
+        for n in range(width // HD):
+            columns = pl.ds(n * HD, HD)
+            part = total_ref[:, columns]
+            for ref, scale in zip(share_refs, scales):
+                part = part + as_float(ref[:, columns]) * scale[:, LEVELS + n : LEVELS + n + 1]
+            out_ref[:, columns] = part
+
+    return on_chip(
+        kernel, (total, *shares), [VMEM] * (count + 1), [jax.ShapeDtypeStruct((rows, width), F32)]
+    )[0]
+
+
 def finish_rows(own, shares, cosine, sine):
     rows, width = own.shape
     share_count = len(shares)
@@ -686,7 +701,7 @@
     steps = (0,) + tuple(range(tensor_count - 1, 0, -1))
     own, *shares = project_rows(kept, landed, weight, span_code, steps)
     shares = [swap(share, "tensor", step) for share, step in zip(shares, steps[1:])]
-    finished = finish_rows(own, shares, cosine, sine)
+    finished = finish_rows(add_shares(own, [shares[0], shares[2]]), [shares[1]], cosine, sine)
     pieces = [finished] + [turn(finished, "tensor", step) for step in steps[1:]]
     block_pool = join_rows(pieces, steps)
     attended = merge_spans(span, shares, row_queries, new_keys, new_values, key_value_weight.shape[1])

time: 33.6 us -> 32.5 us (0.967)
  waiting for transfers between devices: 12 us -> 10.7 us
  starting transfers between devices: 12 us -> 12.8 us
  Pallas kernels: 8.12 us -> 7.57 us
    ppermute x3, waiting for transfers between devices: 3.28 us -> 2.15 us  [turn(): lax.ppermute(piece, axis, [(i, (i + step) % count) for i in range(count)])]
    ppermute x3, starting transfers between devices: 3.88 us -> 4.62 us  [turn(): lax.ppermute(piece, axis, [(i, (i + step) % count) for i in range(count)])]
    pallas_call x7 -> x8, Pallas kernels: 8.12 us -> 7.57 us  [on_chip(): pl.pallas_call(kernel, out_shape=out_shapes, in_specs=in_specs, out_specs...]
  transfers between devices with their start and end apart: 8 -> 8, of which waited for: 6 -> 7; matrix products, arithmetic and copies ran while one was open for 2% -> 2% of each run, Pallas kernels for 14% -> 15%
where the time goes in v5:
time: 32.5 us; the launch traced here: 32.3 us
  starting transfers between devices  12.8 us (39%)
  waiting for transfers between devices  10.7 us (33%)
  Pallas kernels  7.57 us (23%)
  between operations  0.69 us (2%)
  local copies, waits for them, and re-layouts  0.63 us (2%)
    ppermute x5, waiting for transfers between devices, swap(): lax.ppermute(piece, axis, [(i, i ^ step) for i in range(lax.axis_size(axi...  8.51 us
    ppermute x5, starting transfers between devices, swap(): lax.ppermute(piece, axis, [(i, i ^ step) for i in range(lax.axis_size(axi...  8.16 us
    pallas_call x8, Pallas kernels, on_chip(): pl.pallas_call(kernel, out_shape=out_shapes, in_specs=in_specs, out_specs...  7.57 us
    ppermute x3, starting transfers between devices, turn(): lax.ppermute(piece, axis, [(i, (i + step) % count) for i in range(count)])  4.62 us
    ppermute x3, waiting for transfers between devices, turn(): lax.ppermute(piece, axis, [(i, (i + step) % count) for i in range(count)])  2.15 us
  transfers between devices with their start and end apart: 8, of which 7 were waited for; matrix products, arithmetic and copies ran while one was open for 2% of the time, Pallas kernels for 15%

profile of v5, /device:TPU:0, one launch (start us, length us, event | category | flops | bytes accessed | tf_op | source)
XLA Modules:
  0.0 32.3 jit_solution(14801406050772220818)
XLA Ops:
  0.6 0.5 %collective-permute-start = (bf16[256,1280]{1,0:T(8,128)(2,1)}, bf16[256,1280]{1,0:T(8,128)(2,1)S(1)}, u32[]{:S(2)}, u32[]{:S(2)}) collective-permute-start(bf16[256,1280]{1,0:T(8,128)(2,1)} %bitcast.8), channel_id=1, source_target_pairs={{0,4},{4,0},{8,12},{12,8},{1,5},{5,1},{9,13},{13,9},{2,6},{6,2},{1... | collective-permute-start | bytes 1966088 | tf_op jit(solution)/shard_map/ppermute | solution.py:671
  1.1 1.1 %shard_map.131 = (f32[16,128]{1,0:T(8,128)S(1)}, f32[16,128]{1,0:T(8,128)S(1)}, bf16[256,1280]{1,0:T(8,128)(2,1)S(1)}, bf16[128,256]{1,0:T(8,128)(2,1)S(1)}) custom-call(s32[16]{0:T(128)} %refs_0_.2, s32[16]{0:T(128)} %refs_1_.2, s32[6]{0:T(128)} %refs_2_.2, f32[1,128]{1,0:T(1,128)} %bitcast.12, bf16[256,1280]{1,0:T(8,128)(2,1)} %bitcast.9), custom_call_target="tpu_custom_call" | custom-call | bytes 655360 | tf_op jit(solution)/shard_map/pallas_call | solution.py:245
  2.3 0.8 %collective-permute-done.near_ref = bf16[256,1280]{1,0:T(8,128)(2,1)S(1)} collective-permute-done((bf16[256,1280]{1,0:T(8,128)(2,1)}, bf16[256,1280]{1,0:T(8,128)(2,1)S(1)}, u32[]{:S(2)}, u32[]{:S(2)}) %collective-permute-start) | collective-permute-done | bytes 655392 | tf_op jit(solution)/shard_map/ppermute | solution.py:671
  3.1 0.3 shard_map.132
  3.4 2.7 %collective-permute-start.1 = (bf16[64,1280]{1,0:T(8,128)(2,1)S(1)}, bf16[64,1280]{1,0:T(8,128)(2,1)S(1)}, u32[]{:S(2)}, u32[]{:S(2)}) collective-permute-start(bf16[64,1280]{1,0:T(8,128)(2,1)S(1)} %get-tuple-element.20), channel_id=1, source_target_pairs={{0,12},{4,8},{8,4},{12,0},{1,13},{5,9},{9,5},{13,1},{2,14},{6,10},... | collective-permute-start | bytes 491528 | tf_op jit(solution)/shard_map/ppermute | solution.py:671
  6.0 3.2 %shard_map.133 = (f32[64,640]{1,0:T(8,128)S(1)}, s16[64,640]{1,0:T(8,128)(2,1)S(1)}, f32[256,128]{1,0:T(8,128)S(1)}, bf16[1280,2048]{1,0:T(8,128)(2,1)S(1)}) custom-call(s32[4]{0:T(128)} %refs_0_.3, bf16[4,8192]{1,0:T(4,128)(2,1)} %refs_1_.3, bf16[4,128,1024]{2,1,0:T(8,128)(2,1)} %refs_2_.3, bf16[4,128,1024]{2,1,0:T(8,128)(2,1)} %refs_3_.1, ...), custom_call_target="tpu_custom_call" | custom-call | flops 16777216 | bytes 7340032 | tf_op jit(solution)/shard_map/pallas_call | solution.py:245
  9.3 1.0 %collective-permute-done.1.landed_ref = bf16[64,1280]{1,0:T(8,128)(2,1)S(1)} collective-permute-done((bf16[64,1280]{1,0:T(8,128)(2,1)S(1)}, bf16[64,1280]{1,0:T(8,128)(2,1)S(1)}, u32[]{:S(2)}, u32[]{:S(2)}) %collective-permute-start.1) | collective-permute-done | bytes 163872 | tf_op jit(solution)/shard_map/ppermute | solution.py:671
  10.3 1.2 %shard_map.134 = (f32[16,2048]{1,0:T(8,128)S(1)}, s16[16,2688]{1,0:T(8,128)(2,1)S(1)}, s16[16,2688]{1,0:T(8,128)(2,1)S(1)}, s16[16,2688]{1,0:T(8,128)(2,1)S(1)}) custom-call(bf16[64,1280]{1,0:T(8,128)(2,1)S(1)} %get-tuple-element.18.refs_5_.kept_ref, bf16[64,1280]{1,0:T(8,128)(2,1)S(1)} %collective-permute-done.1.landed_ref, ...), custom_call_target="tpu_custom_call" | custom-call | flops 335544320 | bytes 5242880 | tf_op jit(solution)/shard_map/pallas_call | solution.py:245
  11.5 4.3 %collective-permute-start.2 = (s16[16,2688]{1,0:T(8,128)(2,1)S(1)}, s16[16,2688]{1,0:T(8,128)(2,1)S(1)}, u32[]{:S(2)}, u32[]{:S(2)}) collective-permute-start(s16[16,2688]{1,0:T(8,128)(2,1)S(1)} %get-tuple-element.23), channel_id=1, source_target_pairs={{0,3},{1,2},{2,1},{3,0},{4,7},{5,6},{6,5},{7,4},{8,11},{9,10},{10,... | collective-permute-start | bytes 258056 | tf_op jit(solution)/shard_map/ppermute | solution.py:671
  15.9 0.0 collective-permute-start.4
  15.9 0.6 %collective-permute-start.3 = (s16[16,2688]{1,0:T(8,128)(2,1)S(1)}, s16[16,2688]{1,0:T(8,128)(2,1)S(1)}, u32[]{:S(2)}, u32[]{:S(2)}) collective-permute-start(s16[16,2688]{1,0:T(8,128)(2,1)S(1)} %get-tuple-element.24), channel_id=1, source_target_pairs={{0,2},{1,3},{2,0},{3,1},{4,6},{5,7},{6,4},{7,5},{8,10},{9,11},{10,... | collective-permute-start | bytes 258056 | tf_op jit(solution)/shard_map/ppermute | solution.py:671
  16.5 2.7 %collective-permute-done.2.refs_0_ = s16[16,2688]{1,0:T(8,128)(2,1)S(1)} collective-permute-done((s16[16,2688]{1,0:T(8,128)(2,1)S(1)}, s16[16,2688]{1,0:T(8,128)(2,1)S(1)}, u32[]{:S(2)}, u32[]{:S(2)}) %collective-permute-start.2) | collective-permute-done | bytes 86048 | tf_op jit(solution)/shard_map/ppermute | solution.py:671
  19.2 2.4 %collective-permute-done.4.refs_2_.refs_1_ = s16[16,2688]{1,0:T(8,128)(2,1)S(1)} collective-permute-done((s16[16,2688]{1,0:T(8,128)(2,1)S(1)}, s16[16,2688]{1,0:T(8,128)(2,1)S(1)}, u32[]{:S(2)}, u32[]{:S(2)}) %collective-permute-start.4) | collective-permute-done | bytes 86048 | tf_op jit(solution)/shard_map/ppermute | solution.py:671
  21.7 0.2 shard_map.136.own_ref
  21.8 1.5 %collective-permute-done.3.refs_1_.refs_0_ = s16[16,2688]{1,0:T(8,128)(2,1)S(1)} collective-permute-done((s16[16,2688]{1,0:T(8,128)(2,1)S(1)}, s16[16,2688]{1,0:T(8,128)(2,1)S(1)}, u32[]{:S(2)}, u32[]{:S(2)}) %collective-permute-start.3) | collective-permute-done | bytes 86048 | tf_op jit(solution)/shard_map/ppermute | solution.py:671
  23.4 0.4 %shard_map.137.refs_0_ = bf16[16,2048]{1,0:T(8,128)(2,1)S(1)} custom-call(f32[16,2048]{1,0:T(8,128)S(1)} %shard_map.136.own_ref, s16[16,2688]{1,0:T(8,128)(2,1)S(1)} %collective-permute-done.3.refs_1_.refs_0_, f32[16,128]{1,0:T(8,128)S(1)} %get-tuple-element.28.refs_1_, f32[16,128]{1,0:T(8,128)S(1)} %get-tuple-element.29.refs_2_), custom_call_target="tpu_custom_call" | custom-call | tf_op jit(solution)/shard_map/pallas_call | solution.py:245
  23.8 0.1 collective-permute-start.7
  23.9 3.1 %collective-permute-start.6 = (bf16[16,2048]{1,0:T(8,128)(2,1)S(1)}, bf16[16,2048]{1,0:T(8,128)(2,1)S(1)}, u32[]{:S(2)}, u32[]{:S(2)}) collective-permute-start(bf16[16,2048]{1,0:T(8,128)(2,1)S(1)} %shard_map.137.refs_0_), channel_id=1, source_target_pairs={{0,2},{1,3},{2,0},{3,1},{4,6},{5,7},{6,4},{7,5},{8,10},{9,11},{10,... | collective-permute-start | bytes 196616 | tf_op jit(solution)/shard_map/ppermute | solution.py:676
  27.0 1.4 %collective-permute-start.5 = (bf16[16,2048]{1,0:T(8,128)(2,1)S(1)}, bf16[16,2048]{1,0:T(8,128)(2,1)S(1)}, u32[]{:S(2)}, u32[]{:S(2)}) collective-permute-start(bf16[16,2048]{1,0:T(8,128)(2,1)S(1)} %shard_map.137.refs_0_), channel_id=1, source_target_pairs={{0,3},{1,0},{2,1},{3,2},{4,7},{5,4},{6,5},{7,6},{8,11},{9,8},{10,9... | collective-permute-start | bytes 196616 | tf_op jit(solution)/shard_map/ppermute | solution.py:676
  28.4 0.4 %shard_map.135 = bf16[4,16,128]{2,1,0:T(8,128)(2,1)S(1)} custom-call(f32[64,640]{1,0:T(8,128)S(1)} %get-tuple-element.19.span_ref, s16[16,2688]{1,0:T(8,128)(2,1)S(1)} %collective-permute-done.2.refs_0_, s16[16,2688]{1,0:T(8,128)(2,1)S(1)} %collective-permute-done.3.refs_1_.refs_0_, s16[16,2688]{1,0:T(8,128)(2,1)S(1)} %collective-permute-done.4.refs_2_.refs_1_, ...), custom_call_target="tpu_custom_call" | custom-call | tf_op jit(solution)/shard_map/pallas_call | solution.py:245
  28.8 0.6 %copy.16 = bf16[1,4,16,128]{3,1,2,0:T(4,128)(2,1)} copy(bf16[1,4,16,128]{3,2,1,0:T(8,128)(2,1)S(1)} %bitcast.7) | data formatting | bytes 32768
  29.4 0.8 %collective-permute-done.7.refs_3_ = bf16[16,2048]{1,0:T(8,128)(2,1)S(1)} collective-permute-done((bf16[16,2048]{1,0:T(8,128)(2,1)S(1)}, bf16[16,2048]{1,0:T(8,128)(2,1)S(1)}, u32[]{:S(2)}, u32[]{:S(2)}) %collective-permute-start.7) | collective-permute-done | bytes 65568 | tf_op jit(solution)/shard_map/ppermute | solution.py:676
  30.2 1.4 %collective-permute-done.6.refs_2_ = bf16[16,2048]{1,0:T(8,128)(2,1)S(1)} collective-permute-done((bf16[16,2048]{1,0:T(8,128)(2,1)S(1)}, bf16[16,2048]{1,0:T(8,128)(2,1)S(1)}, u32[]{:S(2)}, u32[]{:S(2)}) %collective-permute-start.6) | collective-permute-done | bytes 65568 | tf_op jit(solution)/shard_map/ppermute | solution.py:676
  31.6 0.7 %shard_map.138 = bf16[64,2048]{1,0:T(8,128)(2,1)} custom-call(bf16[16,2048]{1,0:T(8,128)(2,1)S(1)} %shard_map.137.refs_0_, bf16[16,2048]{1,0:T(8,128)(2,1)S(1)} %collective-permute-done.5.refs_1_, bf16[16,2048]{1,0:T(8,128)(2,1)S(1)} %collective-permute-done.6.refs_2_, bf16[16,2048]{1,0:T(8,128)(2,1)S(1)} %collective-permute-done.7.refs_3_), custom_call_target="tpu_custom_call" | custom-call | tf_op jit(solution)/shard_map/pallas_call | solution.py:245
  (5 shorter events, 0.0 us)
Async XLA Ops:
  0.6 2.5 %collective-permute-start = (bf16[256,1280]{1,0:T(8,128)(2,1)}, bf16[256,1280]{1,0:T(8,128)(2,1)S(1)}, u32[]{:S(2)}, u32[]{:S(2)}) collective-permute-start(bf16[256,1280]{1,0:T(8,128)(2,1)} %bitcast.8), channel_id=1, source_target_pairs={{0,4},{4,0},{8,12},{12,8},{1,5},{5,1},{9,13},{13,9},{2,6},{6,2},{1... | collective-permute-start | bytes 1966088 | tf_op jit(solution)/shard_map/ppermute | solution.py:671
  3.4 6.9 %collective-permute-start.1 = (bf16[64,1280]{1,0:T(8,128)(2,1)S(1)}, bf16[64,1280]{1,0:T(8,128)(2,1)S(1)}, u32[]{:S(2)}, u32[]{:S(2)}) collective-permute-start(bf16[64,1280]{1,0:T(8,128)(2,1)S(1)} %get-tuple-element.20), channel_id=1, source_target_pairs={{0,12},{4,8},{8,4},{12,0},{1,13},{5,9},{9,5},{13,1},{2,14},{6,10},... | collective-permute-start | bytes 491528 | tf_op jit(solution)/shard_map/ppermute | solution.py:671
  6.0 22.4 %copy-start = (bf16[4,1024]{1,0:T(4,128)(2,1)S(1)}, bf16[4,1024]{1,0:T(4,128)(2,1)}, u32[]{:S(2)}) copy-start(bf16[4,1024]{1,0:T(4,128)(2,1)} %refs_4_.3) | copy-start | bytes 24580
  6.0 22.4 %copy-start.1 = (bf16[4,1024]{1,0:T(4,128)(2,1)S(1)}, bf16[4,1024]{1,0:T(4,128)(2,1)}, u32[]{:S(2)}) copy-start(bf16[4,1024]{1,0:T(4,128)(2,1)} %refs_5_.1) | copy-start | bytes 24580
  11.5 7.7 %collective-permute-start.2 = (s16[16,2688]{1,0:T(8,128)(2,1)S(1)}, s16[16,2688]{1,0:T(8,128)(2,1)S(1)}, u32[]{:S(2)}, u32[]{:S(2)}) collective-permute-start(s16[16,2688]{1,0:T(8,128)(2,1)S(1)} %get-tuple-element.23), channel_id=1, source_target_pairs={{0,3},{1,2},{2,1},{3,0},{4,7},{5,6},{6,5},{7,4},{8,11},{9,10},{10,... | collective-permute-start | bytes 258056 | tf_op jit(solution)/shard_map/ppermute | solution.py:671
  15.9 5.8 %collective-permute-start.4 = (s16[16,2688]{1,0:T(8,128)(2,1)S(1)}, s16[16,2688]{1,0:T(8,128)(2,1)S(1)}, u32[]{:S(2)}, u32[]{:S(2)}) collective-permute-start(s16[16,2688]{1,0:T(8,128)(2,1)S(1)} %get-tuple-element.25), channel_id=1, source_target_pairs={{0,1},{1,0},{2,3},{3,2},{4,5},{5,4},{6,7},{7,6},{8,9},{9,8},{10,11... | collective-permute-start | bytes 258056 | tf_op jit(solution)/shard_map/ppermute | solution.py:671
  15.9 7.5 %collective-permute-start.3 = (s16[16,2688]{1,0:T(8,128)(2,1)S(1)}, s16[16,2688]{1,0:T(8,128)(2,1)S(1)}, u32[]{:S(2)}, u32[]{:S(2)}) collective-permute-start(s16[16,2688]{1,0:T(8,128)(2,1)S(1)} %get-tuple-element.24), channel_id=1, source_target_pairs={{0,2},{1,3},{2,0},{3,1},{4,6},{5,7},{6,4},{7,5},{8,10},{9,11},{10,... | collective-permute-start | bytes 258056 | tf_op jit(solution)/shard_map/ppermute | solution.py:671
  23.8 6.4 %collective-permute-start.7 = (bf16[16,2048]{1,0:T(8,128)(2,1)S(1)}, bf16[16,2048]{1,0:T(8,128)(2,1)S(1)}, u32[]{:S(2)}, u32[]{:S(2)}) collective-permute-start(bf16[16,2048]{1,0:T(8,128)(2,1)S(1)} %shard_map.137.refs_0_), channel_id=1, source_target_pairs={{0,1},{1,2},{2,3},{3,0},{4,5},{5,6},{6,7},{7,4},{8,9},{9,10},{10,1... | collective-permute-start | bytes 196616 | tf_op jit(solution)/shard_map/ppermute | solution.py:676
  23.9 7.7 %collective-permute-start.6 = (bf16[16,2048]{1,0:T(8,128)(2,1)S(1)}, bf16[16,2048]{1,0:T(8,128)(2,1)S(1)}, u32[]{:S(2)}, u32[]{:S(2)}) collective-permute-start(bf16[16,2048]{1,0:T(8,128)(2,1)S(1)} %shard_map.137.refs_0_), channel_id=1, source_target_pairs={{0,2},{1,3},{2,0},{3,1},{4,6},{5,7},{6,4},{7,5},{8,10},{9,11},{10,... | collective-permute-start | bytes 196616 | tf_op jit(solution)/shard_map/ppermute | solution.py:676
  27.0 4.6 %collective-permute-start.5 = (bf16[16,2048]{1,0:T(8,128)(2,1)S(1)}, bf16[16,2048]{1,0:T(8,128)(2,1)S(1)}, u32[]{:S(2)}, u32[]{:S(2)}) collective-permute-start(bf16[16,2048]{1,0:T(8,128)(2,1)S(1)} %shard_map.137.refs_0_), channel_id=1, source_target_pairs={{0,3},{1,0},{2,1},{3,2},{4,7},{5,4},{6,5},{7,6},{8,11},{9,8},{10,9... | collective-permute-start | bytes 196616 | tf_op jit(solution)/shard_map/ppermute | solution.py:676

commit v6 on v5

--- a/solution.py
+++ b/solution.py
@@ -269,8 +269,9 @@
     return value.astype(jnp.int32).astype(F32)
 
 
-def prepare(states, key_gain, block_owner, block_slot, prompt_blocks):
+def prepare(states, weight, key_gain, block_owner, block_slot, prompt_blocks):
     token_count = states.shape[0]
+    half_depth = weight.shape[0] // 2
     rows_here = CAP * BLK // lax.axis_size("tensor")
     slots_here = rows_here // BLK
     prompt_count = prompt_blocks.shape[0]
@@ -278,12 +279,12 @@
     count = len(fetched)
 
     def kernel(*refs):
-        sources, states_hbm = refs[:count], refs[count]
-        cosine_ref, sine_ref, states_ref, table_ref = refs[count + 1 : count + 5]
-        held, (source, sems) = refs[count + 5 : 2 * count + 5], refs[2 * count + 5 :]
+        sources, states_hbm, weight_hbm = refs[:count], refs[count], refs[count + 1]
+        cosine_ref, sine_ref, states_ref, table_ref, weight_ref = refs[count + 2 : count + 7]
+        held, (source, sems) = refs[count + 7 : 2 * count + 7], refs[2 * count + 7 :]
         owner, slot, prompts, gain = held
-        copies = [pltpu.make_async_copy(s, d, sems.at[i]) for i, (s, d) in enumerate(zip(sources, held))]
-        copies.append(pltpu.make_async_copy(states_hbm, states_ref, sems.at[count]))
+        pairs = [*zip(sources, held), (states_hbm, states_ref), (weight_hbm.at[pl.ds(0, half_depth)], weight_ref)]
+        copies = [pltpu.make_async_copy(s, d, sems.at[i]) for i, (s, d) in enumerate(pairs)]
         for copy in copies:
             copy.start()
         group = lax.axis_index("section")
@@ -328,24 +329,26 @@
             sine = jnp.sin(angles) * far_gain
             sine_ref[pl.ds(s * BLK, BLK), :] = jnp.where(lane < HD // 2, -sine, sine)
         copies[count].wait()
+        copies[count + 1].wait()
 
     return on_chip(
         kernel,
-        [stays(array) for array in (*fetched, states)],
-        [HBM] * (count + 1),
+        [stays(array) for array in (*fetched, states, weight)],
+        [HBM] * (count + 2),
         [
             jax.ShapeDtypeStruct((rows_here, HD), F32),
             jax.ShapeDtypeStruct((rows_here, HD), F32),
             jax.ShapeDtypeStruct(states.shape, BF16),
             jax.ShapeDtypeStruct((2 * CAP * BLK, token_count), BF16),
+            jax.ShapeDtypeStruct((half_depth, weight.shape[1]), BF16),
         ],
         [pltpu.SMEM(array.shape, jnp.int32) for array in fetched[:3]]
         + [
             pltpu.VMEM((1, HD), F32),
             pltpu.SMEM((2 * CAP,), jnp.int32),
-            pltpu.SemaphoreType.DMA((count + 1,)),
+            pltpu.SemaphoreType.DMA((count + 2,)),
         ],
-        moved=2 * states.size,
+        moved=2 * states.size + weight.size,
     )
 
 
@@ -353,13 +356,14 @@
     width = own_states.shape[1]
     rows = CAP * BLK
 
-    def kernel(own_ref, near_ref, table_ref, keep_ref, send_ref):
+    def kernel(own_ref, near_ref, table_ref, keep_ref, *send_refs):
         core = lax.rem(lax.axis_index("section"), 2)
 
         def place(states):
             placed = jnp.dot(table_ref[...], states[...], preferred_element_type=F32).astype(BF16)
             keep_ref[...] = placed[:rows]
-            send_ref[...] = placed[rows:]
+            for k, send_ref in enumerate(send_refs):
+                send_ref[...] = placed[rows:, k * width // 2 : (k + 1) * width // 2]
 
         @pl.when(core == 0)
         def _():
@@ -373,12 +377,13 @@
         kernel,
         (own_states, near_states, table),
         [VMEM] * 3,
-        [jax.ShapeDtypeStruct((rows, width), BF16)] * 2,
+        [jax.ShapeDtypeStruct((rows, width), BF16)] + [jax.ShapeDtypeStruct((rows, width // 2), BF16)] * 2,
         moved=own_states.size * 2,
     )
 
 
 def attend_span(queries, cache_keys, cache_values, decode_lengths, weight, after):
+    half_depth = weight.shape[0] // 2
     row_count, local_len = cache_keys.shape[0], cache_keys.shape[1]
     width = row_count * HD
     fetched = [decode_lengths, queries, cache_keys, cache_values]
@@ -390,7 +395,8 @@
         held, (scores, weights, sems) = refs[count + 6 : 2 * count + 6], refs[2 * count + 6 :]
         length, packed, keys, values = held
         copies = [pltpu.make_async_copy(s, d, sems.at[i]) for i, (s, d) in enumerate(zip(sources, held))]
-        copies.append(pltpu.make_async_copy(weight_hbm, weight_ref, sems.at[count]))
+        rest = weight_hbm.at[pl.ds(half_depth, half_depth)]
+        copies.append(pltpu.make_async_copy(rest, weight_ref, sems.at[count]))
         for copy in copies:
             copy.start()
         rank = lax.axis_index("tensor")
@@ -460,7 +466,7 @@
             jax.ShapeDtypeStruct((H, width + HD), F32),
             jax.ShapeDtypeStruct((H, width + HD), I16),
             jax.ShapeDtypeStruct((row_count * H, HD), F32),
-            jax.ShapeDtypeStruct(weight.shape, BF16),
+            jax.ShapeDtypeStruct((half_depth, weight.shape[1]), BF16),
         ],
         [pltpu.SMEM((row_count,), jnp.int32)]
         + [pltpu.VMEM(array.shape, array.dtype) for array in fetched[1:]]
@@ -470,12 +476,33 @@
             pltpu.SemaphoreType.DMA((count + 1,)),
         ],
         flops=4 * row_count * H * HD * local_len,
-        moved=4 * cache_keys.size + 2 * weight.size,
-    )
-
-
-def project_rows(kept, landed, weight, span_code, steps):
-    slot_rows, depth = kept.shape
+        moved=4 * cache_keys.size + weight.size,
+    )
+
+
+def begin_rows(kept, landed, weight):
+    slot_rows, depth = landed.shape
+    width = weight.shape[1]
+
+    def kernel(kept_ref, landed_ref, weight_ref, out_ref):
+        far = lax.axis_index("section") >= 2
+        rows = jnp.where(far, landed_ref[...], kept_ref[:, pl.ds(0, depth)])
+        for c in range(0, width, 512):
+            columns = pl.ds(c, 512)
+            out_ref[:, columns] = jnp.dot(rows, weight_ref[:, columns], preferred_element_type=F32)
+
+    return on_chip(
+        kernel,
+        (kept, landed, weight),
+        [VMEM] * 3,
+        [jax.ShapeDtypeStruct((slot_rows, width), F32)],
+        flops=2 * slot_rows * depth * width,
+        moved=2 * weight.size,
+    )[0]
+
+
+def project_rows(begun, kept, landed, weight, span_code, steps):
+    slot_rows, depth = landed.shape
     width = weight.shape[1]
     rows_here = slot_rows // len(steps)
     heads_here = H // len(steps)
@@ -483,15 +510,17 @@
     share_width = width + span_width + HD
     step_width = 256
 
-    def kernel(kept_ref, landed_ref, weight_ref, span_ref, own_ref, *refs):
+    def kernel(begun_ref, kept_ref, landed_ref, weight_ref, span_ref, own_ref, *refs):
         share_refs, (held, code) = refs[:-2], refs[-2:]
         far = lax.axis_index("section") >= 2
         rank = lax.axis_index("tensor")
-        rows = jnp.where(far, landed_ref[...], kept_ref[...])
+        rows = jnp.where(far, landed_ref[...], kept_ref[:, pl.ds(depth, depth)])
         lane = lax.broadcasted_iota(jnp.int32, (slot_rows, HD), 1)
         levels = jnp.zeros((slot_rows, HD), F32)
         for c in range(0, width, step_width):
-            product = jnp.dot(rows, weight_ref[:, c : c + step_width], preferred_element_type=F32)
+            product = begun_ref[:, c : c + step_width] + jnp.dot(
+                rows, weight_ref[:, c : c + step_width], preferred_element_type=F32
+            )
             held[:, c : c + step_width] = product
             for m in range(0, step_width, HD):
                 tile = product[:, m : m + HD]
@@ -515,8 +544,8 @@
 
     return on_chip(
         kernel,
-        (kept, landed, weight, span_code),
-        [VMEM] * 4,
+        (begun, kept, landed, weight, span_code),
+        [VMEM] * 5,
         [jax.ShapeDtypeStruct((rows_here, width), F32)]
         + [jax.ShapeDtypeStruct((rows_here, share_width), I16)] * (len(steps) - 1),
         [pltpu.VMEM((slot_rows, width), F32), pltpu.VMEM((slot_rows, width + HD), I16)],
@@ -692,14 +721,17 @@
 ):
     tensor_count = lax.axis_size("tensor")
     near_states = swap(prompt[0], "section", 1)
-    cosine, sine, states, table = prepare(prompt[0], key_gain, block_owner, block_slot, prompt_blocks)
-    kept, sent = place_rows(states, near_states, table)
-    landed = swap(sent, "section", 3)
-    span, span_code, row_queries, weight = attend_span(
+    cosine, sine, states, table, first_weight = prepare(
+        prompt[0], key_value_weight, key_gain, block_owner, block_slot, prompt_blocks
+    )
+    kept, *sent = place_rows(states, near_states, table)
+    landed = [swap(half, "section", 3) for half in sent]
+    span, span_code, row_queries, rest_weight = attend_span(
         queries, cache_keys, cache_values, decode_lengths, key_value_weight, kept
     )
     steps = (0,) + tuple(range(tensor_count - 1, 0, -1))
-    own, *shares = project_rows(kept, landed, weight, span_code, steps)
+    begun = begin_rows(kept, landed[0], first_weight)
+    own, *shares = project_rows(begun, kept, landed[1], rest_weight, span_code, steps)
     shares = [swap(share, "tensor", step) for share, step in zip(shares, steps[1:])]
     finished = finish_rows(add_shares(own, [shares[0], shares[2]]), [shares[1]], cosine, sine)
     pieces = [finished] + [turn(finished, "tensor", step) for step in steps[1:]]

time: 32.5 us -> 32.3 us (level)
  waiting for transfers between devices: 10.7 us -> 10.2 us
  Pallas kernels: 7.57 us -> 8.06 us
    ppermute x5 -> x6, waiting for transfers between devices: 8.51 us -> 7.73 us  [swap(): lax.ppermute(piece, axis, [(i, i ^ step) for i in range(lax.axis_size(axi...]
    pallas_call x8 -> x9, Pallas kernels: 7.57 us -> 8.06 us  [on_chip(): pl.pallas_call(kernel, out_shape=out_shapes, in_specs=in_specs, out_specs...]
    ppermute x5 -> x6, starting transfers between devices: 8.16 us -> 7.96 us  [swap(): lax.ppermute(piece, axis, [(i, i ^ step) for i in range(lax.axis_size(axi...]
  transfers between devices with their start and end apart: 8 -> 9, of which waited for: 7 -> 6; matrix products, arithmetic and copies ran while one was open for 2% -> 2% of each run, Pallas kernels for 15% -> 18%
where the time goes in v6:
time: 32.3 us; the launch traced here: 32.2 us
  starting transfers between devices  12.6 us (39%)
  waiting for transfers between devices  10.2 us (32%)
  Pallas kernels  8.06 us (25%)
  between operations  0.73 us (2%)
  local copies, waits for them, and re-layouts  0.63 us (2%)
    pallas_call x9, Pallas kernels, on_chip(): pl.pallas_call(kernel, out_shape=out_shapes, in_specs=in_specs, out_specs...  8.06 us
    ppermute x6, starting transfers between devices, swap(): lax.ppermute(piece, axis, [(i, i ^ step) for i in range(lax.axis_size(axi...  7.96 us
    ppermute x6, waiting for transfers between devices, swap(): lax.ppermute(piece, axis, [(i, i ^ step) for i in range(lax.axis_size(axi...  7.73 us
    ppermute x3, starting transfers between devices, turn(): lax.ppermute(piece, axis, [(i, (i + step) % count) for i in range(count)])  4.62 us
    ppermute x3, waiting for transfers between devices, turn(): lax.ppermute(piece, axis, [(i, (i + step) % count) for i in range(count)])  2.44 us
  transfers between devices with their start and end apart: 9, of which 6 were waited for; matrix products, arithmetic and copies ran while one was open for 2% of the time, Pallas kernels for 18%

profile of v6, /device:TPU:0, one launch (start us, length us, event | category | flops | bytes accessed | tf_op | source)
XLA Modules:
  0.0 32.2 jit_solution(8083834217347626766)
XLA Ops:
  0.6 0.5 %collective-permute-start = (bf16[256,1280]{1,0:T(8,128)(2,1)}, bf16[256,1280]{1,0:T(8,128)(2,1)S(1)}, u32[]{:S(2)}, u32[]{:S(2)}) collective-permute-start(bf16[256,1280]{1,0:T(8,128)(2,1)} %bitcast.8), channel_id=1, source_target_pairs={{0,4},{4,0},{8,12},{12,8},{1,5},{5,1},{9,13},{13,9},{2,6},{6,2},{1... | collective-permute-start | bytes 1966088 | tf_op jit(solution)/shard_map/ppermute | solution.py:700
  1.1 2.0 %shard_map.131 = (f32[16,128]{1,0:T(8,128)S(1)}, f32[16,128]{1,0:T(8,128)S(1)}, bf16[256,1280]{1,0:T(8,128)(2,1)S(1)}, bf16[128,256]{1,0:T(8,128)(2,1)S(1)}, bf16[640,2048]{1,0:T(8,128)(2,1)S(1)}) custom-call(s32[16]{0:T(128)} %refs_0_.2, s32[16]{0:T(128)} %refs_1_.2, s32[6]{0:T(128)} %refs_2_.2, f32[1,128]{1,0:T(1,128)} %bitcast.12, ...), custom_call_target="tpu_custom_call" | custom-call | bytes 3276800 | tf_op jit(solution)/shard_map/pallas_call | solution.py:245
  3.2 0.3 shard_map.132
  3.5 2.7 %collective-permute-start.1 = (bf16[64,640]{1,0:T(8,128)(2,1)S(1)}, bf16[64,640]{1,0:T(8,128)(2,1)S(1)}, u32[]{:S(2)}, u32[]{:S(2)}) collective-permute-start(bf16[64,640]{1,0:T(8,128)(2,1)S(1)} %get-tuple-element.22), channel_id=1, source_target_pairs={{0,12},{4,8},{8,4},{12,0},{1,13},{5,9},{9,5},{13,1},{2,14},{6,10},... | collective-permute-start | bytes 245768 | tf_op jit(solution)/shard_map/ppermute | solution.py:700
  6.1 0.1 collective-permute-start.2
  6.2 2.7 %shard_map.133 = (f32[64,640]{1,0:T(8,128)S(1)}, s16[64,640]{1,0:T(8,128)(2,1)S(1)}, f32[256,128]{1,0:T(8,128)S(1)}, bf16[640,2048]{1,0:T(8,128)(2,1)S(1)}) custom-call(s32[4]{0:T(128)} %refs_0_.3, bf16[4,8192]{1,0:T(4,128)(2,1)} %refs_1_.3, bf16[4,128,1024]{2,1,0:T(8,128)(2,1)} %refs_2_.3, bf16[4,128,1024]{2,1,0:T(8,128)(2,1)} %refs_3_.1, ...), custom_call_target="tpu_custom_call" | custom-call | flops 16777216 | bytes 4718592 | tf_op jit(solution)/shard_map/pallas_call | solution.py:245
  8.9 0.6 %shard_map.134.begun_ref = f32[64,2048]{1,0:T(8,128)S(1)} custom-call(bf16[64,1280]{1,0:T(8,128)(2,1)S(1)} %get-tuple-element.20.refs_5_.kept_ref, bf16[64,640]{1,0:T(8,128)(2,1)S(1)} %collective-permute-done.1.landed_ref, bf16[640,2048]{1,0:T(8,128)(2,1)S(1)} %get-tuple-element.23.weight_ref), custom_call_target="tpu_custom_call" | custom-call | flops 167772160 | bytes 2621440 | tf_op jit(solution)/shard_map/pallas_call | solution.py:245
  9.6 1.0 %collective-permute-done.2.landed_ref = bf16[64,640]{1,0:T(8,128)(2,1)S(1)} collective-permute-done((bf16[64,640]{1,0:T(8,128)(2,1)S(1)}, bf16[64,640]{1,0:T(8,128)(2,1)S(1)}, u32[]{:S(2)}, u32[]{:S(2)}) %collective-permute-start.2) | collective-permute-done | bytes 81952 | tf_op jit(solution)/shard_map/ppermute | solution.py:700
  10.5 0.8 %shard_map.135 = (f32[16,2048]{1,0:T(8,128)S(1)}, s16[16,2688]{1,0:T(8,128)(2,1)S(1)}, s16[16,2688]{1,0:T(8,128)(2,1)S(1)}, s16[16,2688]{1,0:T(8,128)(2,1)S(1)}) custom-call(f32[64,2048]{1,0:T(8,128)S(1)} %shard_map.134.begun_ref, bf16[64,1280]{1,0:T(8,128)(2,1)S(1)} %get-tuple-element.20.refs_5_.kept_ref, ...), custom_call_target="tpu_custom_call" | custom-call | flops 167772160 | bytes 2621440 | tf_op jit(solution)/shard_map/pallas_call | solution.py:245
  11.3 4.1 %collective-permute-start.3 = (s16[16,2688]{1,0:T(8,128)(2,1)S(1)}, s16[16,2688]{1,0:T(8,128)(2,1)S(1)}, u32[]{:S(2)}, u32[]{:S(2)}) collective-permute-start(s16[16,2688]{1,0:T(8,128)(2,1)S(1)} %get-tuple-element.27), channel_id=1, source_target_pairs={{0,3},{1,2},{2,1},{3,0},{4,7},{5,6},{6,5},{7,4},{8,11},{9,10},{10,... | collective-permute-start | bytes 258056 | tf_op jit(solution)/shard_map/ppermute | solution.py:700
  15.4 0.6 %collective-permute-start.4 = (s16[16,2688]{1,0:T(8,128)(2,1)S(1)}, s16[16,2688]{1,0:T(8,128)(2,1)S(1)}, u32[]{:S(2)}, u32[]{:S(2)}) collective-permute-start(s16[16,2688]{1,0:T(8,128)(2,1)S(1)} %get-tuple-element.28), channel_id=1, source_target_pairs={{0,2},{1,3},{2,0},{3,1},{4,6},{5,7},{6,4},{7,5},{8,10},{9,11},{10,... | collective-permute-start | bytes 258056 | tf_op jit(solution)/shard_map/ppermute | solution.py:700
  16.0 2.7 %collective-permute-done.3.refs_0_ = s16[16,2688]{1,0:T(8,128)(2,1)S(1)} collective-permute-done((s16[16,2688]{1,0:T(8,128)(2,1)S(1)}, s16[16,2688]{1,0:T(8,128)(2,1)S(1)}, u32[]{:S(2)}, u32[]{:S(2)}) %collective-permute-start.3) | collective-permute-done | bytes 86048 | tf_op jit(solution)/shard_map/ppermute | solution.py:700
  18.7 2.5 %collective-permute-done.5.refs_2_.refs_1_ = s16[16,2688]{1,0:T(8,128)(2,1)S(1)} collective-permute-done((s16[16,2688]{1,0:T(8,128)(2,1)S(1)}, s16[16,2688]{1,0:T(8,128)(2,1)S(1)}, u32[]{:S(2)}, u32[]{:S(2)}) %collective-permute-start.5) | collective-permute-done | bytes 86048 | tf_op jit(solution)/shard_map/ppermute | solution.py:700
  21.2 0.2 shard_map.137.own_ref
  21.4 1.5 %collective-permute-done.4.refs_1_.refs_0_ = s16[16,2688]{1,0:T(8,128)(2,1)S(1)} collective-permute-done((s16[16,2688]{1,0:T(8,128)(2,1)S(1)}, s16[16,2688]{1,0:T(8,128)(2,1)S(1)}, u32[]{:S(2)}, u32[]{:S(2)}) %collective-permute-start.4) | collective-permute-done | bytes 86048 | tf_op jit(solution)/shard_map/ppermute | solution.py:700
  22.9 0.4 %shard_map.138.refs_0_ = bf16[16,2048]{1,0:T(8,128)(2,1)S(1)} custom-call(f32[16,2048]{1,0:T(8,128)S(1)} %shard_map.137.own_ref, s16[16,2688]{1,0:T(8,128)(2,1)S(1)} %collective-permute-done.4.refs_1_.refs_0_, f32[16,128]{1,0:T(8,128)S(1)} %get-tuple-element.32.refs_1_, f32[16,128]{1,0:T(8,128)S(1)} %get-tuple-element.33.refs_2_), custom_call_target="tpu_custom_call" | custom-call | tf_op jit(solution)/shard_map/pallas_call | solution.py:245
  23.3 0.1 collective-permute-start.8
  23.4 3.1 %collective-permute-start.7 = (bf16[16,2048]{1,0:T(8,128)(2,1)S(1)}, bf16[16,2048]{1,0:T(8,128)(2,1)S(1)}, u32[]{:S(2)}, u32[]{:S(2)}) collective-permute-start(bf16[16,2048]{1,0:T(8,128)(2,1)S(1)} %shard_map.138.refs_0_), channel_id=1, source_target_pairs={{0,2},{1,3},{2,0},{3,1},{4,6},{5,7},{6,4},{7,5},{8,10},{9,11},{10,... | collective-permute-start | bytes 196616 | tf_op jit(solution)/shard_map/ppermute | solution.py:705
  26.6 1.4 %collective-permute-start.6 = (bf16[16,2048]{1,0:T(8,128)(2,1)S(1)}, bf16[16,2048]{1,0:T(8,128)(2,1)S(1)}, u32[]{:S(2)}, u32[]{:S(2)}) collective-permute-start(bf16[16,2048]{1,0:T(8,128)(2,1)S(1)} %shard_map.138.refs_0_), channel_id=1, source_target_pairs={{0,3},{1,0},{2,1},{3,2},{4,7},{5,4},{6,5},{7,6},{8,11},{9,8},{10,9... | collective-permute-start | bytes 196616 | tf_op jit(solution)/shard_map/ppermute | solution.py:705
  28.0 0.4 %shard_map.136 = bf16[4,16,128]{2,1,0:T(8,128)(2,1)S(1)} custom-call(f32[64,640]{1,0:T(8,128)S(1)} %get-tuple-element.21.span_ref, s16[16,2688]{1,0:T(8,128)(2,1)S(1)} %collective-permute-done.3.refs_0_, s16[16,2688]{1,0:T(8,128)(2,1)S(1)} %collective-permute-done.4.refs_1_.refs_0_, s16[16,2688]{1,0:T(8,128)(2,1)S(1)} %collective-permute-done.5.refs_2_.refs_1_, ...), custom_call_target="tpu_custom_call" | custom-call | tf_op jit(solution)/shard_map/pallas_call | solution.py:245
  28.4 0.6 %copy.16 = bf16[1,4,16,128]{3,1,2,0:T(4,128)(2,1)} copy(bf16[1,4,16,128]{3,2,1,0:T(8,128)(2,1)S(1)} %bitcast.7) | data formatting | bytes 32768
  29.0 1.1 %collective-permute-done.8.refs_3_ = bf16[16,2048]{1,0:T(8,128)(2,1)S(1)} collective-permute-done((bf16[16,2048]{1,0:T(8,128)(2,1)S(1)}, bf16[16,2048]{1,0:T(8,128)(2,1)S(1)}, u32[]{:S(2)}, u32[]{:S(2)}) %collective-permute-start.8) | collective-permute-done | bytes 65568 | tf_op jit(solution)/shard_map/ppermute | solution.py:705
  30.1 1.3 %collective-permute-done.7.refs_2_ = bf16[16,2048]{1,0:T(8,128)(2,1)S(1)} collective-permute-done((bf16[16,2048]{1,0:T(8,128)(2,1)S(1)}, bf16[16,2048]{1,0:T(8,128)(2,1)S(1)}, u32[]{:S(2)}, u32[]{:S(2)}) %collective-permute-start.7) | collective-permute-done | bytes 65568 | tf_op jit(solution)/shard_map/ppermute | solution.py:705
  31.4 0.7 %shard_map.139 = bf16[64,2048]{1,0:T(8,128)(2,1)} custom-call(bf16[16,2048]{1,0:T(8,128)(2,1)S(1)} %shard_map.138.refs_0_, bf16[16,2048]{1,0:T(8,128)(2,1)S(1)} %collective-permute-done.6.refs_1_, bf16[16,2048]{1,0:T(8,128)(2,1)S(1)} %collective-permute-done.7.refs_2_, bf16[16,2048]{1,0:T(8,128)(2,1)S(1)} %collective-permute-done.8.refs_3_), custom_call_target="tpu_custom_call" | custom-call | tf_op jit(solution)/shard_map/pallas_call | solution.py:245
  (8 shorter events, 0.0 us)
Async XLA Ops:
  0.6 2.5 %collective-permute-start = (bf16[256,1280]{1,0:T(8,128)(2,1)}, bf16[256,1280]{1,0:T(8,128)(2,1)S(1)}, u32[]{:S(2)}, u32[]{:S(2)}) collective-permute-start(bf16[256,1280]{1,0:T(8,128)(2,1)} %bitcast.8), channel_id=1, source_target_pairs={{0,4},{4,0},{8,12},{12,8},{1,5},{5,1},{9,13},{13,9},{2,6},{6,2},{1... | collective-permute-start | bytes 1966088 | tf_op jit(solution)/shard_map/ppermute | solution.py:700
  3.5 5.5 %collective-permute-start.1 = (bf16[64,640]{1,0:T(8,128)(2,1)S(1)}, bf16[64,640]{1,0:T(8,128)(2,1)S(1)}, u32[]{:S(2)}, u32[]{:S(2)}) collective-permute-start(bf16[64,640]{1,0:T(8,128)(2,1)S(1)} %get-tuple-element.22), channel_id=1, source_target_pairs={{0,12},{4,8},{8,4},{12,0},{1,13},{5,9},{9,5},{13,1},{2,14},{6,10},... | collective-permute-start | bytes 245768 | tf_op jit(solution)/shard_map/ppermute | solution.py:700
  6.1 4.4 %collective-permute-start.2 = (bf16[64,640]{1,0:T(8,128)(2,1)S(1)}, bf16[64,640]{1,0:T(8,128)(2,1)S(1)}, u32[]{:S(2)}, u32[]{:S(2)}) collective-permute-start(bf16[64,640]{1,0:T(8,128)(2,1)S(1)} %get-tuple-element.24), channel_id=1, source_target_pairs={{0,12},{4,8},{8,4},{12,0},{1,13},{5,9},{9,5},{13,1},{2,14},{6,10},... | collective-permute-start | bytes 245768 | tf_op jit(solution)/shard_map/ppermute | solution.py:700
  9.5 18.5 %copy-start = (bf16[4,1024]{1,0:T(4,128)(2,1)S(1)}, bf16[4,1024]{1,0:T(4,128)(2,1)}, u32[]{:S(2)}) copy-start(bf16[4,1024]{1,0:T(4,128)(2,1)} %refs_4_.3) | copy-start | bytes 24580
  9.5 18.4 %copy-start.1 = (bf16[4,1024]{1,0:T(4,128)(2,1)S(1)}, bf16[4,1024]{1,0:T(4,128)(2,1)}, u32[]{:S(2)}) copy-start(bf16[4,1024]{1,0:T(4,128)(2,1)} %refs_5_.3) | copy-start | bytes 24580
  11.3 7.4 %collective-permute-start.3 = (s16[16,2688]{1,0:T(8,128)(2,1)S(1)}, s16[16,2688]{1,0:T(8,128)(2,1)S(1)}, u32[]{:S(2)}, u32[]{:S(2)}) collective-permute-start(s16[16,2688]{1,0:T(8,128)(2,1)S(1)} %get-tuple-element.27), channel_id=1, source_target_pairs={{0,3},{1,2},{2,1},{3,0},{4,7},{5,6},{6,5},{7,4},{8,11},{9,10},{10,... | collective-permute-start | bytes 258056 | tf_op jit(solution)/shard_map/ppermute | solution.py:700
  15.4 5.8 %collective-permute-start.5 = (s16[16,2688]{1,0:T(8,128)(2,1)S(1)}, s16[16,2688]{1,0:T(8,128)(2,1)S(1)}, u32[]{:S(2)}, u32[]{:S(2)}) collective-permute-start(s16[16,2688]{1,0:T(8,128)(2,1)S(1)} %get-tuple-element.29), channel_id=1, source_target_pairs={{0,1},{1,0},{2,3},{3,2},{4,5},{5,4},{6,7},{7,6},{8,9},{9,8},{10,11... | collective-permute-start | bytes 258056 | tf_op jit(solution)/shard_map/ppermute | solution.py:700
  15.4 7.5 %collective-permute-start.4 = (s16[16,2688]{1,0:T(8,128)(2,1)S(1)}, s16[16,2688]{1,0:T(8,128)(2,1)S(1)}, u32[]{:S(2)}, u32[]{:S(2)}) collective-permute-start(s16[16,2688]{1,0:T(8,128)(2,1)S(1)} %get-tuple-element.28), channel_id=1, source_target_pairs={{0,2},{1,3},{2,0},{3,1},{4,6},{5,7},{6,4},{7,5},{8,10},{9,11},{10,... | collective-permute-start | bytes 258056 | tf_op jit(solution)/shard_map/ppermute | solution.py:700
  23.3 6.7 %collective-permute-start.8 = (bf16[16,2048]{1,0:T(8,128)(2,1)S(1)}, bf16[16,2048]{1,0:T(8,128)(2,1)S(1)}, u32[]{:S(2)}, u32[]{:S(2)}) collective-permute-start(bf16[16,2048]{1,0:T(8,128)(2,1)S(1)} %shard_map.138.refs_0_), channel_id=1, source_target_pairs={{0,1},{1,2},{2,3},{3,0},{4,5},{5,6},{6,7},{7,4},{8,9},{9,10},{10,1... | collective-permute-start | bytes 196616 | tf_op jit(solution)/shard_map/ppermute | solution.py:705
  23.4 8.0 %collective-permute-start.7 = (bf16[16,2048]{1,0:T(8,128)(2,1)S(1)}, bf16[16,2048]{1,0:T(8,128)(2,1)S(1)}, u32[]{:S(2)}, u32[]{:S(2)}) collective-permute-start(bf16[16,2048]{1,0:T(8,128)(2,1)S(1)} %shard_map.138.refs_0_), channel_id=1, source_target_pairs={{0,2},{1,3},{2,0},{3,1},{4,6},{5,7},{6,4},{7,5},{8,10},{9,11},{10,... | collective-permute-start | bytes 196616 | tf_op jit(solution)/shard_map/ppermute | solution.py:705
  26.6 4.9 %collective-permute-start.6 = (bf16[16,2048]{1,0:T(8,128)(2,1)S(1)}, bf16[16,2048]{1,0:T(8,128)(2,1)S(1)}, u32[]{:S(2)}, u32[]{:S(2)}) collective-permute-start(bf16[16,2048]{1,0:T(8,128)(2,1)S(1)} %shard_map.138.refs_0_), channel_id=1, source_target_pairs={{0,3},{1,0},{2,1},{3,2},{4,7},{5,4},{6,5},{7,6},{8,11},{9,8},{10,9... | collective-permute-start | bytes 196616 | tf_op jit(solution)/shard_map/ppermute | solution.py:705

commit v7 on v6

--- a/solution.py
+++ b/solution.py
@@ -269,28 +269,31 @@
     return value.astype(jnp.int32).astype(F32)
 
 
-def prepare(states, weight, key_gain, block_owner, block_slot, prompt_blocks):
+def prepare(
+    states, key_gain, block_owner, block_slot, prompt_blocks, queries, cache_keys, cache_values, decode_lengths
+):
     token_count = states.shape[0]
-    half_depth = weight.shape[0] // 2
     rows_here = CAP * BLK // lax.axis_size("tensor")
     slots_here = rows_here // BLK
     prompt_count = prompt_blocks.shape[0]
-    fetched = [block_owner, block_slot, prompt_blocks, key_gain[None, :]]
+    row_count, local_len = cache_keys.shape[0], cache_keys.shape[1]
+    fetched = [block_owner, block_slot, prompt_blocks, decode_lengths, key_gain[None, :], queries, cache_keys]
     count = len(fetched)
 
     def kernel(*refs):
-        sources, states_hbm, weight_hbm = refs[:count], refs[count], refs[count + 1]
-        cosine_ref, sine_ref, states_ref, table_ref, weight_ref = refs[count + 2 : count + 7]
-        held, (source, sems) = refs[count + 7 : 2 * count + 7], refs[2 * count + 7 :]
-        owner, slot, prompts, gain = held
-        pairs = [*zip(sources, held), (states_hbm, states_ref), (weight_hbm.at[pl.ds(0, half_depth)], weight_ref)]
+        sources, states_hbm, value_hbm = refs[:count], refs[count], refs[count + 1]
+        outs, rest = refs[count + 2 : count + 10], refs[count + 10 :]
+        cosine_ref, sine_ref, states_ref, table_ref, weight_ref, stats_ref, query_ref, value_ref = outs
+        held, (source, scores, sems) = rest[:count], rest[count:]
+        owner, slot, prompts, length, gain, packed, keys = held
+        pairs = [*zip(sources, held), (states_hbm, states_ref), (value_hbm, value_ref)]
         copies = [pltpu.make_async_copy(s, d, sems.at[i]) for i, (s, d) in enumerate(pairs)]
         for copy in copies:
             copy.start()
         group = lax.axis_index("section")
         rank = lax.axis_index("tensor")
         core = lax.rem(group, 2)
-        for copy in copies[:count]:
+        for copy in copies[:6]:
             copy.wait()
 
         for j in range(2 * CAP):
@@ -328,84 +331,11 @@
             cosine_ref[pl.ds(s * BLK, BLK), :] = jnp.cos(angles) * gain[...]
             sine = jnp.sin(angles) * far_gain
             sine_ref[pl.ds(s * BLK, BLK), :] = jnp.where(lane < HD // 2, -sine, sine)
-        copies[count].wait()
-        copies[count + 1].wait()
-
-    return on_chip(
-        kernel,
-        [stays(array) for array in (*fetched, states, weight)],
-        [HBM] * (count + 2),
-        [
-            jax.ShapeDtypeStruct((rows_here, HD), F32),
-            jax.ShapeDtypeStruct((rows_here, HD), F32),
-            jax.ShapeDtypeStruct(states.shape, BF16),
-            jax.ShapeDtypeStruct((2 * CAP * BLK, token_count), BF16),
-            jax.ShapeDtypeStruct((half_depth, weight.shape[1]), BF16),
-        ],
-        [pltpu.SMEM(array.shape, jnp.int32) for array in fetched[:3]]
-        + [
-            pltpu.VMEM((1, HD), F32),
-            pltpu.SMEM((2 * CAP,), jnp.int32),
-            pltpu.SemaphoreType.DMA((count + 2,)),
-        ],
-        moved=2 * states.size + weight.size,
-    )
-
-
-def place_rows(own_states, near_states, table):
-    width = own_states.shape[1]
-    rows = CAP * BLK
-
-    def kernel(own_ref, near_ref, table_ref, keep_ref, *send_refs):
-        core = lax.rem(lax.axis_index("section"), 2)
-
-        def place(states):
-            placed = jnp.dot(table_ref[...], states[...], preferred_element_type=F32).astype(BF16)
-            keep_ref[...] = placed[:rows]
-            for k, send_ref in enumerate(send_refs):
-                send_ref[...] = placed[rows:, k * width // 2 : (k + 1) * width // 2]
-
-        @pl.when(core == 0)
-        def _():
-            place(own_ref)
-
-        @pl.when(core == 1)
-        def _():
-            place(near_ref)
-
-    return on_chip(
-        kernel,
-        (own_states, near_states, table),
-        [VMEM] * 3,
-        [jax.ShapeDtypeStruct((rows, width), BF16)] + [jax.ShapeDtypeStruct((rows, width // 2), BF16)] * 2,
-        moved=own_states.size * 2,
-    )
-
-
-def attend_span(queries, cache_keys, cache_values, decode_lengths, weight, after):
-    half_depth = weight.shape[0] // 2
-    row_count, local_len = cache_keys.shape[0], cache_keys.shape[1]
-    width = row_count * HD
-    fetched = [decode_lengths, queries, cache_keys, cache_values]
-    count = len(fetched)
-
-    def kernel(*refs):
-        sources, weight_hbm = refs[:count], refs[count]
-        span_ref, code_ref, query_ref, weight_ref = refs[count + 2 : count + 6]
-        held, (scores, weights, sems) = refs[count + 6 : 2 * count + 6], refs[2 * count + 6 :]
-        length, packed, keys, values = held
-        copies = [pltpu.make_async_copy(s, d, sems.at[i]) for i, (s, d) in enumerate(zip(sources, held))]
-        rest = weight_hbm.at[pl.ds(half_depth, half_depth)]
-        copies.append(pltpu.make_async_copy(rest, weight_ref, sems.at[count]))
-        for copy in copies:
-            copy.start()
-        rank = lax.axis_index("tensor")
-        copies[0].wait()
-        copies[1].wait()
+
         for h in range(H):
             piece = packed[:, pl.ds(h * HD, HD)].astype(F32)
             query_ref[pl.ds(h, row_count, stride=H), :] = piece
-        copies[2].wait()
+        copies[6].wait()
         for r in range(row_count):
             for pair in range(KVH // 2):
                 pair_queries = query_ref[pl.ds(r * H + pair * 2 * G, 2 * G), :].astype(BF16)
@@ -426,28 +356,96 @@
             peak = jnp.max(row_scores, axis=1, keepdims=True)
             weight = jnp.where(live, jnp.exp(row_scores - peak), 0.0)
             total = jnp.sum(weight, axis=1, keepdims=True)
-            weights[r] = weight.astype(BF16)
+            weight_ref[r] = weight.astype(BF16)
             stats = jnp.where(column == r, peak, stats)
             stats = jnp.where(column == row_count + r, total, stats)
-        span_ref[:, pl.ds(width, HD)] = stats
-        copies[3].wait()
-        levels = jnp.zeros((H, HD), F32)
+        stats_ref[...] = stats
+        copies[count].wait()
+        copies[count + 1].wait()
+
+    return on_chip(
+        kernel,
+        [stays(array) for array in (*fetched, states, cache_values)],
+        [HBM] * (count + 2),
+        [
+            jax.ShapeDtypeStruct((rows_here, HD), F32),
+            jax.ShapeDtypeStruct((rows_here, HD), F32),
+            jax.ShapeDtypeStruct(states.shape, BF16),
+            jax.ShapeDtypeStruct((2 * CAP * BLK, token_count), BF16),
+            jax.ShapeDtypeStruct((row_count, H, local_len), BF16),
+            jax.ShapeDtypeStruct((H, HD), F32),
+            jax.ShapeDtypeStruct((row_count * H, HD), F32),
+            jax.ShapeDtypeStruct(cache_values.shape, BF16),
+        ],
+        [pltpu.SMEM(array.shape, jnp.int32) for array in fetched[:4]]
+        + [pltpu.VMEM(array.shape, array.dtype) for array in fetched[4:]]
+        + [
+            pltpu.SMEM((2 * CAP,), jnp.int32),
+            pltpu.VMEM((row_count, H, local_len), F32),
+            pltpu.SemaphoreType.DMA((count + 2,)),
+        ],
+        flops=2 * row_count * H * HD * local_len,
+        moved=2 * (states.size + cache_keys.size + cache_values.size),
+    )
+
+
+def place_rows(own_states, near_states, table):
+    width = own_states.shape[1]
+    rows = CAP * BLK
+
+    def kernel(own_ref, near_ref, table_ref, keep_ref, *send_refs):
+        core = lax.rem(lax.axis_index("section"), 2)
+
+        def place(states):
+            placed = jnp.dot(table_ref[...], states[...], preferred_element_type=F32).astype(BF16)
+            keep_ref[...] = placed[:rows]
+            for k, send_ref in enumerate(send_refs):
+                send_ref[...] = placed[rows:, k * width // 2 : (k + 1) * width // 2]
+
+        @pl.when(core == 0)
+        def _():
+            place(own_ref)
+
+        @pl.when(core == 1)
+        def _():
+            place(near_ref)
+
+    return on_chip(
+        kernel,
+        (own_states, near_states, table),
+        [VMEM] * 3,
+        [jax.ShapeDtypeStruct((rows, width), BF16)] + [jax.ShapeDtypeStruct((rows, width // 2), BF16)] * 2,
+        moved=own_states.size * 2,
+    )
+
+
+def span_sums(weights, stats, values, after, steps):
+    row_count, _, local_len = weights.shape
+    width = row_count * HD
+    heads_here = H // len(steps)
+
+    def kernel(weight_ref, stats_ref, value_ref, after_ref, span_ref, *refs):
+        share_refs, code = refs[:-1], refs[-1]
+        rank = lax.axis_index("tensor")
+        column = lax.broadcasted_iota(jnp.int32, (H, HD), 1)
         for r in range(row_count):
             for pair in range(KVH // 2):
-                pair_weights = weights[r, pl.ds(pair * 2 * G, 2 * G), :]
+                pair_weights = weight_ref[r, pl.ds(pair * 2 * G, 2 * G), :]
                 for n in (2 * pair, 2 * pair + 1):
                     both = jnp.dot(
-                        pair_weights, values[r, :, n * HD : (n + 1) * HD], preferred_element_type=F32
+                        pair_weights, value_ref[r, :, n * HD : (n + 1) * HD], preferred_element_type=F32
                     )
                     span_ref[pl.ds(n * G, G), pl.ds(r * HD, HD)] = both[(n % 2) * G : (n % 2 + 1) * G]
+        stats = stats_ref[...]
+        span_ref[:, pl.ds(width, HD)] = stats
+        levels = jnp.zeros((H, HD), F32)
         for r in range(row_count):
             peak = jnp.max(jnp.abs(span_ref[:, pl.ds(r * HD, HD)]), axis=1, keepdims=True)
             levels = jnp.where(column == r, peak, levels)
         levels = level_of(levels)
         scale = TOP * jnp.exp(levels * (-LN2 / OCTAVE))
         for r in range(row_count):
-            out = span_ref[:, pl.ds(r * HD, HD)]
-            code_ref[:, pl.ds(r * HD, HD)] = as_int16(out * scale[:, r : r + 1])
+            code[:, pl.ds(r * HD, HD)] = as_int16(span_ref[:, pl.ds(r * HD, HD)] * scale[:, r : r + 1])
         peaks = jnp.maximum(stats, -TOP)
         fine = jnp.where(column < row_count, peaks, stats * HD)
         whole = jnp.floor(fine)
@@ -455,28 +453,20 @@
         coded = jnp.where(column < 2 * row_count, whole, 0.0)
         shifted = pltpu.roll(jnp.where(column < 2 * row_count, part, 0.0), 2 * row_count, 1)
         moved = pltpu.roll(jnp.where(column < row_count, levels, 0.0), 4 * row_count, 1)
-        code_ref[:, pl.ds(width, HD)] = as_int16(coded + shifted + moved)
-        copies[count].wait()
-
-    return on_chip(
-        kernel,
-        [stays(array) for array in (*fetched, weight)] + [after],
-        [HBM] * (count + 1) + [pl.BlockSpec(memory_space=pl.ANY)],
-        [
-            jax.ShapeDtypeStruct((H, width + HD), F32),
-            jax.ShapeDtypeStruct((H, width + HD), I16),
-            jax.ShapeDtypeStruct((row_count * H, HD), F32),
-            jax.ShapeDtypeStruct((half_depth, weight.shape[1]), BF16),
-        ],
-        [pltpu.SMEM((row_count,), jnp.int32)]
-        + [pltpu.VMEM(array.shape, array.dtype) for array in fetched[1:]]
-        + [
-            pltpu.VMEM((row_count, H, local_len), F32),
-            pltpu.VMEM((row_count, H, local_len), BF16),
-            pltpu.SemaphoreType.DMA((count + 1,)),
-        ],
-        flops=4 * row_count * H * HD * local_len,
-        moved=4 * cache_keys.size + weight.size,
+        code[:, pl.ds(width, HD)] = as_int16(coded + shifted + moved)
+        for k, step in enumerate(steps[1:]):
+            start = pl.multiple_of((rank ^ step) * heads_here, heads_here)
+            share_refs[k][...] = code[pl.ds(start, heads_here), :]
+
+    return on_chip(
+        kernel,
+        [weights, stats, values, after],
+        [VMEM] * 3 + [pl.BlockSpec(memory_space=pl.ANY)],
+        [jax.ShapeDtypeStruct((H, width + HD), F32)]
+        + [jax.ShapeDtypeStruct((heads_here, width + HD), I16)] * (len(steps) - 1),
+        [pltpu.VMEM((H, width + HD), I16)],
+        flops=2 * row_count * H * HD * local_len,
+        moved=12 * values.size,
     )
 
 
@@ -489,7 +479,7 @@
         rows = jnp.where(far, landed_ref[...], kept_ref[:, pl.ds(0, depth)])
         for c in range(0, width, 512):
             columns = pl.ds(c, 512)
-            out_ref[:, columns] = jnp.dot(rows, weight_ref[:, columns], preferred_element_type=F32)
+            out_ref[:, columns] = jnp.dot(rows, weight_ref[pl.ds(0, depth), columns], preferred_element_type=F32)
 
     return on_chip(
         kernel,
@@ -501,16 +491,14 @@
     )[0]
 
 
-def project_rows(begun, kept, landed, weight, span_code, steps):
+def project_rows(begun, kept, landed, weight, steps):
     slot_rows, depth = landed.shape
     width = weight.shape[1]
     rows_here = slot_rows // len(steps)
-    heads_here = H // len(steps)
-    span_width = span_code.shape[1] - HD
-    share_width = width + span_width + HD
+    share_width = width + HD
     step_width = 256
 
-    def kernel(begun_ref, kept_ref, landed_ref, weight_ref, span_ref, own_ref, *refs):
+    def kernel(begun_ref, kept_ref, landed_ref, weight_ref, own_ref, *refs):
         share_refs, (held, code) = refs[:-2], refs[-2:]
         far = lax.axis_index("section") >= 2
         rank = lax.axis_index("tensor")
@@ -519,7 +507,7 @@
         levels = jnp.zeros((slot_rows, HD), F32)
         for c in range(0, width, step_width):
             product = begun_ref[:, c : c + step_width] + jnp.dot(
-                rows, weight_ref[:, c : c + step_width], preferred_element_type=F32
+                rows, weight_ref[pl.ds(depth, depth), pl.ds(c, step_width)], preferred_element_type=F32
             )
             held[:, c : c + step_width] = product
             for m in range(0, step_width, HD):
@@ -535,17 +523,14 @@
 
         own_ref[...] = held[rows_of(0), :]
         for k, step in enumerate(steps[1:]):
-            heads = pl.ds(pl.multiple_of((rank ^ step) * heads_here, heads_here), heads_here)
+            levels_code = code[rows_of(step), pl.ds(width, HD)]
             share_refs[k][:, pl.ds(0, width)] = code[rows_of(step), pl.ds(0, width)]
-            share_refs[k][:, pl.ds(width, span_width)] = span_ref[heads, pl.ds(0, span_width)]
-            stats = as_float(span_ref[heads, pl.ds(span_width, HD)])
-            both = jnp.where(lane[:rows_here] < LEVELS, stats, as_float(code[rows_of(step), pl.ds(width, HD)]))
-            share_refs[k][:, pl.ds(width + span_width, HD)] = as_int16(both)
-
-    return on_chip(
-        kernel,
-        (begun, kept, landed, weight, span_code),
-        [VMEM] * 5,
+            share_refs[k][:, pl.ds(width, HD)] = levels_code
+
+    return on_chip(
+        kernel,
+        (begun, kept, landed, weight),
+        [VMEM] * 4,
         [jax.ShapeDtypeStruct((rows_here, width), F32)]
         + [jax.ShapeDtypeStruct((rows_here, share_width), I16)] * (len(steps) - 1),
         [pltpu.VMEM((slot_rows, width), F32), pltpu.VMEM((slot_rows, width + HD), I16)],
@@ -554,15 +539,28 @@
     )
 
 
+def hand_on(piece, ahead):
+    count = len(ahead)
+
+    def kernel(piece_ref, *refs):
+        refs[count][...] = piece_ref[...]
+
+    return on_chip(
+        kernel,
+        (piece, *ahead),
+        [VMEM] + [pl.BlockSpec(memory_space=pl.ANY)] * count,
+        [jax.ShapeDtypeStruct(piece.shape, piece.dtype)],
+    )[0]
+
+
 def add_shares(total, shares):
     rows, width = total.shape
     count = len(shares)
-    share_width = shares[0].shape[1]
 
     def kernel(total_ref, *refs):
         share_refs, out_ref = refs[:count], refs[count]
         scales = [
-            jnp.exp(as_float(ref[:, pl.ds(share_width - HD, HD)]) * (LN2 / OCTAVE)) * (1.0 / TOP)
+            jnp.exp(as_float(ref[:, pl.ds(ref.shape[1] - HD, HD)]) * (LN2 / OCTAVE)) * (1.0 / TOP)
             for ref in share_refs
         ]
         for n in range(width // HD):
@@ -580,13 +578,12 @@
 def finish_rows(own, shares, cosine, sine):
     rows, width = own.shape
     share_count = len(shares)
-    share_width = shares[0].shape[1]
 
     def kernel(own_ref, *refs):
         share_refs = refs[:share_count]
         cosine_ref, sine_ref, out_ref = refs[share_count:]
         scales = [
-            jnp.exp(as_float(ref[:, pl.ds(share_width - HD, HD)]) * (LN2 / OCTAVE)) * (1.0 / TOP)
+            jnp.exp(as_float(ref[:, pl.ds(ref.shape[1] - HD, HD)]) * (LN2 / OCTAVE)) * (1.0 / TOP)
             for ref in share_refs
         ]
         for n in range(width // HD):
@@ -608,7 +605,7 @@
     )[0]
 
 
-def merge_spans(span, shares, queries, new_keys, new_values, begin):
+def merge_spans(span, shares, queries, new_keys, new_values):
     row_count = new_keys.shape[0]
     share_count = len(shares)
     heads_here = shares[0].shape[0]
@@ -634,7 +631,7 @@
 
         stats, scales = [span_ref[heads, pl.ds(width, HD)]], []
         for ref in share_refs:
-            code = as_float(ref[:, pl.ds(begin + width, HD)])
+            code = as_float(ref[:, pl.ds(width, HD)])
             column = lax.broadcasted_iota(jnp.int32, code.shape, 1)
             fine = code + pltpu.roll(code, HD - 2 * row_count, 1) * (1.0 / TOP)
             stats.append(jnp.where(column < row_count, fine, fine * (1.0 / HD)))
@@ -643,7 +640,7 @@
         def part(k, r):
             if k == 0:
                 return span_ref[heads, pl.ds(r * HD, HD)]
-            coded = as_float(share_refs[k - 1][:, pl.ds(begin + r * HD, HD)])
+            coded = as_float(share_refs[k - 1][:, pl.ds(r * HD, HD)])
             return coded * scales[k - 1][:, 4 * row_count + r : 4 * row_count + r + 1]
 
         for r in range(row_count):
@@ -721,22 +718,22 @@
 ):
     tensor_count = lax.axis_size("tensor")
     near_states = swap(prompt[0], "section", 1)
-    cosine, sine, states, table, first_weight = prepare(
-        prompt[0], key_value_weight, key_gain, block_owner, block_slot, prompt_blocks
+    cosine, sine, states, table, weights, stats, row_queries, values = prepare(
+        prompt[0], key_gain, block_owner, block_slot, prompt_blocks, queries, cache_keys, cache_values, decode_lengths
     )
     kept, *sent = place_rows(states, near_states, table)
     landed = [swap(half, "section", 3) for half in sent]
-    span, span_code, row_queries, rest_weight = attend_span(
-        queries, cache_keys, cache_values, decode_lengths, key_value_weight, kept
-    )
-    steps = (0,) + tuple(range(tensor_count - 1, 0, -1))
-    begun = begin_rows(kept, landed[0], first_weight)
-    own, *shares = project_rows(begun, kept, landed[1], rest_weight, span_code, steps)
-    shares = [swap(share, "tensor", step) for share, step in zip(shares, steps[1:])]
-    finished = finish_rows(add_shares(own, [shares[0], shares[2]]), [shares[1]], cosine, sine)
+    steps = (0, 3, 2, 1)
+    span, *span_codes = span_sums(weights, stats, values, kept, steps)
+    span_shares = [swap(code, "tensor", step) for code, step in zip(span_codes, steps[1:])]
+    begun = begin_rows(kept, landed[0], key_value_weight)
+    own, far, near, mid = project_rows(begun, kept, landed[1], key_value_weight, (0, 3, 1, 2))
+    far, near = swap(far, "tensor", 3), swap(near, "tensor", 1)
+    mid = swap(hand_on(mid, span_shares), "tensor", 2)
+    finished = finish_rows(add_shares(own, [far, near]), [mid], cosine, sine)
     pieces = [finished] + [turn(finished, "tensor", step) for step in steps[1:]]
     block_pool = join_rows(pieces, steps)
-    attended = merge_spans(span, shares, row_queries, new_keys, new_values, key_value_weight.shape[1])
+    attended = merge_spans(span, span_shares, row_queries, new_keys, new_values)
     return (attended, block_pool.reshape(1, CAP, BLK, -1))
 
 

time: 32.3 us -> 31.7 us (0.981)
  starting transfers between devices: 12.6 us -> 17.4 us
  waiting for transfers between devices: 10.2 us -> 6.49 us
  Pallas kernels: 8.06 us -> 6.37 us
    ppermute x6 -> x9, starting transfers between devices: 7.96 us -> 12.4 us  [swap(): lax.ppermute(piece, axis, [(i, i ^ step) for i in range(lax.axis_size(axi...]
    ppermute x6 -> x9, waiting for transfers between devices: 7.73 us -> 4.66 us  [swap(): lax.ppermute(piece, axis, [(i, i ^ step) for i in range(lax.axis_size(axi...]
    pallas_call x9 -> x10, Pallas kernels: 8.06 us -> 6.37 us  [on_chip(): pl.pallas_call(kernel, out_shape=out_shapes, in_specs=in_specs, out_specs...]
    ppermute x3, waiting for transfers between devices: 2.44 us -> 1.83 us  [turn(): lax.ppermute(piece, axis, [(i, (i + step) % count) for i in range(count)])]
    ppermute x3, starting transfers between devices: 4.62 us -> 5.01 us  [turn(): lax.ppermute(piece, axis, [(i, (i + step) % count) for i in range(count)])]
  transfers between devices with their start and end apart: 9 -> 12, of which waited for: 6 -> 5; matrix products, arithmetic and copies ran while one was open for 2% -> 2% of each run, Pallas kernels for 18% -> 16%
where the time goes in v7:
time: 31.7 us; the launch traced here: 31.6 us
  starting transfers between devices  17.4 us (55%)
  waiting for transfers between devices  6.49 us (20%)
  Pallas kernels  6.37 us (20%)
  between operations  0.74 us (2%)
  local copies, waits for them, and re-layouts  0.63 us (2%)
    ppermute x9, starting transfers between devices, swap(): lax.ppermute(piece, axis, [(i, i ^ step) for i in range(lax.axis_size(axi...  12.4 us
    pallas_call x10, Pallas kernels, on_chip(): pl.pallas_call(kernel, out_shape=out_shapes, in_specs=in_specs, out_specs...  6.37 us
    ppermute x3, starting transfers between devices, turn(): lax.ppermute(piece, axis, [(i, (i + step) % count) for i in range(count)])  5.01 us
    ppermute x9, waiting for transfers between devices, swap(): lax.ppermute(piece, axis, [(i, i ^ step) for i in range(lax.axis_size(axi...  4.66 us
    ppermute x3, waiting for transfers between devices, turn(): lax.ppermute(piece, axis, [(i, (i + step) % count) for i in range(count)])  1.83 us
  transfers between devices with their start and end apart: 12, of which 5 were waited for; matrix products, arithmetic and copies ran while one was open for 2% of the time, Pallas kernels for 16%

profile of v7, /device:TPU:0, one launch (start us, length us, event | category | flops | bytes accessed | tf_op | source)
XLA Modules:
  0.0 31.6 jit_solution(17085350015795864024)
XLA Ops:
  0.6 0.5 %collective-permute-start = (bf16[256,1280]{1,0:T(8,128)(2,1)}, bf16[256,1280]{1,0:T(8,128)(2,1)S(1)}, u32[]{:S(2)}, u32[]{:S(2)}) collective-permute-start(bf16[256,1280]{1,0:T(8,128)(2,1)} %bitcast.8), channel_id=1, source_target_pairs={{0,4},{4,0},{8,12},{12,8},{1,5},{5,1},{9,13},{13,9},{2,6},{6,2},{1... | collective-permute-start | bytes 1966088 | tf_op jit(solution)/shard_map/ppermute | solution.py:697
  1.2 2.4 %shard_map.131 = (f32[16,128]{1,0:T(8,128)S(1)}, f32[16,128]{1,0:T(8,128)S(1)}, bf16[256,1280]{1,0:T(8,128)(2,1)S(1)}, bf16[128,256]{1,0:T(8,128)(2,1)S(1)}, bf1...) custom-call(s32[16]{0:T(128)} %refs_0_.1, ...), custom_call_target="tpu_custom_call" | custom-call | flops 8388608 | bytes 2752512 | tf_op jit(solution)/shard_map/pallas_call | solution.py:245
  3.6 0.3 shard_map.132
  3.9 2.8 %collective-permute-start.4 = (bf16[64,640]{1,0:T(8,128)(2,1)S(1)}, bf16[64,640]{1,0:T(8,128)(2,1)S(1)}, u32[]{:S(2)}, u32[]{:S(2)}) collective-permute-start(bf16[64,640]{1,0:T(8,128)(2,1)S(1)} %get-tuple-element.32), channel_id=1, source_target_pairs={{0,12},{4,8},{8,4},{12,0},{1,13},{5,9},{9,5},{13,1},{2,14},{6,10},... | collective-permute-start | bytes 245768 | tf_op jit(solution)/shard_map/ppermute | solution.py:697
  6.7 0.6 %shard_map.133 = (f32[64,640]{1,0:T(8,128)S(1)}, s16[16,640]{1,0:T(8,128)(2,1)S(1)}, s16[16,640]{1,0:T(8,128)(2,1)S(1)}, s16[16,640]{1,0:T(8,128)(2,1)S(1)}) custom-call(bf16[4,64,128]{2,1,0:T(8,128)(2,1)S(1)} %get-tuple-element.21.weight_ref, f32[64,128]{1,0:T(8,128)S(1)} %get-tuple-element.22.stats_ref, ...), custom_call_target="tpu_custom_call" | custom-call | flops 8388608 | bytes 6291456 | tf_op jit(solution)/shard_map/pallas_call | solution.py:245
  7.3 3.7 %collective-permute-start.1 = (s16[16,640]{1,0:T(8,128)(2,1)S(1)}, s16[16,640]{1,0:T(8,128)(2,1)S(1)}, u32[]{:S(2)}, u32[]{:S(2)}) collective-permute-start(s16[16,640]{1,0:T(8,128)(2,1)S(1)} %get-tuple-element.28), channel_id=1, source_target_pairs={{0,3},{1,2},{2,1},{3,0},{4,7},{5,6},{6,5},{7,4},{8,11},{9,10},{10,... | collective-permute-start | bytes 61448 | tf_op jit(solution)/shard_map/ppermute | solution.py:697
  11.0 0.8 %collective-permute-start.3 = (s16[16,640]{1,0:T(8,128)(2,1)S(1)}, s16[16,640]{1,0:T(8,128)(2,1)S(1)}, u32[]{:S(2)}, u32[]{:S(2)}) collective-permute-start(s16[16,640]{1,0:T(8,128)(2,1)S(1)} %get-tuple-element.30), channel_id=1, source_target_pairs={{0,1},{1,0},{2,3},{3,2},{4,5},{5,4},{6,7},{7,6},{8,9},{9,8},{10,11... | collective-permute-start | bytes 61448 | tf_op jit(solution)/shard_map/ppermute | solution.py:697
  11.8 0.6 %shard_map.135.begun_ref = f32[64,2048]{1,0:T(8,128)S(1)} custom-call(bf16[64,1280]{1,0:T(8,128)(2,1)S(1)} %get-tuple-element.26.after_ref.kept_ref, bf16[64,640]{1,0:T(8,128)(2,1)S(1)} %collective-permute-done.4.landed_ref, bf16[1280,2048]{1,0:T(8,128)(2,1)S(1)} %copy-done), custom_call_target="tpu_custom_call" | custom-call | flops 167772160 | bytes 5242880 | tf_op jit(solution)/shard_map/pallas_call | solution.py:245
  12.4 0.8 %shard_map.136 = (f32[16,2048]{1,0:T(8,128)S(1)}, s16[16,2176]{1,0:T(8,128)(2,1)S(1)}, s16[16,2176]{1,0:T(8,128)(2,1)S(1)}, s16[16,2176]{1,0:T(8,128)(2,1)S(1)}) custom-call(f32[64,2048]{1,0:T(8,128)S(1)} %shard_map.135.begun_ref, bf16[64,1280]{1,0:T(8,128)(2,1)S(1)} %get-tuple-element.26.after_ref.kept_ref, ...), custom_call_target="tpu_custom_call" | custom-call | flops 167772160 | bytes 5242880 | tf_op jit(solution)/shard_map/pallas_call | solution.py:245
  13.2 3.7 %collective-permute-start.6 = (s16[16,2176]{1,0:T(8,128)(2,1)S(1)}, s16[16,2176]{1,0:T(8,128)(2,1)S(1)}, u32[]{:S(2)}, u32[]{:S(2)}) collective-permute-start(s16[16,2176]{1,0:T(8,128)(2,1)S(1)} %get-tuple-element.35), channel_id=1, source_target_pairs={{0,3},{1,2},{2,1},{3,0},{4,7},{5,6},{6,5},{7,4},{8,11},{9,10},{10,... | collective-permute-start | bytes 208904 | tf_op jit(solution)/shard_map/ppermute | solution.py:697
  16.9 0.9 %collective-permute-start.8 = (s16[16,2176]{1,0:T(8,128)(2,1)S(1)}, s16[16,2176]{1,0:T(8,128)(2,1)S(1)}, u32[]{:S(2)}, u32[]{:S(2)}) collective-permute-start(s16[16,2176]{1,0:T(8,128)(2,1)S(1)} %shard_map.138), channel_id=1, source_target_pairs={{0,2},{1,3},{2,0},{3,1},{4,6},{5,7},{6,4},{7,5},{8,10},{9,11},{10,... | collective-permute-start | bytes 208904 | tf_op jit(solution)/shard_map/ppermute | solution.py:697
  17.8 2.1 %collective-permute-done.6.refs_0_ = s16[16,2176]{1,0:T(8,128)(2,1)S(1)} collective-permute-done((s16[16,2176]{1,0:T(8,128)(2,1)S(1)}, s16[16,2176]{1,0:T(8,128)(2,1)S(1)}, u32[]{:S(2)}, u32[]{:S(2)}) %collective-permute-start.6) | collective-permute-done | bytes 69664 | tf_op jit(solution)/shard_map/ppermute | solution.py:697
  19.9 1.9 %collective-permute-done.7.refs_1_ = s16[16,2176]{1,0:T(8,128)(2,1)S(1)} collective-permute-done((s16[16,2176]{1,0:T(8,128)(2,1)S(1)}, s16[16,2176]{1,0:T(8,128)(2,1)S(1)}, u32[]{:S(2)}, u32[]{:S(2)}) %collective-permute-start.7) | collective-permute-done | bytes 69664 | tf_op jit(solution)/shard_map/ppermute | solution.py:697
  21.8 0.2 shard_map.137.own_ref
  22.0 0.6 %collective-permute-done.8.refs_0_ = s16[16,2176]{1,0:T(8,128)(2,1)S(1)} collective-permute-done((s16[16,2176]{1,0:T(8,128)(2,1)S(1)}, s16[16,2176]{1,0:T(8,128)(2,1)S(1)}, u32[]{:S(2)}, u32[]{:S(2)}) %collective-permute-start.8) | collective-permute-done | bytes 69664 | tf_op jit(solution)/shard_map/ppermute | solution.py:697
  22.6 0.4 %shard_map.139.refs_0_ = bf16[16,2048]{1,0:T(8,128)(2,1)S(1)} custom-call(f32[16,2048]{1,0:T(8,128)S(1)} %shard_map.137.own_ref, s16[16,2176]{1,0:T(8,128)(2,1)S(1)} %collective-permute-done.8.refs_0_, f32[16,128]{1,0:T(8,128)S(1)} %get-tuple-element.38.refs_1_, f32[16,128]{1,0:T(8,128)S(1)} %get-tuple-element.39.refs_2_), custom_call_target="tpu_custom_call" | custom-call | tf_op jit(solution)/shard_map/pallas_call | solution.py:245
  23.0 1.7 %collective-permute-start.11 = (bf16[16,2048]{1,0:T(8,128)(2,1)S(1)}, bf16[16,2048]{1,0:T(8,128)(2,1)S(1)}, u32[]{:S(2)}, u32[]{:S(2)}) collective-permute-start(bf16[16,2048]{1,0:T(8,128)(2,1)S(1)} %shard_map.139.refs_0_), channel_id=1, source_target_pairs={{0,1},{1,2},{2,3},{3,0},{4,5},{5,6},{6,7},{7,4},{8,9},{9,10},{10,1... | collective-permute-start | bytes 196616 | tf_op jit(solution)/shard_map/ppermute | solution.py:702
  24.7 1.1 %collective-permute-start.10 = (bf16[16,2048]{1,0:T(8,128)(2,1)S(1)}, bf16[16,2048]{1,0:T(8,128)(2,1)S(1)}, u32[]{:S(2)}, u32[]{:S(2)}) collective-permute-start(bf16[16,2048]{1,0:T(8,128)(2,1)S(1)} %shard_map.139.refs_0_), channel_id=1, source_target_pairs={{0,2},{1,3},{2,0},{3,1},{4,6},{5,7},{6,4},{7,5},{8,10},{9,11},{10,... | collective-permute-start | bytes 196616 | tf_op jit(solution)/shard_map/ppermute | solution.py:702
  25.8 2.2 %collective-permute-start.9 = (bf16[16,2048]{1,0:T(8,128)(2,1)S(1)}, bf16[16,2048]{1,0:T(8,128)(2,1)S(1)}, u32[]{:S(2)}, u32[]{:S(2)}) collective-permute-start(bf16[16,2048]{1,0:T(8,128)(2,1)S(1)} %shard_map.139.refs_0_), channel_id=1, source_target_pairs={{0,3},{1,0},{2,1},{3,2},{4,7},{5,4},{6,5},{7,6},{8,11},{9,8},{10,9... | collective-permute-start | bytes 196616 | tf_op jit(solution)/shard_map/ppermute | solution.py:702
  28.0 0.4 %shard_map.134 = bf16[4,16,128]{2,1,0:T(8,128)(2,1)S(1)} custom-call(f32[64,640]{1,0:T(8,128)S(1)} %get-tuple-element.27.span_ref, s16[16,640]{1,0:T(8,128)(2,1)S(1)} %collective-permute-done.1.refs_0_, s16[16,640]{1,0:T(8,128)(2,1)S(1)} %collective-permute-done.2.refs_1_, s16[16,640]{1,0:T(8,128)(2,1)S(1)} %collective-permute-done.3.refs_2_, ...), custom_call_target="tpu_custom_call" | custom-call | tf_op jit(solution)/shard_map/pallas_call | solution.py:245
  28.4 0.6 %copy.16 = bf16[1,4,16,128]{3,1,2,0:T(4,128)(2,1)} copy(bf16[1,4,16,128]{3,2,1,0:T(8,128)(2,1)S(1)} %bitcast.7) | data formatting | bytes 32768
  29.0 0.3 %collective-permute-done.11.refs_3_ = bf16[16,2048]{1,0:T(8,128)(2,1)S(1)} collective-permute-done((bf16[16,2048]{1,0:T(8,128)(2,1)S(1)}, bf16[16,2048]{1,0:T(8,128)(2,1)S(1)}, u32[]{:S(2)}, u32[]{:S(2)}) %collective-permute-start.11) | collective-permute-done | bytes 65568 | tf_op jit(solution)/shard_map/ppermute | solution.py:702
  29.4 1.5 %collective-permute-done.10.refs_2_ = bf16[16,2048]{1,0:T(8,128)(2,1)S(1)} collective-permute-done((bf16[16,2048]{1,0:T(8,128)(2,1)S(1)}, bf16[16,2048]{1,0:T(8,128)(2,1)S(1)}, u32[]{:S(2)}, u32[]{:S(2)}) %collective-permute-start.10) | collective-permute-done | bytes 65568 | tf_op jit(solution)/shard_map/ppermute | solution.py:702
  30.9 0.7 %shard_map.140 = bf16[64,2048]{1,0:T(8,128)(2,1)} custom-call(bf16[16,2048]{1,0:T(8,128)(2,1)S(1)} %shard_map.139.refs_0_, bf16[16,2048]{1,0:T(8,128)(2,1)S(1)} %collective-permute-done.9.refs_1_, bf16[16,2048]{1,0:T(8,128)(2,1)S(1)} %collective-permute-done.10.refs_2_, bf16[16,2048]{1,0:T(8,128)(2,1)S(1)} %collective-permute-done.11.refs_3_), custom_call_target="tpu_custom_call" | custom-call | tf_op jit(solution)/shard_map/pallas_call | solution.py:245
  (17 shorter events, 0.1 us)
Async XLA Ops:
  0.6 11.2 %copy-start = (bf16[1280,2048]{1,0:T(8,128)(2,1)S(1)}, bf16[1280,2048]{1,0:T(8,128)(2,1)}, u32[]{:S(2)}) copy-start(bf16[1280,2048]{1,0:T(8,128)(2,1)} %weight_ref.3) | copy-start | bytes 15728644
  0.6 3.0 %collective-permute-start = (bf16[256,1280]{1,0:T(8,128)(2,1)}, bf16[256,1280]{1,0:T(8,128)(2,1)S(1)}, u32[]{:S(2)}, u32[]{:S(2)}) collective-permute-start(bf16[256,1280]{1,0:T(8,128)(2,1)} %bitcast.8), channel_id=1, source_target_pairs={{0,4},{4,0},{8,12},{12,8},{1,5},{5,1},{9,13},{13,9},{2,6},{6,2},{1... | collective-permute-start | bytes 1966088 | tf_op jit(solution)/shard_map/ppermute | solution.py:697
  3.9 7.9 %collective-permute-start.4 = (bf16[64,640]{1,0:T(8,128)(2,1)S(1)}, bf16[64,640]{1,0:T(8,128)(2,1)S(1)}, u32[]{:S(2)}, u32[]{:S(2)}) collective-permute-start(bf16[64,640]{1,0:T(8,128)(2,1)S(1)} %get-tuple-element.32), channel_id=1, source_target_pairs={{0,12},{4,8},{8,4},{12,0},{1,13},{5,9},{9,5},{13,1},{2,14},{6,10},... | collective-permute-start | bytes 245768 | tf_op jit(solution)/shard_map/ppermute | solution.py:697
  6.7 5.7 %collective-permute-start.5 = (bf16[64,640]{1,0:T(8,128)(2,1)S(1)}, bf16[64,640]{1,0:T(8,128)(2,1)S(1)}, u32[]{:S(2)}, u32[]{:S(2)}) collective-permute-start(bf16[64,640]{1,0:T(8,128)(2,1)S(1)} %get-tuple-element.33), channel_id=1, source_target_pairs={{0,12},{4,8},{8,4},{12,0},{1,13},{5,9},{9,5},{13,1},{2,14},{6,10},... | collective-permute-start | bytes 245768 | tf_op jit(solution)/shard_map/ppermute | solution.py:697
  7.3 9.5 %collective-permute-start.1 = (s16[16,640]{1,0:T(8,128)(2,1)S(1)}, s16[16,640]{1,0:T(8,128)(2,1)S(1)}, u32[]{:S(2)}, u32[]{:S(2)}) collective-permute-start(s16[16,640]{1,0:T(8,128)(2,1)S(1)} %get-tuple-element.28), channel_id=1, source_target_pairs={{0,3},{1,2},{2,1},{3,0},{4,7},{5,6},{6,5},{7,4},{8,11},{9,10},{10,... | collective-permute-start | bytes 61448 | tf_op jit(solution)/shard_map/ppermute | solution.py:697
  11.0 5.9 %collective-permute-start.2 = (s16[16,640]{1,0:T(8,128)(2,1)S(1)}, s16[16,640]{1,0:T(8,128)(2,1)S(1)}, u32[]{:S(2)}, u32[]{:S(2)}) collective-permute-start(s16[16,640]{1,0:T(8,128)(2,1)S(1)} %get-tuple-element.29), channel_id=1, source_target_pairs={{0,2},{1,3},{2,0},{3,1},{4,6},{5,7},{6,4},{7,5},{8,10},{9,11},{10,... | collective-permute-start | bytes 61448 | tf_op jit(solution)/shard_map/ppermute | solution.py:697
  11.0 17.0 %copy-start.1 = (bf16[4,1024]{1,0:T(4,128)(2,1)S(1)}, bf16[4,1024]{1,0:T(4,128)(2,1)}, u32[]{:S(2)}) copy-start(bf16[4,1024]{1,0:T(4,128)(2,1)} %refs_4_.1) | copy-start | bytes 24580
  11.0 17.0 %copy-start.2 = (bf16[4,1024]{1,0:T(4,128)(2,1)S(1)}, bf16[4,1024]{1,0:T(4,128)(2,1)}, u32[]{:S(2)}) copy-start(bf16[4,1024]{1,0:T(4,128)(2,1)} %refs_5_.3) | copy-start | bytes 24580
  11.0 5.9 %collective-permute-start.3 = (s16[16,640]{1,0:T(8,128)(2,1)S(1)}, s16[16,640]{1,0:T(8,128)(2,1)S(1)}, u32[]{:S(2)}, u32[]{:S(2)}) collective-permute-start(s16[16,640]{1,0:T(8,128)(2,1)S(1)} %get-tuple-element.30), channel_id=1, source_target_pairs={{0,1},{1,0},{2,3},{3,2},{4,5},{5,4},{6,7},{7,6},{8,9},{9,8},{10,11... | collective-permute-start | bytes 61448 | tf_op jit(solution)/shard_map/ppermute | solution.py:697
  13.2 6.7 %collective-permute-start.6 = (s16[16,2176]{1,0:T(8,128)(2,1)S(1)}, s16[16,2176]{1,0:T(8,128)(2,1)S(1)}, u32[]{:S(2)}, u32[]{:S(2)}) collective-permute-start(s16[16,2176]{1,0:T(8,128)(2,1)S(1)} %get-tuple-element.35), channel_id=1, source_target_pairs={{0,3},{1,2},{2,1},{3,0},{4,7},{5,6},{6,5},{7,4},{8,11},{9,10},{10,... | collective-permute-start | bytes 208904 | tf_op jit(solution)/shard_map/ppermute | solution.py:697
  16.9 4.9 %collective-permute-start.7 = (s16[16,2176]{1,0:T(8,128)(2,1)S(1)}, s16[16,2176]{1,0:T(8,128)(2,1)S(1)}, u32[]{:S(2)}, u32[]{:S(2)}) collective-permute-start(s16[16,2176]{1,0:T(8,128)(2,1)S(1)} %get-tuple-element.36), channel_id=1, source_target_pairs={{0,1},{1,0},{2,3},{3,2},{4,5},{5,4},{6,7},{7,6},{8,9},{9,8},{10,11... | collective-permute-start | bytes 208904 | tf_op jit(solution)/shard_map/ppermute | solution.py:697
  16.9 5.7 %collective-permute-start.8 = (s16[16,2176]{1,0:T(8,128)(2,1)S(1)}, s16[16,2176]{1,0:T(8,128)(2,1)S(1)}, u32[]{:S(2)}, u32[]{:S(2)}) collective-permute-start(s16[16,2176]{1,0:T(8,128)(2,1)S(1)} %shard_map.138), channel_id=1, source_target_pairs={{0,2},{1,3},{2,0},{3,1},{4,6},{5,7},{6,4},{7,5},{8,10},{9,11},{10,... | collective-permute-start | bytes 208904 | tf_op jit(solution)/shard_map/ppermute | solution.py:697
  23.0 6.4 %collective-permute-start.11 = (bf16[16,2048]{1,0:T(8,128)(2,1)S(1)}, bf16[16,2048]{1,0:T(8,128)(2,1)S(1)}, u32[]{:S(2)}, u32[]{:S(2)}) collective-permute-start(bf16[16,2048]{1,0:T(8,128)(2,1)S(1)} %shard_map.139.refs_0_), channel_id=1, source_target_pairs={{0,1},{1,2},{2,3},{3,0},{4,5},{5,6},{6,7},{7,4},{8,9},{9,10},{10,1... | collective-permute-start | bytes 196616 | tf_op jit(solution)/shard_map/ppermute | solution.py:702
  24.7 6.2 %collective-permute-start.10 = (bf16[16,2048]{1,0:T(8,128)(2,1)S(1)}, bf16[16,2048]{1,0:T(8,128)(2,1)S(1)}, u32[]{:S(2)}, u32[]{:S(2)}) collective-permute-start(bf16[16,2048]{1,0:T(8,128)(2,1)S(1)} %shard_map.139.refs_0_), channel_id=1, source_target_pairs={{0,2},{1,3},{2,0},{3,1},{4,6},{5,7},{6,4},{7,5},{8,10},{9,11},{10,... | collective-permute-start | bytes 196616 | tf_op jit(solution)/shard_map/ppermute | solution.py:702
  25.8 5.0 %collective-permute-start.9 = (bf16[16,2048]{1,0:T(8,128)(2,1)S(1)}, bf16[16,2048]{1,0:T(8,128)(2,1)S(1)}, u32[]{:S(2)}, u32[]{:S(2)}) collective-permute-start(bf16[16,2048]{1,0:T(8,128)(2,1)S(1)} %shard_map.139.refs_0_), channel_id=1, source_target_pairs={{0,3},{1,0},{2,1},{3,2},{4,7},{5,4},{6,5},{7,6},{8,11},{9,8},{10,9... | collective-permute-start | bytes 196616 | tf_op jit(solution)/shard_map/ppermute | solution.py:702

commit v8 on v7

--- a/solution.py
+++ b/solution.py
@@ -393,14 +393,13 @@
     width = own_states.shape[1]
     rows = CAP * BLK
 
-    def kernel(own_ref, near_ref, table_ref, keep_ref, *send_refs):
+    def kernel(own_ref, near_ref, table_ref, keep_ref, send_ref):
         core = lax.rem(lax.axis_index("section"), 2)
 
         def place(states):
             placed = jnp.dot(table_ref[...], states[...], preferred_element_type=F32).astype(BF16)
             keep_ref[...] = placed[:rows]
-            for k, send_ref in enumerate(send_refs):
-                send_ref[...] = placed[rows:, k * width // 2 : (k + 1) * width // 2]
+            send_ref[...] = placed[rows:]
 
         @pl.when(core == 0)
         def _():
@@ -414,7 +413,7 @@
         kernel,
         (own_states, near_states, table),
         [VMEM] * 3,
-        [jax.ShapeDtypeStruct((rows, width), BF16)] + [jax.ShapeDtypeStruct((rows, width // 2), BF16)] * 2,
+        [jax.ShapeDtypeStruct((rows, width), BF16)] * 2,
         moved=own_states.size * 2,
     )
 
@@ -470,45 +469,22 @@
     )
 
 
-def begin_rows(kept, landed, weight):
-    slot_rows, depth = landed.shape
-    width = weight.shape[1]
-
-    def kernel(kept_ref, landed_ref, weight_ref, out_ref):
-        far = lax.axis_index("section") >= 2
-        rows = jnp.where(far, landed_ref[...], kept_ref[:, pl.ds(0, depth)])
-        for c in range(0, width, 512):
-            columns = pl.ds(c, 512)
-            out_ref[:, columns] = jnp.dot(rows, weight_ref[pl.ds(0, depth), columns], preferred_element_type=F32)
-
-    return on_chip(
-        kernel,
-        (kept, landed, weight),
-        [VMEM] * 3,
-        [jax.ShapeDtypeStruct((slot_rows, width), F32)],
-        flops=2 * slot_rows * depth * width,
-        moved=2 * weight.size,
-    )[0]
-
-
-def project_rows(begun, kept, landed, weight, steps):
+def project_rows(kept, landed, weight, steps):
     slot_rows, depth = landed.shape
     width = weight.shape[1]
     rows_here = slot_rows // len(steps)
     share_width = width + HD
     step_width = 256
 
-    def kernel(begun_ref, kept_ref, landed_ref, weight_ref, own_ref, *refs):
+    def kernel(kept_ref, landed_ref, weight_ref, own_ref, *refs):
         share_refs, (held, code) = refs[:-2], refs[-2:]
         far = lax.axis_index("section") >= 2
         rank = lax.axis_index("tensor")
-        rows = jnp.where(far, landed_ref[...], kept_ref[:, pl.ds(depth, depth)])
+        rows = jnp.where(far, landed_ref[...], kept_ref[...])
         lane = lax.broadcasted_iota(jnp.int32, (slot_rows, HD), 1)
         levels = jnp.zeros((slot_rows, HD), F32)
         for c in range(0, width, step_width):
-            product = begun_ref[:, c : c + step_width] + jnp.dot(
-                rows, weight_ref[pl.ds(depth, depth), pl.ds(c, step_width)], preferred_element_type=F32
-            )
+            product = jnp.dot(rows, weight_ref[:, pl.ds(c, step_width)], preferred_element_type=F32)
             held[:, c : c + step_width] = product
             for m in range(0, step_width, HD):
                 tile = product[:, m : m + HD]
@@ -529,8 +505,8 @@
 
     return on_chip(
         kernel,
-        (begun, kept, landed, weight),
-        [VMEM] * 4,
+        (kept, landed, weight),
+        [VMEM] * 3,
         [jax.ShapeDtypeStruct((rows_here, width), F32)]
         + [jax.ShapeDtypeStruct((rows_here, share_width), I16)] * (len(steps) - 1),
         [pltpu.VMEM((slot_rows, width), F32), pltpu.VMEM((slot_rows, width + HD), I16)],
@@ -721,13 +697,12 @@
     cosine, sine, states, table, weights, stats, row_queries, values = prepare(
         prompt[0], key_gain, block_owner, block_slot, prompt_blocks, queries, cache_keys, cache_values, decode_lengths
     )
-    kept, *sent = place_rows(states, near_states, table)
-    landed = [swap(half, "section", 3) for half in sent]
+    kept, sent = place_rows(states, near_states, table)
+    landed = swap(sent, "section", 3)
     steps = (0, 3, 2, 1)
     span, *span_codes = span_sums(weights, stats, values, kept, steps)
     span_shares = [swap(code, "tensor", step) for code, step in zip(span_codes, steps[1:])]
-    begun = begin_rows(kept, landed[0], key_value_weight)
-    own, far, near, mid = project_rows(begun, kept, landed[1], key_value_weight, (0, 3, 1, 2))
+    own, far, near, mid = project_rows(kept, landed, key_value_weight, (0, 3, 1, 2))
     far, near = swap(far, "tensor", 3), swap(near, "tensor", 1)
     mid = swap(hand_on(mid, span_shares), "tensor", 2)
     finished = finish_rows(add_shares(own, [far, near]), [mid], cosine, sine)

time: 31.7 us -> 31.3 us (0.987)
    ppermute x9 -> x8, waiting for transfers between devices: 4.66 us -> 4.36 us  [swap(): lax.ppermute(piece, axis, [(i, i ^ step) for i in range(lax.axis_size(axi...]
    pallas_call x10 -> x9, Pallas kernels: 6.37 us -> 6.22 us  [on_chip(): pl.pallas_call(kernel, out_shape=out_shapes, in_specs=in_specs, out_specs...]
    ppermute x9 -> x8, starting transfers between devices: 12.4 us -> 12.4 us  [swap(): lax.ppermute(piece, axis, [(i, i ^ step) for i in range(lax.axis_size(axi...]
  transfers between devices with their start and end apart: 12 -> 11, of which waited for: 5 -> 5; matrix products, arithmetic and copies ran while one was open for 2% -> 2% of each run, Pallas kernels for 16% -> 15%
where the time goes in v8:
time: 31.3 us; the launch traced here: 31.2 us
  starting transfers between devices  17.4 us (56%)
  Pallas kernels  6.22 us (20%)
  waiting for transfers between devices  6.2 us (20%)
  between operations  0.73 us (2%)
  local copies, waits for them, and re-layouts  0.63 us (2%)
    ppermute x8, starting transfers between devices, swap(): lax.ppermute(piece, axis, [(i, i ^ step) for i in range(lax.axis_size(axi...  12.4 us
    pallas_call x9, Pallas kernels, on_chip(): pl.pallas_call(kernel, out_shape=out_shapes, in_specs=in_specs, out_specs...  6.22 us
    ppermute x3, starting transfers between devices, turn(): lax.ppermute(piece, axis, [(i, (i + step) % count) for i in range(count)])  4.97 us
    ppermute x8, waiting for transfers between devices, swap(): lax.ppermute(piece, axis, [(i, i ^ step) for i in range(lax.axis_size(axi...  4.36 us
    ppermute x3, waiting for transfers between devices, turn(): lax.ppermute(piece, axis, [(i, (i + step) % count) for i in range(count)])  1.85 us
    unnamed x7, local copies, waits for them, and re-layouts  0.63 us
  transfers between devices with their start and end apart: 11, of which 5 were waited for; matrix products, arithmetic and copies ran while one was open for 2% of the time, Pallas kernels for 15%

profile of v8, /device:TPU:0, one launch (start us, length us, event | category | flops | bytes accessed | tf_op | source)
XLA Modules:
  0.0 31.2 jit_solution(5913933127421907955)
XLA Ops:
  0.6 0.5 %collective-permute-start = (bf16[256,1280]{1,0:T(8,128)(2,1)}, bf16[256,1280]{1,0:T(8,128)(2,1)S(1)}, u32[]{:S(2)}, u32[]{:S(2)}) collective-permute-start(bf16[256,1280]{1,0:T(8,128)(2,1)} %bitcast.8), channel_id=1, source_target_pairs={{0,4},{4,0},{8,12},{12,8},{1,5},{5,1},{9,13},{13,9},{2,6},{6,2},{1... | collective-permute-start | bytes 1966088 | tf_op jit(solution)/shard_map/ppermute | solution.py:673
  1.2 2.4 %shard_map.131 = (f32[16,128]{1,0:T(8,128)S(1)}, f32[16,128]{1,0:T(8,128)S(1)}, bf16[256,1280]{1,0:T(8,128)(2,1)S(1)}, bf16[128,256]{1,0:T(8,128)(2,1)S(1)}, bf1...) custom-call(s32[16]{0:T(128)} %refs_0_.1, ...), custom_call_target="tpu_custom_call" | custom-call | flops 8388608 | bytes 2752512 | tf_op jit(solution)/shard_map/pallas_call | solution.py:245
  3.6 0.0 copy-start.1
  3.6 0.3 shard_map.132
  3.9 2.8 %collective-permute-start.4 = (bf16[64,1280]{1,0:T(8,128)(2,1)S(1)}, bf16[64,1280]{1,0:T(8,128)(2,1)S(1)}, u32[]{:S(2)}, u32[]{:S(2)}) collective-permute-start(bf16[64,1280]{1,0:T(8,128)(2,1)S(1)} %get-tuple-element.31), channel_id=1, source_target_pairs={{0,12},{4,8},{8,4},{12,0},{1,13},{5,9},{9,5},{13,1},{2,14},{6,10},... | collective-permute-start | bytes 491528 | tf_op jit(solution)/shard_map/ppermute | solution.py:673
  6.7 0.6 %shard_map.133 = (f32[64,640]{1,0:T(8,128)S(1)}, s16[16,640]{1,0:T(8,128)(2,1)S(1)}, s16[16,640]{1,0:T(8,128)(2,1)S(1)}, s16[16,640]{1,0:T(8,128)(2,1)S(1)}) custom-call(bf16[4,64,128]{2,1,0:T(8,128)(2,1)S(1)} %get-tuple-element.20.weight_ref, f32[64,128]{1,0:T(8,128)S(1)} %get-tuple-element.21.stats_ref, ...), custom_call_target="tpu_custom_call" | custom-call | flops 8388608 | bytes 6291456 | tf_op jit(solution)/shard_map/pallas_call | solution.py:245
  7.3 3.7 %collective-permute-start.1 = (s16[16,640]{1,0:T(8,128)(2,1)S(1)}, s16[16,640]{1,0:T(8,128)(2,1)S(1)}, u32[]{:S(2)}, u32[]{:S(2)}) collective-permute-start(s16[16,640]{1,0:T(8,128)(2,1)S(1)} %get-tuple-element.27), channel_id=1, source_target_pairs={{0,3},{1,2},{2,1},{3,0},{4,7},{5,6},{6,5},{7,4},{8,11},{9,10},{10,... | collective-permute-start | bytes 61448 | tf_op jit(solution)/shard_map/ppermute | solution.py:673
  11.0 0.8 %collective-permute-start.3 = (s16[16,640]{1,0:T(8,128)(2,1)S(1)}, s16[16,640]{1,0:T(8,128)(2,1)S(1)}, u32[]{:S(2)}, u32[]{:S(2)}) collective-permute-start(s16[16,640]{1,0:T(8,128)(2,1)S(1)} %get-tuple-element.29), channel_id=1, source_target_pairs={{0,1},{1,0},{2,3},{3,2},{4,5},{5,4},{6,7},{7,6},{8,9},{9,8},{10,11... | collective-permute-start | bytes 61448 | tf_op jit(solution)/shard_map/ppermute | solution.py:673
  11.7 1.2 %shard_map.135 = (f32[16,2048]{1,0:T(8,128)S(1)}, s16[16,2176]{1,0:T(8,128)(2,1)S(1)}, s16[16,2176]{1,0:T(8,128)(2,1)S(1)}, s16[16,2176]{1,0:T(8,128)(2,1)S(1)}) custom-call(bf16[64,1280]{1,0:T(8,128)(2,1)S(1)} %get-tuple-element.25.after_ref.kept_ref, bf16[64,1280]{1,0:T(8,128)(2,1)S(1)} %collective-permute-done.4.landed_ref, bf16[1280,2048]{1,0:T(8,128)(2,1)S(1)} %copy-done), custom_call_target="tpu_custom_call" | custom-call | flops 335544320 | bytes 5242880 | tf_op jit(solution)/shard_map/pallas_call | solution.py:245
  13.0 3.7 %collective-permute-start.5 = (s16[16,2176]{1,0:T(8,128)(2,1)S(1)}, s16[16,2176]{1,0:T(8,128)(2,1)S(1)}, u32[]{:S(2)}, u32[]{:S(2)}) collective-permute-start(s16[16,2176]{1,0:T(8,128)(2,1)S(1)} %get-tuple-element.33), channel_id=1, source_target_pairs={{0,3},{1,2},{2,1},{3,0},{4,7},{5,6},{6,5},{7,4},{8,11},{9,10},{10,... | collective-permute-start | bytes 208904 | tf_op jit(solution)/shard_map/ppermute | solution.py:673
  16.7 1.0 %collective-permute-start.7 = (s16[16,2176]{1,0:T(8,128)(2,1)S(1)}, s16[16,2176]{1,0:T(8,128)(2,1)S(1)}, u32[]{:S(2)}, u32[]{:S(2)}) collective-permute-start(s16[16,2176]{1,0:T(8,128)(2,1)S(1)} %shard_map.137), channel_id=1, source_target_pairs={{0,2},{1,3},{2,0},{3,1},{4,6},{5,7},{6,4},{7,5},{8,10},{9,11},{10,... | collective-permute-start | bytes 208904 | tf_op jit(solution)/shard_map/ppermute | solution.py:673
  17.7 1.9 %collective-permute-done.5.refs_0_ = s16[16,2176]{1,0:T(8,128)(2,1)S(1)} collective-permute-done((s16[16,2176]{1,0:T(8,128)(2,1)S(1)}, s16[16,2176]{1,0:T(8,128)(2,1)S(1)}, u32[]{:S(2)}, u32[]{:S(2)}) %collective-permute-start.5) | collective-permute-done | bytes 69664 | tf_op jit(solution)/shard_map/ppermute | solution.py:673
  19.6 1.9 %collective-permute-done.6.refs_1_ = s16[16,2176]{1,0:T(8,128)(2,1)S(1)} collective-permute-done((s16[16,2176]{1,0:T(8,128)(2,1)S(1)}, s16[16,2176]{1,0:T(8,128)(2,1)S(1)}, u32[]{:S(2)}, u32[]{:S(2)}) %collective-permute-start.6) | collective-permute-done | bytes 69664 | tf_op jit(solution)/shard_map/ppermute | solution.py:673
  21.5 0.2 shard_map.136.own_ref
  21.6 0.5 %collective-permute-done.7.refs_0_ = s16[16,2176]{1,0:T(8,128)(2,1)S(1)} collective-permute-done((s16[16,2176]{1,0:T(8,128)(2,1)S(1)}, s16[16,2176]{1,0:T(8,128)(2,1)S(1)}, u32[]{:S(2)}, u32[]{:S(2)}) %collective-permute-start.7) | collective-permute-done | bytes 69664 | tf_op jit(solution)/shard_map/ppermute | solution.py:673
  22.2 0.4 %shard_map.138.refs_0_ = bf16[16,2048]{1,0:T(8,128)(2,1)S(1)} custom-call(f32[16,2048]{1,0:T(8,128)S(1)} %shard_map.136.own_ref, s16[16,2176]{1,0:T(8,128)(2,1)S(1)} %collective-permute-done.7.refs_0_, f32[16,128]{1,0:T(8,128)S(1)} %get-tuple-element.36.refs_1_, f32[16,128]{1,0:T(8,128)S(1)} %get-tuple-element.37.refs_2_), custom_call_target="tpu_custom_call" | custom-call | tf_op jit(solution)/shard_map/pallas_call | solution.py:245
  22.6 1.8 %collective-permute-start.10 = (bf16[16,2048]{1,0:T(8,128)(2,1)S(1)}, bf16[16,2048]{1,0:T(8,128)(2,1)S(1)}, u32[]{:S(2)}, u32[]{:S(2)}) collective-permute-start(bf16[16,2048]{1,0:T(8,128)(2,1)S(1)} %shard_map.138.refs_0_), channel_id=1, source_target_pairs={{0,1},{1,2},{2,3},{3,0},{4,5},{5,6},{6,7},{7,4},{8,9},{9,10},{10,1... | collective-permute-start | bytes 196616 | tf_op jit(solution)/shard_map/ppermute | solution.py:678
  24.4 0.9 %collective-permute-start.9 = (bf16[16,2048]{1,0:T(8,128)(2,1)S(1)}, bf16[16,2048]{1,0:T(8,128)(2,1)S(1)}, u32[]{:S(2)}, u32[]{:S(2)}) collective-permute-start(bf16[16,2048]{1,0:T(8,128)(2,1)S(1)} %shard_map.138.refs_0_), channel_id=1, source_target_pairs={{0,2},{1,3},{2,0},{3,1},{4,6},{5,7},{6,4},{7,5},{8,10},{9,11},{10,... | collective-permute-start | bytes 196616 | tf_op jit(solution)/shard_map/ppermute | solution.py:678
  25.4 2.2 %collective-permute-start.8 = (bf16[16,2048]{1,0:T(8,128)(2,1)S(1)}, bf16[16,2048]{1,0:T(8,128)(2,1)S(1)}, u32[]{:S(2)}, u32[]{:S(2)}) collective-permute-start(bf16[16,2048]{1,0:T(8,128)(2,1)S(1)} %shard_map.138.refs_0_), channel_id=1, source_target_pairs={{0,3},{1,0},{2,1},{3,2},{4,7},{5,4},{6,5},{7,6},{8,11},{9,8},{10,9... | collective-permute-start | bytes 196616 | tf_op jit(solution)/shard_map/ppermute | solution.py:678
  27.6 0.4 %shard_map.134 = bf16[4,16,128]{2,1,0:T(8,128)(2,1)S(1)} custom-call(f32[64,640]{1,0:T(8,128)S(1)} %get-tuple-element.26.span_ref, s16[16,640]{1,0:T(8,128)(2,1)S(1)} %collective-permute-done.1.refs_0_, s16[16,640]{1,0:T(8,128)(2,1)S(1)} %collective-permute-done.2.refs_1_, s16[16,640]{1,0:T(8,128)(2,1)S(1)} %collective-permute-done.3.refs_2_, ...), custom_call_target="tpu_custom_call" | custom-call | tf_op jit(solution)/shard_map/pallas_call | solution.py:245
  28.0 0.6 %copy.16 = bf16[1,4,16,128]{3,1,2,0:T(4,128)(2,1)} copy(bf16[1,4,16,128]{3,2,1,0:T(8,128)(2,1)S(1)} %bitcast.7) | data formatting | bytes 32768
  28.6 0.5 %collective-permute-done.10.refs_3_ = bf16[16,2048]{1,0:T(8,128)(2,1)S(1)} collective-permute-done((bf16[16,2048]{1,0:T(8,128)(2,1)S(1)}, bf16[16,2048]{1,0:T(8,128)(2,1)S(1)}, u32[]{:S(2)}, u32[]{:S(2)}) %collective-permute-start.10) | collective-permute-done | bytes 65568 | tf_op jit(solution)/shard_map/ppermute | solution.py:678
  29.0 1.4 %collective-permute-done.9.refs_2_ = bf16[16,2048]{1,0:T(8,128)(2,1)S(1)} collective-permute-done((bf16[16,2048]{1,0:T(8,128)(2,1)S(1)}, bf16[16,2048]{1,0:T(8,128)(2,1)S(1)}, u32[]{:S(2)}, u32[]{:S(2)}) %collective-permute-start.9) | collective-permute-done | bytes 65568 | tf_op jit(solution)/shard_map/ppermute | solution.py:678
  30.4 0.7 %shard_map.139 = bf16[64,2048]{1,0:T(8,128)(2,1)} custom-call(bf16[16,2048]{1,0:T(8,128)(2,1)S(1)} %shard_map.138.refs_0_, bf16[16,2048]{1,0:T(8,128)(2,1)S(1)} %collective-permute-done.8.refs_1_, bf16[16,2048]{1,0:T(8,128)(2,1)S(1)} %collective-permute-done.9.refs_2_, bf16[16,2048]{1,0:T(8,128)(2,1)S(1)} %collective-permute-done.10.refs_3_), custom_call_target="tpu_custom_call" | custom-call | tf_op jit(solution)/shard_map/pallas_call | solution.py:245
  (14 shorter events, 0.0 us)
Async XLA Ops:
  0.6 11.1 %copy-start = (bf16[1280,2048]{1,0:T(8,128)(2,1)S(1)}, bf16[1280,2048]{1,0:T(8,128)(2,1)}, u32[]{:S(2)}) copy-start(bf16[1280,2048]{1,0:T(8,128)(2,1)} %weight_ref.1) | copy-start | bytes 15728644
  0.6 3.0 %collective-permute-start = (bf16[256,1280]{1,0:T(8,128)(2,1)}, bf16[256,1280]{1,0:T(8,128)(2,1)S(1)}, u32[]{:S(2)}, u32[]{:S(2)}) collective-permute-start(bf16[256,1280]{1,0:T(8,128)(2,1)} %bitcast.8), channel_id=1, source_target_pairs={{0,4},{4,0},{8,12},{12,8},{1,5},{5,1},{9,13},{13,9},{2,6},{6,2},{1... | collective-permute-start | bytes 1966088 | tf_op jit(solution)/shard_map/ppermute | solution.py:673
  3.6 24.0 %copy-start.1 = (bf16[4,1024]{1,0:T(4,128)(2,1)S(1)}, bf16[4,1024]{1,0:T(4,128)(2,1)}, u32[]{:S(2)}) copy-start(bf16[4,1024]{1,0:T(4,128)(2,1)} %refs_4_.1) | copy-start | bytes 24580
  3.6 24.0 %copy-start.2 = (bf16[4,1024]{1,0:T(4,128)(2,1)S(1)}, bf16[4,1024]{1,0:T(4,128)(2,1)}, u32[]{:S(2)}) copy-start(bf16[4,1024]{1,0:T(4,128)(2,1)} %refs_5_.3) | copy-start | bytes 24580
  3.9 7.8 %collective-permute-start.4 = (bf16[64,1280]{1,0:T(8,128)(2,1)S(1)}, bf16[64,1280]{1,0:T(8,128)(2,1)S(1)}, u32[]{:S(2)}, u32[]{:S(2)}) collective-permute-start(bf16[64,1280]{1,0:T(8,128)(2,1)S(1)} %get-tuple-element.31), channel_id=1, source_target_pairs={{0,12},{4,8},{8,4},{12,0},{1,13},{5,9},{9,5},{13,1},{2,14},{6,10},... | collective-permute-start | bytes 491528 | tf_op jit(solution)/shard_map/ppermute | solution.py:673
  7.3 9.4 %collective-permute-start.1 = (s16[16,640]{1,0:T(8,128)(2,1)S(1)}, s16[16,640]{1,0:T(8,128)(2,1)S(1)}, u32[]{:S(2)}, u32[]{:S(2)}) collective-permute-start(s16[16,640]{1,0:T(8,128)(2,1)S(1)} %get-tuple-element.27), channel_id=1, source_target_pairs={{0,3},{1,2},{2,1},{3,0},{4,7},{5,6},{6,5},{7,4},{8,11},{9,10},{10,... | collective-permute-start | bytes 61448 | tf_op jit(solution)/shard_map/ppermute | solution.py:673
  10.9 5.7 %collective-permute-start.2 = (s16[16,640]{1,0:T(8,128)(2,1)S(1)}, s16[16,640]{1,0:T(8,128)(2,1)S(1)}, u32[]{:S(2)}, u32[]{:S(2)}) collective-permute-start(s16[16,640]{1,0:T(8,128)(2,1)S(1)} %get-tuple-element.28), channel_id=1, source_target_pairs={{0,2},{1,3},{2,0},{3,1},{4,6},{5,7},{6,4},{7,5},{8,10},{9,11},{10,... | collective-permute-start | bytes 61448 | tf_op jit(solution)/shard_map/ppermute | solution.py:673
  11.0 5.7 %collective-permute-start.3 = (s16[16,640]{1,0:T(8,128)(2,1)S(1)}, s16[16,640]{1,0:T(8,128)(2,1)S(1)}, u32[]{:S(2)}, u32[]{:S(2)}) collective-permute-start(s16[16,640]{1,0:T(8,128)(2,1)S(1)} %get-tuple-element.29), channel_id=1, source_target_pairs={{0,1},{1,0},{2,3},{3,2},{4,5},{5,4},{6,7},{7,6},{8,9},{9,8},{10,11... | collective-permute-start | bytes 61448 | tf_op jit(solution)/shard_map/ppermute | solution.py:673
  13.0 6.6 %collective-permute-start.5 = (s16[16,2176]{1,0:T(8,128)(2,1)S(1)}, s16[16,2176]{1,0:T(8,128)(2,1)S(1)}, u32[]{:S(2)}, u32[]{:S(2)}) collective-permute-start(s16[16,2176]{1,0:T(8,128)(2,1)S(1)} %get-tuple-element.33), channel_id=1, source_target_pairs={{0,3},{1,2},{2,1},{3,0},{4,7},{5,6},{6,5},{7,4},{8,11},{9,10},{10,... | collective-permute-start | bytes 208904 | tf_op jit(solution)/shard_map/ppermute | solution.py:673
  16.6 4.8 %collective-permute-start.6 = (s16[16,2176]{1,0:T(8,128)(2,1)S(1)}, s16[16,2176]{1,0:T(8,128)(2,1)S(1)}, u32[]{:S(2)}, u32[]{:S(2)}) collective-permute-start(s16[16,2176]{1,0:T(8,128)(2,1)S(1)} %get-tuple-element.34), channel_id=1, source_target_pairs={{0,1},{1,0},{2,3},{3,2},{4,5},{5,4},{6,7},{7,6},{8,9},{9,8},{10,11... | collective-permute-start | bytes 208904 | tf_op jit(solution)/shard_map/ppermute | solution.py:673
  16.7 5.5 %collective-permute-start.7 = (s16[16,2176]{1,0:T(8,128)(2,1)S(1)}, s16[16,2176]{1,0:T(8,128)(2,1)S(1)}, u32[]{:S(2)}, u32[]{:S(2)}) collective-permute-start(s16[16,2176]{1,0:T(8,128)(2,1)S(1)} %shard_map.137), channel_id=1, source_target_pairs={{0,2},{1,3},{2,0},{3,1},{4,6},{5,7},{6,4},{7,5},{8,10},{9,11},{10,... | collective-permute-start | bytes 208904 | tf_op jit(solution)/shard_map/ppermute | solution.py:673
  22.6 6.4 %collective-permute-start.10 = (bf16[16,2048]{1,0:T(8,128)(2,1)S(1)}, bf16[16,2048]{1,0:T(8,128)(2,1)S(1)}, u32[]{:S(2)}, u32[]{:S(2)}) collective-permute-start(bf16[16,2048]{1,0:T(8,128)(2,1)S(1)} %shard_map.138.refs_0_), channel_id=1, source_target_pairs={{0,1},{1,2},{2,3},{3,0},{4,5},{5,6},{6,7},{7,4},{8,9},{9,10},{10,1... | collective-permute-start | bytes 196616 | tf_op jit(solution)/shard_map/ppermute | solution.py:678
  24.4 6.0 %collective-permute-start.9 = (bf16[16,2048]{1,0:T(8,128)(2,1)S(1)}, bf16[16,2048]{1,0:T(8,128)(2,1)S(1)}, u32[]{:S(2)}, u32[]{:S(2)}) collective-permute-start(bf16[16,2048]{1,0:T(8,128)(2,1)S(1)} %shard_map.138.refs_0_), channel_id=1, source_target_pairs={{0,2},{1,3},{2,0},{3,1},{4,6},{5,7},{6,4},{7,5},{8,10},{9,11},{10,... | collective-permute-start | bytes 196616 | tf_op jit(solution)/shard_map/ppermute | solution.py:678
  25.4 5.1 %collective-permute-start.8 = (bf16[16,2048]{1,0:T(8,128)(2,1)S(1)}, bf16[16,2048]{1,0:T(8,128)(2,1)S(1)}, u32[]{:S(2)}, u32[]{:S(2)}) collective-permute-start(bf16[16,2048]{1,0:T(8,128)(2,1)S(1)} %shard_map.138.refs_0_), channel_id=1, source_target_pairs={{0,3},{1,0},{2,1},{3,2},{4,7},{5,4},{6,5},{7,6},{8,11},{9,8},{10,9... | collective-permute-start | bytes 196616 | tf_op jit(solution)/shard_map/ppermute | solution.py:678

commit v9 on v8

--- a/solution.py
+++ b/solution.py
@@ -284,7 +284,7 @@
         sources, states_hbm, value_hbm = refs[:count], refs[count], refs[count + 1]
         outs, rest = refs[count + 2 : count + 10], refs[count + 10 :]
         cosine_ref, sine_ref, states_ref, table_ref, weight_ref, stats_ref, query_ref, value_ref = outs
-        held, (source, scores, sems) = rest[:count], rest[count:]
+        held, (source, sems) = rest[:count], rest[count:]
         owner, slot, prompts, length, gain, packed, keys = held
         pairs = [*zip(sources, held), (states_hbm, states_ref), (value_hbm, value_ref)]
         copies = [pltpu.make_async_copy(s, d, sems.at[i]) for i, (s, d) in enumerate(pairs)]
@@ -336,7 +336,11 @@
             piece = packed[:, pl.ds(h * HD, HD)].astype(F32)
             query_ref[pl.ds(h, row_count, stride=H), :] = piece
         copies[6].wait()
+        place = lax.broadcasted_iota(jnp.int32, (H, local_len), 1) + rank * local_len
+        column = lax.broadcasted_iota(jnp.int32, (H, HD), 1)
+        stats = jnp.zeros((H, HD), F32)
         for r in range(row_count):
+            parts = []
             for pair in range(KVH // 2):
                 pair_queries = query_ref[pl.ds(r * H + pair * 2 * G, 2 * G), :].astype(BF16)
                 for n in (2 * pair, 2 * pair + 1):
@@ -346,13 +350,9 @@
                         (((1,), (1,)), ((), ())),
                         preferred_element_type=F32,
                     )
-                    scores[r, pl.ds(n * G, G), :] = both[(n % 2) * G : (n % 2 + 1) * G]
-        place = lax.broadcasted_iota(jnp.int32, (H, local_len), 1) + rank * local_len
-        column = lax.broadcasted_iota(jnp.int32, (H, HD), 1)
-        stats = jnp.zeros((H, HD), F32)
-        for r in range(row_count):
+                    parts.append(both[(n % 2) * G : (n % 2 + 1) * G])
             live = place < length[r]
-            row_scores = jnp.where(live, scores[r] * HD ** (-0.5), MASKED_SCORE)
+            row_scores = jnp.where(live, jnp.concatenate(parts, axis=0) * HD ** (-0.5), MASKED_SCORE)
             peak = jnp.max(row_scores, axis=1, keepdims=True)
             weight = jnp.where(live, jnp.exp(row_scores - peak), 0.0)
             total = jnp.sum(weight, axis=1, keepdims=True)
@@ -381,7 +381,6 @@
         + [pltpu.VMEM(array.shape, array.dtype) for array in fetched[4:]]
         + [
             pltpu.SMEM((2 * CAP,), jnp.int32),
-            pltpu.VMEM((row_count, H, local_len), F32),
             pltpu.SemaphoreType.DMA((count + 2,)),
         ],
         flops=2 * row_count * H * HD * local_len,

time: 31.3 us -> 31.3 us (level)
  no operation moved by 1% of the time
where the time goes in v9:
time: 31.3 us; the launch traced here: 31.2 us
  starting transfers between devices  17.4 us (56%)
  Pallas kernels  6.22 us (20%)
  waiting for transfers between devices  6.2 us (20%)
  between operations  0.73 us (2%)
  local copies, waits for them, and re-layouts  0.63 us (2%)
    ppermute x8, starting transfers between devices, swap(): lax.ppermute(piece, axis, [(i, i ^ step) for i in range(lax.axis_size(axi...  12.4 us
    pallas_call x9, Pallas kernels, on_chip(): pl.pallas_call(kernel, out_shape=out_shapes, in_specs=in_specs, out_specs...  6.22 us
    ppermute x3, starting transfers between devices, turn(): lax.ppermute(piece, axis, [(i, (i + step) % count) for i in range(count)])  4.97 us
    ppermute x8, waiting for transfers between devices, swap(): lax.ppermute(piece, axis, [(i, i ^ step) for i in range(lax.axis_size(axi...  4.36 us
    ppermute x3, waiting for transfers between devices, turn(): lax.ppermute(piece, axis, [(i, (i + step) % count) for i in range(count)])  1.85 us
    unnamed x7, local copies, waits for them, and re-layouts  0.63 us
  transfers between devices with their start and end apart: 11, of which 5 were waited for; matrix products, arithmetic and copies ran while one was open for 2% of the time, Pallas kernels for 15%

profile of v9, /device:TPU:0, one launch (start us, length us, event | category | flops | bytes accessed | tf_op | source)
XLA Modules:
  0.0 31.2 jit_solution(5913933127421907955)
XLA Ops:
  0.6 0.5 %collective-permute-start = (bf16[256,1280]{1,0:T(8,128)(2,1)}, bf16[256,1280]{1,0:T(8,128)(2,1)S(1)}, u32[]{:S(2)}, u32[]{:S(2)}) collective-permute-start(bf16[256,1280]{1,0:T(8,128)(2,1)} %bitcast.8), channel_id=1, source_target_pairs={{0,4},{4,0},{8,12},{12,8},{1,5},{5,1},{9,13},{13,9},{2,6},{6,2},{1... | collective-permute-start | bytes 1966088 | tf_op jit(solution)/shard_map/ppermute | solution.py:672
  1.2 2.4 %shard_map.131 = (f32[16,128]{1,0:T(8,128)S(1)}, f32[16,128]{1,0:T(8,128)S(1)}, bf16[256,1280]{1,0:T(8,128)(2,1)S(1)}, bf16[128,256]{1,0:T(8,128)(2,1)S(1)}, bf1...) custom-call(s32[16]{0:T(128)} %refs_0_.1, ...), custom_call_target="tpu_custom_call" | custom-call | flops 8388608 | bytes 2752512 | tf_op jit(solution)/shard_map/pallas_call | solution.py:245
  3.6 0.0 copy-start.1
  3.6 0.3 shard_map.132
  3.9 2.8 %collective-permute-start.4 = (bf16[64,1280]{1,0:T(8,128)(2,1)S(1)}, bf16[64,1280]{1,0:T(8,128)(2,1)S(1)}, u32[]{:S(2)}, u32[]{:S(2)}) collective-permute-start(bf16[64,1280]{1,0:T(8,128)(2,1)S(1)} %get-tuple-element.31), channel_id=1, source_target_pairs={{0,12},{4,8},{8,4},{12,0},{1,13},{5,9},{9,5},{13,1},{2,14},{6,10},... | collective-permute-start | bytes 491528 | tf_op jit(solution)/shard_map/ppermute | solution.py:672
  6.7 0.6 %shard_map.133 = (f32[64,640]{1,0:T(8,128)S(1)}, s16[16,640]{1,0:T(8,128)(2,1)S(1)}, s16[16,640]{1,0:T(8,128)(2,1)S(1)}, s16[16,640]{1,0:T(8,128)(2,1)S(1)}) custom-call(bf16[4,64,128]{2,1,0:T(8,128)(2,1)S(1)} %get-tuple-element.20.weight_ref, f32[64,128]{1,0:T(8,128)S(1)} %get-tuple-element.21.stats_ref, ...), custom_call_target="tpu_custom_call" | custom-call | flops 8388608 | bytes 6291456 | tf_op jit(solution)/shard_map/pallas_call | solution.py:245
  7.3 3.7 %collective-permute-start.1 = (s16[16,640]{1,0:T(8,128)(2,1)S(1)}, s16[16,640]{1,0:T(8,128)(2,1)S(1)}, u32[]{:S(2)}, u32[]{:S(2)}) collective-permute-start(s16[16,640]{1,0:T(8,128)(2,1)S(1)} %get-tuple-element.27), channel_id=1, source_target_pairs={{0,3},{1,2},{2,1},{3,0},{4,7},{5,6},{6,5},{7,4},{8,11},{9,10},{10,... | collective-permute-start | bytes 61448 | tf_op jit(solution)/shard_map/ppermute | solution.py:672
  11.0 0.8 %collective-permute-start.3 = (s16[16,640]{1,0:T(8,128)(2,1)S(1)}, s16[16,640]{1,0:T(8,128)(2,1)S(1)}, u32[]{:S(2)}, u32[]{:S(2)}) collective-permute-start(s16[16,640]{1,0:T(8,128)(2,1)S(1)} %get-tuple-element.29), channel_id=1, source_target_pairs={{0,1},{1,0},{2,3},{3,2},{4,5},{5,4},{6,7},{7,6},{8,9},{9,8},{10,11... | collective-permute-start | bytes 61448 | tf_op jit(solution)/shard_map/ppermute | solution.py:672
  11.7 1.2 %shard_map.135 = (f32[16,2048]{1,0:T(8,128)S(1)}, s16[16,2176]{1,0:T(8,128)(2,1)S(1)}, s16[16,2176]{1,0:T(8,128)(2,1)S(1)}, s16[16,2176]{1,0:T(8,128)(2,1)S(1)}) custom-call(bf16[64,1280]{1,0:T(8,128)(2,1)S(1)} %get-tuple-element.25.after_ref.kept_ref, bf16[64,1280]{1,0:T(8,128)(2,1)S(1)} %collective-permute-done.4.landed_ref, bf16[1280,2048]{1,0:T(8,128)(2,1)S(1)} %copy-done), custom_call_target="tpu_custom_call" | custom-call | flops 335544320 | bytes 5242880 | tf_op jit(solution)/shard_map/pallas_call | solution.py:245
  13.0 3.7 %collective-permute-start.5 = (s16[16,2176]{1,0:T(8,128)(2,1)S(1)}, s16[16,2176]{1,0:T(8,128)(2,1)S(1)}, u32[]{:S(2)}, u32[]{:S(2)}) collective-permute-start(s16[16,2176]{1,0:T(8,128)(2,1)S(1)} %get-tuple-element.33), channel_id=1, source_target_pairs={{0,3},{1,2},{2,1},{3,0},{4,7},{5,6},{6,5},{7,4},{8,11},{9,10},{10,... | collective-permute-start | bytes 208904 | tf_op jit(solution)/shard_map/ppermute | solution.py:672
  16.7 1.0 %collective-permute-start.7 = (s16[16,2176]{1,0:T(8,128)(2,1)S(1)}, s16[16,2176]{1,0:T(8,128)(2,1)S(1)}, u32[]{:S(2)}, u32[]{:S(2)}) collective-permute-start(s16[16,2176]{1,0:T(8,128)(2,1)S(1)} %shard_map.137), channel_id=1, source_target_pairs={{0,2},{1,3},{2,0},{3,1},{4,6},{5,7},{6,4},{7,5},{8,10},{9,11},{10,... | collective-permute-start | bytes 208904 | tf_op jit(solution)/shard_map/ppermute | solution.py:672
  17.7 1.9 %collective-permute-done.5.refs_0_ = s16[16,2176]{1,0:T(8,128)(2,1)S(1)} collective-permute-done((s16[16,2176]{1,0:T(8,128)(2,1)S(1)}, s16[16,2176]{1,0:T(8,128)(2,1)S(1)}, u32[]{:S(2)}, u32[]{:S(2)}) %collective-permute-start.5) | collective-permute-done | bytes 69664 | tf_op jit(solution)/shard_map/ppermute | solution.py:672
  19.6 1.9 %collective-permute-done.6.refs_1_ = s16[16,2176]{1,0:T(8,128)(2,1)S(1)} collective-permute-done((s16[16,2176]{1,0:T(8,128)(2,1)S(1)}, s16[16,2176]{1,0:T(8,128)(2,1)S(1)}, u32[]{:S(2)}, u32[]{:S(2)}) %collective-permute-start.6) | collective-permute-done | bytes 69664 | tf_op jit(solution)/shard_map/ppermute | solution.py:672
  21.5 0.2 shard_map.136.own_ref
  21.6 0.5 %collective-permute-done.7.refs_0_ = s16[16,2176]{1,0:T(8,128)(2,1)S(1)} collective-permute-done((s16[16,2176]{1,0:T(8,128)(2,1)S(1)}, s16[16,2176]{1,0:T(8,128)(2,1)S(1)}, u32[]{:S(2)}, u32[]{:S(2)}) %collective-permute-start.7) | collective-permute-done | bytes 69664 | tf_op jit(solution)/shard_map/ppermute | solution.py:672
  22.2 0.4 %shard_map.138.refs_0_ = bf16[16,2048]{1,0:T(8,128)(2,1)S(1)} custom-call(f32[16,2048]{1,0:T(8,128)S(1)} %shard_map.136.own_ref, s16[16,2176]{1,0:T(8,128)(2,1)S(1)} %collective-permute-done.7.refs_0_, f32[16,128]{1,0:T(8,128)S(1)} %get-tuple-element.36.refs_1_, f32[16,128]{1,0:T(8,128)S(1)} %get-tuple-element.37.refs_2_), custom_call_target="tpu_custom_call" | custom-call | tf_op jit(solution)/shard_map/pallas_call | solution.py:245
  22.6 1.8 %collective-permute-start.10 = (bf16[16,2048]{1,0:T(8,128)(2,1)S(1)}, bf16[16,2048]{1,0:T(8,128)(2,1)S(1)}, u32[]{:S(2)}, u32[]{:S(2)}) collective-permute-start(bf16[16,2048]{1,0:T(8,128)(2,1)S(1)} %shard_map.138.refs_0_), channel_id=1, source_target_pairs={{0,1},{1,2},{2,3},{3,0},{4,5},{5,6},{6,7},{7,4},{8,9},{9,10},{10,1... | collective-permute-start | bytes 196616 | tf_op jit(solution)/shard_map/ppermute | solution.py:677
  24.4 0.9 %collective-permute-start.9 = (bf16[16,2048]{1,0:T(8,128)(2,1)S(1)}, bf16[16,2048]{1,0:T(8,128)(2,1)S(1)}, u32[]{:S(2)}, u32[]{:S(2)}) collective-permute-start(bf16[16,2048]{1,0:T(8,128)(2,1)S(1)} %shard_map.138.refs_0_), channel_id=1, source_target_pairs={{0,2},{1,3},{2,0},{3,1},{4,6},{5,7},{6,4},{7,5},{8,10},{9,11},{10,... | collective-permute-start | bytes 196616 | tf_op jit(solution)/shard_map/ppermute | solution.py:677
  25.4 2.2 %collective-permute-start.8 = (bf16[16,2048]{1,0:T(8,128)(2,1)S(1)}, bf16[16,2048]{1,0:T(8,128)(2,1)S(1)}, u32[]{:S(2)}, u32[]{:S(2)}) collective-permute-start(bf16[16,2048]{1,0:T(8,128)(2,1)S(1)} %shard_map.138.refs_0_), channel_id=1, source_target_pairs={{0,3},{1,0},{2,1},{3,2},{4,7},{5,4},{6,5},{7,6},{8,11},{9,8},{10,9... | collective-permute-start | bytes 196616 | tf_op jit(solution)/shard_map/ppermute | solution.py:677
  27.6 0.4 %shard_map.134 = bf16[4,16,128]{2,1,0:T(8,128)(2,1)S(1)} custom-call(f32[64,640]{1,0:T(8,128)S(1)} %get-tuple-element.26.span_ref, s16[16,640]{1,0:T(8,128)(2,1)S(1)} %collective-permute-done.1.refs_0_, s16[16,640]{1,0:T(8,128)(2,1)S(1)} %collective-permute-done.2.refs_1_, s16[16,640]{1,0:T(8,128)(2,1)S(1)} %collective-permute-done.3.refs_2_, ...), custom_call_target="tpu_custom_call" | custom-call | tf_op jit(solution)/shard_map/pallas_call | solution.py:245
  28.0 0.6 %copy.16 = bf16[1,4,16,128]{3,1,2,0:T(4,128)(2,1)} copy(bf16[1,4,16,128]{3,2,1,0:T(8,128)(2,1)S(1)} %bitcast.7) | data formatting | bytes 32768
  28.6 0.5 %collective-permute-done.10.refs_3_ = bf16[16,2048]{1,0:T(8,128)(2,1)S(1)} collective-permute-done((bf16[16,2048]{1,0:T(8,128)(2,1)S(1)}, bf16[16,2048]{1,0:T(8,128)(2,1)S(1)}, u32[]{:S(2)}, u32[]{:S(2)}) %collective-permute-start.10) | collective-permute-done | bytes 65568 | tf_op jit(solution)/shard_map/ppermute | solution.py:677
  29.0 1.4 %collective-permute-done.9.refs_2_ = bf16[16,2048]{1,0:T(8,128)(2,1)S(1)} collective-permute-done((bf16[16,2048]{1,0:T(8,128)(2,1)S(1)}, bf16[16,2048]{1,0:T(8,128)(2,1)S(1)}, u32[]{:S(2)}, u32[]{:S(2)}) %collective-permute-start.9) | collective-permute-done | bytes 65568 | tf_op jit(solution)/shard_map/ppermute | solution.py:677
  30.4 0.7 %shard_map.139 = bf16[64,2048]{1,0:T(8,128)(2,1)} custom-call(bf16[16,2048]{1,0:T(8,128)(2,1)S(1)} %shard_map.138.refs_0_, bf16[16,2048]{1,0:T(8,128)(2,1)S(1)} %collective-permute-done.8.refs_1_, bf16[16,2048]{1,0:T(8,128)(2,1)S(1)} %collective-permute-done.9.refs_2_, bf16[16,2048]{1,0:T(8,128)(2,1)S(1)} %collective-permute-done.10.refs_3_), custom_call_target="tpu_custom_call" | custom-call | tf_op jit(solution)/shard_map/pallas_call | solution.py:245
  (14 shorter events, 0.0 us)
Async XLA Ops:
  0.6 11.1 %copy-start = (bf16[1280,2048]{1,0:T(8,128)(2,1)S(1)}, bf16[1280,2048]{1,0:T(8,128)(2,1)}, u32[]{:S(2)}) copy-start(bf16[1280,2048]{1,0:T(8,128)(2,1)} %weight_ref.1) | copy-start | bytes 15728644
  0.6 3.0 %collective-permute-start = (bf16[256,1280]{1,0:T(8,128)(2,1)}, bf16[256,1280]{1,0:T(8,128)(2,1)S(1)}, u32[]{:S(2)}, u32[]{:S(2)}) collective-permute-start(bf16[256,1280]{1,0:T(8,128)(2,1)} %bitcast.8), channel_id=1, source_target_pairs={{0,4},{4,0},{8,12},{12,8},{1,5},{5,1},{9,13},{13,9},{2,6},{6,2},{1... | collective-permute-start | bytes 1966088 | tf_op jit(solution)/shard_map/ppermute | solution.py:672
  3.6 24.0 %copy-start.1 = (bf16[4,1024]{1,0:T(4,128)(2,1)S(1)}, bf16[4,1024]{1,0:T(4,128)(2,1)}, u32[]{:S(2)}) copy-start(bf16[4,1024]{1,0:T(4,128)(2,1)} %refs_4_.1) | copy-start | bytes 24580
  3.6 24.0 %copy-start.2 = (bf16[4,1024]{1,0:T(4,128)(2,1)S(1)}, bf16[4,1024]{1,0:T(4,128)(2,1)}, u32[]{:S(2)}) copy-start(bf16[4,1024]{1,0:T(4,128)(2,1)} %refs_5_.3) | copy-start | bytes 24580
  3.9 7.8 %collective-permute-start.4 = (bf16[64,1280]{1,0:T(8,128)(2,1)S(1)}, bf16[64,1280]{1,0:T(8,128)(2,1)S(1)}, u32[]{:S(2)}, u32[]{:S(2)}) collective-permute-start(bf16[64,1280]{1,0:T(8,128)(2,1)S(1)} %get-tuple-element.31), channel_id=1, source_target_pairs={{0,12},{4,8},{8,4},{12,0},{1,13},{5,9},{9,5},{13,1},{2,14},{6,10},... | collective-permute-start | bytes 491528 | tf_op jit(solution)/shard_map/ppermute | solution.py:672
  7.3 9.4 %collective-permute-start.1 = (s16[16,640]{1,0:T(8,128)(2,1)S(1)}, s16[16,640]{1,0:T(8,128)(2,1)S(1)}, u32[]{:S(2)}, u32[]{:S(2)}) collective-permute-start(s16[16,640]{1,0:T(8,128)(2,1)S(1)} %get-tuple-element.27), channel_id=1, source_target_pairs={{0,3},{1,2},{2,1},{3,0},{4,7},{5,6},{6,5},{7,4},{8,11},{9,10},{10,... | collective-permute-start | bytes 61448 | tf_op jit(solution)/shard_map/ppermute | solution.py:672
  10.9 5.7 %collective-permute-start.2 = (s16[16,640]{1,0:T(8,128)(2,1)S(1)}, s16[16,640]{1,0:T(8,128)(2,1)S(1)}, u32[]{:S(2)}, u32[]{:S(2)}) collective-permute-start(s16[16,640]{1,0:T(8,128)(2,1)S(1)} %get-tuple-element.28), channel_id=1, source_target_pairs={{0,2},{1,3},{2,0},{3,1},{4,6},{5,7},{6,4},{7,5},{8,10},{9,11},{10,... | collective-permute-start | bytes 61448 | tf_op jit(solution)/shard_map/ppermute | solution.py:672
  11.0 5.7 %collective-permute-start.3 = (s16[16,640]{1,0:T(8,128)(2,1)S(1)}, s16[16,640]{1,0:T(8,128)(2,1)S(1)}, u32[]{:S(2)}, u32[]{:S(2)}) collective-permute-start(s16[16,640]{1,0:T(8,128)(2,1)S(1)} %get-tuple-element.29), channel_id=1, source_target_pairs={{0,1},{1,0},{2,3},{3,2},{4,5},{5,4},{6,7},{7,6},{8,9},{9,8},{10,11... | collective-permute-start | bytes 61448 | tf_op jit(solution)/shard_map/ppermute | solution.py:672
  13.0 6.6 %collective-permute-start.5 = (s16[16,2176]{1,0:T(8,128)(2,1)S(1)}, s16[16,2176]{1,0:T(8,128)(2,1)S(1)}, u32[]{:S(2)}, u32[]{:S(2)}) collective-permute-start(s16[16,2176]{1,0:T(8,128)(2,1)S(1)} %get-tuple-element.33), channel_id=1, source_target_pairs={{0,3},{1,2},{2,1},{3,0},{4,7},{5,6},{6,5},{7,4},{8,11},{9,10},{10,... | collective-permute-start | bytes 208904 | tf_op jit(solution)/shard_map/ppermute | solution.py:672
  16.6 4.8 %collective-permute-start.6 = (s16[16,2176]{1,0:T(8,128)(2,1)S(1)}, s16[16,2176]{1,0:T(8,128)(2,1)S(1)}, u32[]{:S(2)}, u32[]{:S(2)}) collective-permute-start(s16[16,2176]{1,0:T(8,128)(2,1)S(1)} %get-tuple-element.34), channel_id=1, source_target_pairs={{0,1},{1,0},{2,3},{3,2},{4,5},{5,4},{6,7},{7,6},{8,9},{9,8},{10,11... | collective-permute-start | bytes 208904 | tf_op jit(solution)/shard_map/ppermute | solution.py:672
  16.7 5.5 %collective-permute-start.7 = (s16[16,2176]{1,0:T(8,128)(2,1)S(1)}, s16[16,2176]{1,0:T(8,128)(2,1)S(1)}, u32[]{:S(2)}, u32[]{:S(2)}) collective-permute-start(s16[16,2176]{1,0:T(8,128)(2,1)S(1)} %shard_map.137), channel_id=1, source_target_pairs={{0,2},{1,3},{2,0},{3,1},{4,6},{5,7},{6,4},{7,5},{8,10},{9,11},{10,... | collective-permute-start | bytes 208904 | tf_op jit(solution)/shard_map/ppermute | solution.py:672
  22.6 6.4 %collective-permute-start.10 = (bf16[16,2048]{1,0:T(8,128)(2,1)S(1)}, bf16[16,2048]{1,0:T(8,128)(2,1)S(1)}, u32[]{:S(2)}, u32[]{:S(2)}) collective-permute-start(bf16[16,2048]{1,0:T(8,128)(2,1)S(1)} %shard_map.138.refs_0_), channel_id=1, source_target_pairs={{0,1},{1,2},{2,3},{3,0},{4,5},{5,6},{6,7},{7,4},{8,9},{9,10},{10,1... | collective-permute-start | bytes 196616 | tf_op jit(solution)/shard_map/ppermute | solution.py:677
  24.4 6.0 %collective-permute-start.9 = (bf16[16,2048]{1,0:T(8,128)(2,1)S(1)}, bf16[16,2048]{1,0:T(8,128)(2,1)S(1)}, u32[]{:S(2)}, u32[]{:S(2)}) collective-permute-start(bf16[16,2048]{1,0:T(8,128)(2,1)S(1)} %shard_map.138.refs_0_), channel_id=1, source_target_pairs={{0,2},{1,3},{2,0},{3,1},{4,6},{5,7},{6,4},{7,5},{8,10},{9,11},{10,... | collective-permute-start | bytes 196616 | tf_op jit(solution)/shard_map/ppermute | solution.py:677
  25.4 5.1 %collective-permute-start.8 = (bf16[16,2048]{1,0:T(8,128)(2,1)S(1)}, bf16[16,2048]{1,0:T(8,128)(2,1)S(1)}, u32[]{:S(2)}, u32[]{:S(2)}) collective-permute-start(bf16[16,2048]{1,0:T(8,128)(2,1)S(1)} %shard_map.138.refs_0_), channel_id=1, source_target_pairs={{0,3},{1,0},{2,1},{3,2},{4,7},{5,4},{6,5},{7,6},{8,11},{9,8},{10,9... | collective-permute-start | bytes 196616 | tf_op jit(solution)/shard_map/ppermute | solution.py:677

commit v10 on v9

--- a/solution.py
+++ b/solution.py
@@ -651,7 +651,7 @@
         rank = lax.axis_index("tensor")
         copies = []
         for step in range(count):
-            place = pl.ds(pl.multiple_of(lax.rem(rank + count - steps[step], count) * rows, rows), rows)
+            place = pl.ds(pl.multiple_of((rank ^ steps[step]) * rows, rows), rows)
             copies.append(pltpu.make_async_copy(piece_refs[step], out_hbm.at[place], sems.at[step]))
         for copy in copies:
             copy.start()
@@ -705,7 +705,8 @@
     far, near = swap(far, "tensor", 3), swap(near, "tensor", 1)
     mid = swap(hand_on(mid, span_shares), "tensor", 2)
     finished = finish_rows(add_shares(own, [far, near]), [mid], cosine, sine)
-    pieces = [finished] + [turn(finished, "tensor", step) for step in steps[1:]]
+    steps = (0, 2, 1, 3)
+    pieces = [finished] + [swap(finished, "tensor", step) for step in steps[1:]]
     block_pool = join_rows(pieces, steps)
     attended = merge_spans(span, span_shares, row_queries, new_keys, new_values)
     return (attended, block_pool.reshape(1, CAP, BLK, -1))

time: 31.3 us -> 31.3 us (level)
  starting transfers between devices: 17.4 us -> 16.8 us
  waiting for transfers between devices: 6.2 us -> 6.7 us
    ppermute x3 -> x0, starting transfers between devices: 4.97 us -> none  [turn(): lax.ppermute(piece, axis, [(i, (i + step) % count) for i in range(count)])]
    ppermute x8 -> x11, starting transfers between devices: 12.4 us -> 16.8 us  [swap(): lax.ppermute(piece, axis, [(i, i ^ step) for i in range(lax.axis_size(axi...]
    ppermute x8 -> x11, waiting for transfers between devices: 4.36 us -> 6.7 us  [swap(): lax.ppermute(piece, axis, [(i, i ^ step) for i in range(lax.axis_size(axi...]
    ppermute x3 -> x0, waiting for transfers between devices: 1.85 us -> none  [turn(): lax.ppermute(piece, axis, [(i, (i + step) % count) for i in range(count)])]
  transfers between devices with their start and end apart: 11 -> 11, of which waited for: 5 -> 6; matrix products, arithmetic and copies ran while one was open for 2% -> 2% of each run, Pallas kernels for 15% -> 15%
where the time goes in v10:
time: 31.3 us; the launch traced here: 31.1 us
  starting transfers between devices  16.8 us (54%)
  waiting for transfers between devices  6.7 us (21%)
  Pallas kernels  6.22 us (20%)
  between operations  0.73 us (2%)
  local copies, waits for them, and re-layouts  0.63 us (2%)
    ppermute x11, starting transfers between devices, swap(): lax.ppermute(piece, axis, [(i, i ^ step) for i in range(lax.axis_size(axi...  16.8 us
    ppermute x11, waiting for transfers between devices, swap(): lax.ppermute(piece, axis, [(i, i ^ step) for i in range(lax.axis_size(axi...  6.7 us
    pallas_call x9, Pallas kernels, on_chip(): pl.pallas_call(kernel, out_shape=out_shapes, in_specs=in_specs, out_specs...  6.22 us
    unnamed x7, local copies, waits for them, and re-layouts  0.63 us
  transfers between devices with their start and end apart: 11, of which 6 were waited for; matrix products, arithmetic and copies ran while one was open for 2% of the time, Pallas kernels for 15%

profile of v10, /device:TPU:0, one launch (start us, length us, event | category | flops | bytes accessed | tf_op | source)
XLA Modules:
  0.0 31.1 jit_solution(8530154058762892802)
XLA Ops:
  0.6 0.5 %collective-permute-start = (bf16[256,1280]{1,0:T(8,128)(2,1)}, bf16[256,1280]{1,0:T(8,128)(2,1)S(1)}, u32[]{:S(2)}, u32[]{:S(2)}) collective-permute-start(bf16[256,1280]{1,0:T(8,128)(2,1)} %bitcast.8), channel_id=1, source_target_pairs={{0,4},{4,0},{8,12},{12,8},{1,5},{5,1},{9,13},{13,9},{2,6},{6,2},{1... | collective-permute-start | bytes 1966088 | tf_op jit(solution)/shard_map/ppermute | solution.py:672
  1.2 2.4 %shard_map.131 = (f32[16,128]{1,0:T(8,128)S(1)}, f32[16,128]{1,0:T(8,128)S(1)}, bf16[256,1280]{1,0:T(8,128)(2,1)S(1)}, bf16[128,256]{1,0:T(8,128)(2,1)S(1)}, bf1...) custom-call(s32[16]{0:T(128)} %refs_0_.1, ...), custom_call_target="tpu_custom_call" | custom-call | flops 8388608 | bytes 2752512 | tf_op jit(solution)/shard_map/pallas_call | solution.py:245
  3.6 0.3 shard_map.132
  3.9 2.8 %collective-permute-start.4 = (bf16[64,1280]{1,0:T(8,128)(2,1)S(1)}, bf16[64,1280]{1,0:T(8,128)(2,1)S(1)}, u32[]{:S(2)}, u32[]{:S(2)}) collective-permute-start(bf16[64,1280]{1,0:T(8,128)(2,1)S(1)} %get-tuple-element.31), channel_id=1, source_target_pairs={{0,12},{4,8},{8,4},{12,0},{1,13},{5,9},{9,5},{13,1},{2,14},{6,10},... | collective-permute-start | bytes 491528 | tf_op jit(solution)/shard_map/ppermute | solution.py:672
  6.7 0.6 %shard_map.133 = (f32[64,640]{1,0:T(8,128)S(1)}, s16[16,640]{1,0:T(8,128)(2,1)S(1)}, s16[16,640]{1,0:T(8,128)(2,1)S(1)}, s16[16,640]{1,0:T(8,128)(2,1)S(1)}) custom-call(bf16[4,64,128]{2,1,0:T(8,128)(2,1)S(1)} %get-tuple-element.20.weight_ref, f32[64,128]{1,0:T(8,128)S(1)} %get-tuple-element.21.stats_ref, ...), custom_call_target="tpu_custom_call" | custom-call | flops 8388608 | bytes 6291456 | tf_op jit(solution)/shard_map/pallas_call | solution.py:245
  7.3 3.7 %collective-permute-start.1 = (s16[16,640]{1,0:T(8,128)(2,1)S(1)}, s16[16,640]{1,0:T(8,128)(2,1)S(1)}, u32[]{:S(2)}, u32[]{:S(2)}) collective-permute-start(s16[16,640]{1,0:T(8,128)(2,1)S(1)} %get-tuple-element.27), channel_id=1, source_target_pairs={{0,3},{1,2},{2,1},{3,0},{4,7},{5,6},{6,5},{7,4},{8,11},{9,10},{10,... | collective-permute-start | bytes 61448 | tf_op jit(solution)/shard_map/ppermute | solution.py:672
  11.0 0.8 %collective-permute-start.3 = (s16[16,640]{1,0:T(8,128)(2,1)S(1)}, s16[16,640]{1,0:T(8,128)(2,1)S(1)}, u32[]{:S(2)}, u32[]{:S(2)}) collective-permute-start(s16[16,640]{1,0:T(8,128)(2,1)S(1)} %get-tuple-element.29), channel_id=1, source_target_pairs={{0,1},{1,0},{2,3},{3,2},{4,5},{5,4},{6,7},{7,6},{8,9},{9,8},{10,11... | collective-permute-start | bytes 61448 | tf_op jit(solution)/shard_map/ppermute | solution.py:672
  11.7 1.2 %shard_map.135 = (f32[16,2048]{1,0:T(8,128)S(1)}, s16[16,2176]{1,0:T(8,128)(2,1)S(1)}, s16[16,2176]{1,0:T(8,128)(2,1)S(1)}, s16[16,2176]{1,0:T(8,128)(2,1)S(1)}) custom-call(bf16[64,1280]{1,0:T(8,128)(2,1)S(1)} %get-tuple-element.25.after_ref.kept_ref, bf16[64,1280]{1,0:T(8,128)(2,1)S(1)} %collective-permute-done.4.landed_ref, bf16[1280,2048]{1,0:T(8,128)(2,1)S(1)} %copy-done), custom_call_target="tpu_custom_call" | custom-call | flops 335544320 | bytes 5242880 | tf_op jit(solution)/shard_map/pallas_call | solution.py:245
  13.0 3.7 %collective-permute-start.5 = (s16[16,2176]{1,0:T(8,128)(2,1)S(1)}, s16[16,2176]{1,0:T(8,128)(2,1)S(1)}, u32[]{:S(2)}, u32[]{:S(2)}) collective-permute-start(s16[16,2176]{1,0:T(8,128)(2,1)S(1)} %get-tuple-element.33), channel_id=1, source_target_pairs={{0,3},{1,2},{2,1},{3,0},{4,7},{5,6},{6,5},{7,4},{8,11},{9,10},{10,... | collective-permute-start | bytes 208904 | tf_op jit(solution)/shard_map/ppermute | solution.py:672
  16.7 1.0 %collective-permute-start.7 = (s16[16,2176]{1,0:T(8,128)(2,1)S(1)}, s16[16,2176]{1,0:T(8,128)(2,1)S(1)}, u32[]{:S(2)}, u32[]{:S(2)}) collective-permute-start(s16[16,2176]{1,0:T(8,128)(2,1)S(1)} %shard_map.137), channel_id=1, source_target_pairs={{0,2},{1,3},{2,0},{3,1},{4,6},{5,7},{6,4},{7,5},{8,10},{9,11},{10,... | collective-permute-start | bytes 208904 | tf_op jit(solution)/shard_map/ppermute | solution.py:672
  17.7 1.9 %collective-permute-done.5.refs_0_ = s16[16,2176]{1,0:T(8,128)(2,1)S(1)} collective-permute-done((s16[16,2176]{1,0:T(8,128)(2,1)S(1)}, s16[16,2176]{1,0:T(8,128)(2,1)S(1)}, u32[]{:S(2)}, u32[]{:S(2)}) %collective-permute-start.5) | collective-permute-done | bytes 69664 | tf_op jit(solution)/shard_map/ppermute | solution.py:672
  19.6 1.9 %collective-permute-done.6.refs_1_ = s16[16,2176]{1,0:T(8,128)(2,1)S(1)} collective-permute-done((s16[16,2176]{1,0:T(8,128)(2,1)S(1)}, s16[16,2176]{1,0:T(8,128)(2,1)S(1)}, u32[]{:S(2)}, u32[]{:S(2)}) %collective-permute-start.6) | collective-permute-done | bytes 69664 | tf_op jit(solution)/shard_map/ppermute | solution.py:672
  21.5 0.2 shard_map.136.own_ref
  21.6 0.5 %collective-permute-done.7.refs_0_ = s16[16,2176]{1,0:T(8,128)(2,1)S(1)} collective-permute-done((s16[16,2176]{1,0:T(8,128)(2,1)S(1)}, s16[16,2176]{1,0:T(8,128)(2,1)S(1)}, u32[]{:S(2)}, u32[]{:S(2)}) %collective-permute-start.7) | collective-permute-done | bytes 69664 | tf_op jit(solution)/shard_map/ppermute | solution.py:672
  22.2 0.4 %shard_map.138.refs_0_ = bf16[16,2048]{1,0:T(8,128)(2,1)S(1)} custom-call(f32[16,2048]{1,0:T(8,128)S(1)} %shard_map.136.own_ref, s16[16,2176]{1,0:T(8,128)(2,1)S(1)} %collective-permute-done.7.refs_0_, f32[16,128]{1,0:T(8,128)S(1)} %get-tuple-element.36.refs_1_, f32[16,128]{1,0:T(8,128)S(1)} %get-tuple-element.37.refs_2_), custom_call_target="tpu_custom_call" | custom-call | tf_op jit(solution)/shard_map/pallas_call | solution.py:245
  22.6 2.2 %collective-permute-start.10 = (bf16[16,2048]{1,0:T(8,128)(2,1)S(1)}, bf16[16,2048]{1,0:T(8,128)(2,1)S(1)}, u32[]{:S(2)}, u32[]{:S(2)}) collective-permute-start(bf16[16,2048]{1,0:T(8,128)(2,1)S(1)} %shard_map.138.refs_0_), channel_id=1, source_target_pairs={{0,3},{1,2},{2,1},{3,0},{4,7},{5,6},{6,5},{7,4},{8,11},{9,10},{10,... | collective-permute-start | bytes 196616 | tf_op jit(solution)/shard_map/ppermute | solution.py:672
  24.8 0.4 %collective-permute-start.9 = (bf16[16,2048]{1,0:T(8,128)(2,1)S(1)}, bf16[16,2048]{1,0:T(8,128)(2,1)S(1)}, u32[]{:S(2)}, u32[]{:S(2)}) collective-permute-start(bf16[16,2048]{1,0:T(8,128)(2,1)S(1)} %shard_map.138.refs_0_), channel_id=1, source_target_pairs={{0,1},{1,0},{2,3},{3,2},{4,5},{5,4},{6,7},{7,6},{8,9},{9,8},{10,11... | collective-permute-start | bytes 196616 | tf_op jit(solution)/shard_map/ppermute | solution.py:672
  25.2 1.8 %collective-permute-start.8 = (bf16[16,2048]{1,0:T(8,128)(2,1)S(1)}, bf16[16,2048]{1,0:T(8,128)(2,1)S(1)}, u32[]{:S(2)}, u32[]{:S(2)}) collective-permute-start(bf16[16,2048]{1,0:T(8,128)(2,1)S(1)} %shard_map.138.refs_0_), channel_id=1, source_target_pairs={{0,2},{1,3},{2,0},{3,1},{4,6},{5,7},{6,4},{7,5},{8,10},{9,11},{10,... | collective-permute-start | bytes 196616 | tf_op jit(solution)/shard_map/ppermute | solution.py:672
  27.1 0.4 %shard_map.134 = bf16[4,16,128]{2,1,0:T(8,128)(2,1)S(1)} custom-call(f32[64,640]{1,0:T(8,128)S(1)} %get-tuple-element.26.span_ref, s16[16,640]{1,0:T(8,128)(2,1)S(1)} %collective-permute-done.1.refs_0_, s16[16,640]{1,0:T(8,128)(2,1)S(1)} %collective-permute-done.2.refs_1_, s16[16,640]{1,0:T(8,128)(2,1)S(1)} %collective-permute-done.3.refs_2_, ...), custom_call_target="tpu_custom_call" | custom-call | tf_op jit(solution)/shard_map/pallas_call | solution.py:245
  27.5 0.6 %copy.16 = bf16[1,4,16,128]{3,1,2,0:T(4,128)(2,1)} copy(bf16[1,4,16,128]{3,2,1,0:T(8,128)(2,1)S(1)} %bitcast.7) | data formatting | bytes 32768
  28.1 1.1 %collective-permute-done.10.refs_3_ = bf16[16,2048]{1,0:T(8,128)(2,1)S(1)} collective-permute-done((bf16[16,2048]{1,0:T(8,128)(2,1)S(1)}, bf16[16,2048]{1,0:T(8,128)(2,1)S(1)}, u32[]{:S(2)}, u32[]{:S(2)}) %collective-permute-start.10) | collective-permute-done | bytes 65568 | tf_op jit(solution)/shard_map/ppermute | solution.py:672
  29.2 0.5 %collective-permute-done.9.refs_2_ = bf16[16,2048]{1,0:T(8,128)(2,1)S(1)} collective-permute-done((bf16[16,2048]{1,0:T(8,128)(2,1)S(1)}, bf16[16,2048]{1,0:T(8,128)(2,1)S(1)}, u32[]{:S(2)}, u32[]{:S(2)}) %collective-permute-start.9) | collective-permute-done | bytes 65568 | tf_op jit(solution)/shard_map/ppermute | solution.py:672
  29.7 0.7 %collective-permute-done.8.refs_1_ = bf16[16,2048]{1,0:T(8,128)(2,1)S(1)} collective-permute-done((bf16[16,2048]{1,0:T(8,128)(2,1)S(1)}, bf16[16,2048]{1,0:T(8,128)(2,1)S(1)}, u32[]{:S(2)}, u32[]{:S(2)}) %collective-permute-start.8) | collective-permute-done | bytes 65568 | tf_op jit(solution)/shard_map/ppermute | solution.py:672
  30.4 0.7 %shard_map.139 = bf16[64,2048]{1,0:T(8,128)(2,1)} custom-call(bf16[16,2048]{1,0:T(8,128)(2,1)S(1)} %shard_map.138.refs_0_, bf16[16,2048]{1,0:T(8,128)(2,1)S(1)} %collective-permute-done.8.refs_1_, bf16[16,2048]{1,0:T(8,128)(2,1)S(1)} %collective-permute-done.9.refs_2_, bf16[16,2048]{1,0:T(8,128)(2,1)S(1)} %collective-permute-done.10.refs_3_), custom_call_target="tpu_custom_call" | custom-call | tf_op jit(solution)/shard_map/pallas_call | solution.py:245
  (14 shorter events, 0.0 us)
Async XLA Ops:
  0.6 11.1 %copy-start = (bf16[1280,2048]{1,0:T(8,128)(2,1)S(1)}, bf16[1280,2048]{1,0:T(8,128)(2,1)}, u32[]{:S(2)}) copy-start(bf16[1280,2048]{1,0:T(8,128)(2,1)} %weight_ref.1) | copy-start | bytes 15728644
  0.6 3.0 %collective-permute-start = (bf16[256,1280]{1,0:T(8,128)(2,1)}, bf16[256,1280]{1,0:T(8,128)(2,1)S(1)}, u32[]{:S(2)}, u32[]{:S(2)}) collective-permute-start(bf16[256,1280]{1,0:T(8,128)(2,1)} %bitcast.8), channel_id=1, source_target_pairs={{0,4},{4,0},{8,12},{12,8},{1,5},{5,1},{9,13},{13,9},{2,6},{6,2},{1... | collective-permute-start | bytes 1966088 | tf_op jit(solution)/shard_map/ppermute | solution.py:672
  3.6 23.5 %copy-start.1 = (bf16[4,1024]{1,0:T(4,128)(2,1)S(1)}, bf16[4,1024]{1,0:T(4,128)(2,1)}, u32[]{:S(2)}) copy-start(bf16[4,1024]{1,0:T(4,128)(2,1)} %refs_4_.1) | copy-start | bytes 24580
  3.6 23.5 %copy-start.2 = (bf16[4,1024]{1,0:T(4,128)(2,1)S(1)}, bf16[4,1024]{1,0:T(4,128)(2,1)}, u32[]{:S(2)}) copy-start(bf16[4,1024]{1,0:T(4,128)(2,1)} %refs_5_.3) | copy-start | bytes 24580
  3.9 7.8 %collective-permute-start.4 = (bf16[64,1280]{1,0:T(8,128)(2,1)S(1)}, bf16[64,1280]{1,0:T(8,128)(2,1)S(1)}, u32[]{:S(2)}, u32[]{:S(2)}) collective-permute-start(bf16[64,1280]{1,0:T(8,128)(2,1)S(1)} %get-tuple-element.31), channel_id=1, source_target_pairs={{0,12},{4,8},{8,4},{12,0},{1,13},{5,9},{9,5},{13,1},{2,14},{6,10},... | collective-permute-start | bytes 491528 | tf_op jit(solution)/shard_map/ppermute | solution.py:672
  7.3 9.4 %collective-permute-start.1 = (s16[16,640]{1,0:T(8,128)(2,1)S(1)}, s16[16,640]{1,0:T(8,128)(2,1)S(1)}, u32[]{:S(2)}, u32[]{:S(2)}) collective-permute-start(s16[16,640]{1,0:T(8,128)(2,1)S(1)} %get-tuple-element.27), channel_id=1, source_target_pairs={{0,3},{1,2},{2,1},{3,0},{4,7},{5,6},{6,5},{7,4},{8,11},{9,10},{10,... | collective-permute-start | bytes 61448 | tf_op jit(solution)/shard_map/ppermute | solution.py:672
  10.9 5.7 %collective-permute-start.2 = (s16[16,640]{1,0:T(8,128)(2,1)S(1)}, s16[16,640]{1,0:T(8,128)(2,1)S(1)}, u32[]{:S(2)}, u32[]{:S(2)}) collective-permute-start(s16[16,640]{1,0:T(8,128)(2,1)S(1)} %get-tuple-element.28), channel_id=1, source_target_pairs={{0,2},{1,3},{2,0},{3,1},{4,6},{5,7},{6,4},{7,5},{8,10},{9,11},{10,... | collective-permute-start | bytes 61448 | tf_op jit(solution)/shard_map/ppermute | solution.py:672
  11.0 5.7 %collective-permute-start.3 = (s16[16,640]{1,0:T(8,128)(2,1)S(1)}, s16[16,640]{1,0:T(8,128)(2,1)S(1)}, u32[]{:S(2)}, u32[]{:S(2)}) collective-permute-start(s16[16,640]{1,0:T(8,128)(2,1)S(1)} %get-tuple-element.29), channel_id=1, source_target_pairs={{0,1},{1,0},{2,3},{3,2},{4,5},{5,4},{6,7},{7,6},{8,9},{9,8},{10,11... | collective-permute-start | bytes 61448 | tf_op jit(solution)/shard_map/ppermute | solution.py:672
  13.0 6.6 %collective-permute-start.5 = (s16[16,2176]{1,0:T(8,128)(2,1)S(1)}, s16[16,2176]{1,0:T(8,128)(2,1)S(1)}, u32[]{:S(2)}, u32[]{:S(2)}) collective-permute-start(s16[16,2176]{1,0:T(8,128)(2,1)S(1)} %get-tuple-element.33), channel_id=1, source_target_pairs={{0,3},{1,2},{2,1},{3,0},{4,7},{5,6},{6,5},{7,4},{8,11},{9,10},{10,... | collective-permute-start | bytes 208904 | tf_op jit(solution)/shard_map/ppermute | solution.py:672
  16.6 4.8 %collective-permute-start.6 = (s16[16,2176]{1,0:T(8,128)(2,1)S(1)}, s16[16,2176]{1,0:T(8,128)(2,1)S(1)}, u32[]{:S(2)}, u32[]{:S(2)}) collective-permute-start(s16[16,2176]{1,0:T(8,128)(2,1)S(1)} %get-tuple-element.34), channel_id=1, source_target_pairs={{0,1},{1,0},{2,3},{3,2},{4,5},{5,4},{6,7},{7,6},{8,9},{9,8},{10,11... | collective-permute-start | bytes 208904 | tf_op jit(solution)/shard_map/ppermute | solution.py:672
  16.7 5.5 %collective-permute-start.7 = (s16[16,2176]{1,0:T(8,128)(2,1)S(1)}, s16[16,2176]{1,0:T(8,128)(2,1)S(1)}, u32[]{:S(2)}, u32[]{:S(2)}) collective-permute-start(s16[16,2176]{1,0:T(8,128)(2,1)S(1)} %shard_map.137), channel_id=1, source_target_pairs={{0,2},{1,3},{2,0},{3,1},{4,6},{5,7},{6,4},{7,5},{8,10},{9,11},{10,... | collective-permute-start | bytes 208904 | tf_op jit(solution)/shard_map/ppermute | solution.py:672
  22.6 6.6 %collective-permute-start.10 = (bf16[16,2048]{1,0:T(8,128)(2,1)S(1)}, bf16[16,2048]{1,0:T(8,128)(2,1)S(1)}, u32[]{:S(2)}, u32[]{:S(2)}) collective-permute-start(bf16[16,2048]{1,0:T(8,128)(2,1)S(1)} %shard_map.138.refs_0_), channel_id=1, source_target_pairs={{0,3},{1,2},{2,1},{3,0},{4,7},{5,6},{6,5},{7,4},{8,11},{9,10},{10,... | collective-permute-start | bytes 196616 | tf_op jit(solution)/shard_map/ppermute | solution.py:672
  24.8 4.9 %collective-permute-start.9 = (bf16[16,2048]{1,0:T(8,128)(2,1)S(1)}, bf16[16,2048]{1,0:T(8,128)(2,1)S(1)}, u32[]{:S(2)}, u32[]{:S(2)}) collective-permute-start(bf16[16,2048]{1,0:T(8,128)(2,1)S(1)} %shard_map.138.refs_0_), channel_id=1, source_target_pairs={{0,1},{1,0},{2,3},{3,2},{4,5},{5,4},{6,7},{7,6},{8,9},{9,8},{10,11... | collective-permute-start | bytes 196616 | tf_op jit(solution)/shard_map/ppermute | solution.py:672
  25.2 5.2 %collective-permute-start.8 = (bf16[16,2048]{1,0:T(8,128)(2,1)S(1)}, bf16[16,2048]{1,0:T(8,128)(2,1)S(1)}, u32[]{:S(2)}, u32[]{:S(2)}) collective-permute-start(bf16[16,2048]{1,0:T(8,128)(2,1)S(1)} %shard_map.138.refs_0_), channel_id=1, source_target_pairs={{0,2},{1,3},{2,0},{3,1},{4,6},{5,7},{6,4},{7,5},{8,10},{9,11},{10,... | collective-permute-start | bytes 196616 | tf_op jit(solution)/shard_map/ppermute | solution.py:672
